TPU v7x, 512 devices: a whole 4x8x8 slice. The times are simulated.
512 devices in a mesh: ctx: 64 (over z, x, core), kvh: 8 (over y).
Axes of the slice: x: 4, y: 8, z: 8, core: 2. Of those that a mesh axis runs over, the one named last changes fastest.
Arguments:
- query_states: bfloat16 [24576, 4096], P('ctx', 'kvh')
- key_states: bfloat16 [24576, 1024], P('ctx', 'kvh')
- value_states: bfloat16 [24576, 1024], P('ctx', 'kvh'), may hold values from -6 to 6
- grad_output: bfloat16 [24576, 4096], P(('ctx', 'kvh')), may hold values from -6 to 6
- doc_start: int32 [192], P('ctx'), may hold values from 0 to 23424, as said below
Outputs:
- grad_query: bfloat16 [24576, 4096], P(('ctx', 'kvh'))
- grad_key: bfloat16 [24576, 1024], P('ctx', 'kvh')
- grad_value: bfloat16 [24576, 1024], P('ctx', 'kvh')
Inputs may be any that keep to these rules, and one draw needn't show every extreme that they name: Documents are whole runs of blocks; doc_start is the same for all blocks of one document and equals the position of its first block. Every document has at most 1152 tokens, and the last 1152 tokens of the sequence form one document.
All inputs are finite; a program needn't handle non-finite values.
Results may differ from a plain program's by a relative error of at most 0.03.
Values may be sent and summed in bfloat16 or wider, within the bound.
No kernel may reach another device: no remote copies, remote signals or barrier semaphores. Data moves between devices by JAX's collectives and lax.ppermute only.
A program may use at most 64 MiB of HBM per device.

v0:
```python
import jax
import jax.numpy as jnp
from jax import lax
from jax.sharding import PartitionSpec as P

SPAN = 4


masked_score = -1e30


def passed_along(value, axis, by):
    length = lax.axis_size(axis)
    pairs = [(i, i + by) for i in range(length) if 0 <= i + by < length]
    return lax.ppermute(value, axis, pairs)


def body(query_states, key_states, value_states, grad_output, doc_start):
    row_count = query_states.shape[0]
    head_dim = key_states.shape[1]
    group_size = query_states.shape[1] // head_dim
    block_len = row_count // doc_start.shape[0]
    inv_root = head_dim ** (-0.5)
    device_idx = lax.axis_index("ctx")
    grad_rows = lax.all_to_all(grad_output, "kvh", split_axis=1, concat_axis=0, tiled=True)
    query_heads = query_states.reshape(row_count, group_size, head_dim)
    grad_heads = grad_rows.reshape(row_count, group_size, head_dim)
    starts = jnp.repeat(doc_start, block_len)
    offsets = jnp.arange(row_count, dtype=jnp.int32)
    query_pos = device_idx * row_count + offsets
    paired = jnp.stack([key_states, value_states])
    carried = [paired]
    moving = paired
    for distance in range(1, SPAN):
        moving = passed_along(moving, "ctx", 1)
        carried.append(moving)

    def allowed(distance):
        key_pos = (device_idx - distance) * row_count + offsets
        return (key_pos[None, :] >= starts[:, None]) & (key_pos[None, :] <= query_pos[:, None])

    def scores(distance):
        return (
            jnp.einsum(
                "tjd,pd->jtp", query_heads, carried[distance][0], preferred_element_type=jnp.float32
            )
            * inv_root
        )

    def row_stats(distance):
        masked = jnp.where(allowed(distance)[None], scores(distance), masked_score)
        row_top = jnp.max(masked, axis=-1)
        return (row_top, jnp.sum(jnp.exp(masked - row_top[..., None]), axis=-1))

    row_best, row_total = row_stats(0)
    for distance in range(1, SPAN):
        row_top, row_part = row_stats(distance)
        merged = jnp.maximum(row_best, row_top)
        row_total = row_total * jnp.exp(row_best - merged) + row_part * jnp.exp(row_top - merged)
        row_best = merged
    log_norm = row_best + jnp.log(row_total)

    def weights(distance):
        return jnp.where(
            allowed(distance)[None], jnp.exp(scores(distance) - log_norm[..., None]), 0.0
        )

    def attend(distance):
        weight_b = weights(distance).astype(jnp.bfloat16)
        return jnp.einsum(
            "jtp,pd->jtd", weight_b, carried[distance][1], preferred_element_type=jnp.float32
        )

    attend_acc = attend(0)
    for distance in range(1, SPAN):
        attend_acc = attend_acc + attend(distance)
    attended = attend_acc.astype(jnp.bfloat16)
    delta = jnp.sum(
        grad_heads.astype(jnp.float32).transpose(1, 0, 2) * attended.astype(jnp.float32), axis=-1
    )

    def backward(distance):
        weight_f = weights(distance)
        weight_b = weight_f.astype(jnp.bfloat16)
        key_value = carried[distance]
        dweight = jnp.einsum(
            "tjd,pd->jtp", grad_heads, key_value[1], preferred_element_type=jnp.float32
        )
        dscore = (weight_f * (dweight - delta[..., None]) * inv_root).astype(jnp.bfloat16)
        dquery = jnp.einsum("jtp,pd->tjd", dscore, key_value[0], preferred_element_type=jnp.float32)
        dkey = jnp.einsum("jtp,tjd->pd", dscore, query_heads, preferred_element_type=jnp.float32)
        dvalue = jnp.einsum("jtp,tjd->pd", weight_b, grad_heads, preferred_element_type=jnp.float32)
        return (dquery, jnp.stack([dkey, dvalue]))

    dquery_acc, own_grads = backward(0)
    for distance in range(1, SPAN):
        dquery_part, far_grads = backward(distance)
        dquery_acc = dquery_acc + dquery_part
        own_grads = own_grads + passed_along(
            far_grads.astype(jnp.bfloat16), "ctx", -distance
        ).astype(far_grads.dtype)
    grad_query = dquery_acc.astype(jnp.bfloat16).reshape(row_count, group_size * head_dim)
    grad_query = lax.all_to_all(grad_query, "kvh", split_axis=0, concat_axis=1, tiled=True)
    return (grad_query, own_grads[0].astype(jnp.bfloat16), own_grads[1].astype(jnp.bfloat16))


def solution(mesh):
    in_specs = (
        P("ctx", "kvh"),
        P("ctx", "kvh"),
        P("ctx", "kvh"),
        P(("ctx", "kvh"), None),
        P("ctx"),
    )
    out_specs = (P(("ctx", "kvh"), None), P("ctx", "kvh"), P("ctx", "kvh"))
    return jax.shard_map(body, mesh=mesh, in_specs=in_specs, out_specs=out_specs, check_vma=False)
```

profile of v0, /device:TPU:261, one launch (start us, length us, event | category | flops | bytes accessed | tf_op | source)
XLA Modules:
  0.0 91.1 jit_solution(7483598369566379243)
XLA Ops:
  0.7 1.0 %pad_maximum_fusion = bf16[2,384,128]{2,1,0:T(8,128)(2,1)S(1)} fusion(bf16[1,384,128]{2,1,0:T(8,128)(2,1)} %bitcast.320, bf16[1,384,128]{2,1,0:T(8,128)(2,1)} %bitcast.317), kind=kLoop, calls=%fused_computation.100 | loop fusion | flops 98304 | bytes 393216 | tf_op jit(solution)/shard_map/stack | solution.py:31
  1.7 3.4 %collective-permute-start = (bf16[2,384,128]{2,1,0:T(8,128)(2,1)S(1)}, bf16[2,384,128]{2,1,0:T(8,128)(2,1)}, u32[]{:S(2)}, u32[]{:S(2)}) collective-permute-start(bf16[2,384,128]{2,1,0:T(8,128)(2,1)S(1)} %pad_maximum_fusion), channel_id=1, source_target_pairs={{0,8},{8,16},{16,24},{24,32},{32,40},{40,48},{48,56},{56,64},{64,7... | collective-permute-start | bytes 589832 | tf_op jit(solution)/shard_map/ppermute | solution.py:15
  5.1 1.8 %copy.182 = bf16[6,8,8,512]{3,2,0,1:T(8,128)(2,1)} copy(bf16[6,8,8,512]{3,2,1,0:T(8,128)(2,1)} %bitcast.318) | data formatting | bytes 786432 | tf_op jit(solution)/shard_map/all_to_all | solution.py:25
  6.8 6.8 %all-to-all-start = ((bf16[48,8,512]{2,0,1:T(8,128)(2,1)}), bf16[48,8,512]{2,0,1:T(8,128)(2,1)S(1)}, u32[]{:S(2)}, u32[]{:S(2)}) async-start(bf16[48,8,512]{2,0,1:T(8,128)(2,1)} %bitcast.314), calls=%async_computation | async-start | bytes 786432 | tf_op jit(solution)/shard_map/all_to_all | solution.py:25
  16.1 2.2 %collective-permute-start.1 = (bf16[2,384,128]{2,1,0:T(8,128)(2,1)}, bf16[2,384,128]{2,1,0:T(8,128)(2,1)S(1)}, u32[]{:S(2)}, u32[]{:S(2)}) collective-permute-start(bf16[2,384,128]{2,1,0:T(8,128)(2,1)} %collective-permute-done), channel_id=1, source_target_pairs={{0,8},{8,16},{16,24},{24,32},{32,40},{40,48},{48,56},{56,64},{64,7... | collective-permute-start | bytes 589832 | tf_op jit(solution)/shard_map/ppermute | solution.py:15
  18.3 1.5 %fusion.21 = (f32[4,384]{1,0:T(4,128)S(1)}, f32[384,384,4]{1,0,2:T(8,128)S(1)}) fusion(pred[384,384]{0,1:T(8,128)(4,1)S(1)} %get-tuple-element.8, bf16[2,384,128]{2,1,0:T(8,128)(2,1)} %collective-permute-done, bf16[384,512]{1,0:T(8,128)(2,1)S(1)} %copy-done), kind=kOutput, calls=%fused_computation.37 | convolution fusion | flops 152762880 | bytes 3004416 | tf_op jit(solution)/shard_map/tjd,pd->jtp/dot_general | solution.py:44
  21.2 4.5 %collective-permute-start.2 = (bf16[2,384,128]{2,1,0:T(8,128)(2,1)S(1)}, bf16[2,384,128]{2,1,0:T(8,128)(2,1)S(1)}, u32[]{:S(2)}, u32[]{:S(2)}) collective-permute-start(bf16[2,384,128]{2,1,0:T(8,128)(2,1)S(1)} %collective-permute-done.1), channel_id=1, source_target_pairs={{0,8},{8,16},{16,24},{24,32},{32,40},{40,48},{48,56},{56,64},{64,7... | collective-permute-start | bytes 589832 | tf_op jit(solution)/shard_map/ppermute | solution.py:15
  26.7 1.3 %collective-permute-done.2 = bf16[2,384,128]{2,1,0:T(8,128)(2,1)S(1)} collective-permute-done((bf16[2,384,128]{2,1,0:T(8,128)(2,1)S(1)}, bf16[2,384,128]{2,1,0:T(8,128)(2,1)S(1)}, u32[]{:S(2)}, u32[]{:S(2)}) %collective-permute-start.2) | collective-permute-done | bytes 196640 | tf_op jit(solution)/shard_map/ppermute | solution.py:15
  30.1 1.5 %convolution_add_fusion.2 = f32[4,384,128]{1,2,0:T(8,128)S(1)} fusion(f32[4,384,128]{1,2,0:T(8,128)S(1)} %fusion.63, bf16[2,384,128]{2,1,0:T(8,128)(2,1)} %collective-permute-done, f32[384,384,4]{1,0,2:T(8,128)S(1)} %get-tuple-element.14, f32[4,384]{1,0:T(4,128)S(1)} %log_add_fusion, pred[384,384]{0,1:T(8,128)(4,1)S(1)} %get-tuple-element.8), kind=kOutput, calls=%fused_computation.53 | convolution fusion | flops 153550848 | bytes 4184064 | tf_op jit(solution)/shard_map/jtp,pd->jtd/dot_general | solution.py:70
  31.6 1.5 %convolution_add_fusion.1 = f32[4,384,128]{1,2,0:T(8,128)} fusion(f32[4,384,128]{1,2,0:T(8,128)S(1)} %convolution_add_fusion.2, bf16[2,384,128]{2,1,0:T(8,128)(2,1)S(1)} %collective-permute-done.1, f32[384,384,4]{1,0,2:T(8,128)S(1)} %get-tuple-element.12, f32[4,384]{1,0:T(4,128)S(1)} %log_add_fusion, pred[384,384]{0,1:T(8,128)(4,1)S(1)} %get-tuple-element.6), kind=kOutput, calls=%fused_computation.52 | convolution fusion | flops 153550848 | bytes 4184064 | tf_op jit(solution)/shard_map/jtp,pd->jtd/dot_general | solution.py:70
  33.9 1.2 %copy.81 = bf16[384,4,128]{0,2,1:T(8,128)(2,1)S(1)} copy(bf16[384,4,128]{2,1,0:T(4,128)(2,1)} %reshape.316) | data formatting | bytes 786432 | tf_op jit(solution)/shard_map/reshape | solution.py:27
  35.7 1.1 %copy-done.2 = f32[384,384,4]{1,0,2:T(8,128)S(1)} copy-done((f32[384,384,4]{1,0,2:T(8,128)S(1)}, f32[384,384,4]{1,0,2:T(8,128)}, u32[]{:S(2)}) %copy-start.2) | copy-done | bytes 2359320
  37.4 1.1 %copy-done.6 = f32[384,384,4]{1,0,2:T(8,128)S(1)} copy-done((f32[384,384,4]{1,0,2:T(8,128)S(1)}, f32[384,384,4]{1,0,2:T(8,128)}, u32[]{:S(2)}) %copy-start.6) | copy-done | bytes 2359320
  39.1 1.1 %copy-done.4 = f32[384,384,4]{1,0,2:T(8,128)S(1)} copy-done((f32[384,384,4]{1,0,2:T(8,128)S(1)}, f32[384,384,4]{1,0,2:T(8,128)}, u32[]{:S(2)}) %copy-start.4) | copy-done | bytes 2359320
  40.2 1.2 %convolution_bitcast_fusion.10 = f32[1,384,128]{2,1,0:T(8,128)} fusion(bf16[384,4,128]{0,2,1:T(8,128)(2,1)S(1)} %copy.81, f32[384,384,4]{1,0,2:T(8,128)S(1)} %copy-done.4, f32[4,384]{1,0:T(4,128)S(1)} %log_add_fusion, pred[384,384]{0,1:T(8,128)(4,1)S(1)} %copy-done.12), kind=kOutput, calls=%fused_computation.65 | convolution fusion | flops 153354240 | bytes 3102720 | tf_op jit(solution)/shard_map/jtp,tjd->pd/dot_general | solution.py:92
  42.3 1.0 %fusion.11 = bf16[4,384,384]{1,2,0:T(8,128)(2,1)S(1)} fusion(f32[384,384,4]{1,0,2:T(8,128)S(1)} %copy-done.4, bf16[384,4,128]{0,2,1:T(8,128)(2,1)S(1)} %copy.81, f32[4,384]{1,0:T(4,128)S(1)} %fusion.35, f32[4,384]{1,0:T(4,128)S(1)} %log_add_fusion, pred[384,384]{0,1:T(8,128)(4,1)S(1)} %copy-done.12, bf16[384,128]{1,0:T(8,128)(2,1)S(1)} %copy-done.21), kind=kOutput, calls=%fused_computation.15 | convolution fusion | flops 155123712 | bytes 4190208 | tf_op jit(solution)/shard_map/tjd,pd->jtp/dot_general | solution.py:86
  43.3 2.0 %fusion.8 = bf16[4,384,384]{1,2,0:T(8,128)(2,1)S(1)} fusion(f32[384,384,4]{1,0,2:T(8,128)S(1)} %get-tuple-element.14, bf16[384,4,128]{0,2,1:T(8,128)(2,1)S(1)} %copy.81, f32[4,384]{1,0:T(4,128)S(1)} %fusion.35, f32[4,384]{1,0:T(4,128)S(1)} %log_add_fusion, pred[384,384]{0,1:T(8,128)(4,1)S(1)} %get-tuple-element.8, bf16[2,384,128]{2,1,0:T(8,128)(2,1)} %collective-permute-done), kind=kOutput, calls=%fused_computation.11 | convolution fusion | flops 155123712 | bytes 4190208 | tf_op jit(solution)/shard_map/tjd,pd->jtp/dot_general | solution.py:86
  45.8 3.6 %collective-permute-start.3 = (bf16[2,384,128]{2,1,0:T(8,128)(2,1)S(1)}, bf16[2,384,128]{2,1,0:T(8,128)(2,1)S(1)}, u32[]{:S(2)}, u32[]{:S(2)}) collective-permute-start(bf16[2,384,128]{2,1,0:T(8,128)(2,1)S(1)} %pad_maximum_fusion.1), channel_id=1, source_target_pairs={{8,0},{16,8},{24,16},{32,24},{40,32},{48,40},{56,48},{64,56},{72,6... | collective-permute-start | bytes 589832 | tf_op jit(solution)/shard_map/ppermute | solution.py:15
  49.4 1.0 %fusion.5 = bf16[4,384,384]{1,2,0:T(8,128)(2,1)S(1)} fusion(f32[384,384,4]{1,0,2:T(8,128)S(1)} %copy-done.2, bf16[384,4,128]{0,2,1:T(8,128)(2,1)S(1)} %copy.81, f32[4,384]{1,0:T(4,128)S(1)} %fusion.35, f32[4,384]{1,0:T(4,128)S(1)} %log_add_fusion, pred[384,384]{0,1:T(8,128)(4,1)S(1)} %get-tuple-element.6, bf16[2,384,128]{2,1,0:T(8,128)(2,1)S(1)} %copy-done.16), kind=kOutput, calls=%fused_computation.7 | convolution fusion | flops 155123712 | bytes 4190208 | tf_op jit(solution)/shard_map/tjd,pd->jtp/dot_general | solution.py:86
  50.9 2.1 %collective-permute-start.4 = (bf16[2,384,128]{2,1,0:T(8,128)(2,1)S(1)}, bf16[2,384,128]{2,1,0:T(8,128)(2,1)S(1)}, u32[]{:S(2)}, u32[]{:S(2)}) collective-permute-start(bf16[2,384,128]{2,1,0:T(8,128)(2,1)S(1)} %pad_maximum_fusion.2), channel_id=1, source_target_pairs={{16,0},{24,8},{32,16},{40,24},{48,32},{56,40},{64,48},{72,56},{80,... | collective-permute-start | bytes 589832 | tf_op jit(solution)/shard_map/ppermute | solution.py:15
  54.5 9.2 %collective-permute-start.5 = (bf16[2,384,128]{2,1,0:T(8,128)(2,1)S(1)}, bf16[2,384,128]{2,1,0:T(8,128)(2,1)S(1)}, u32[]{:S(2)}, u32[]{:S(2)}) collective-permute-start(bf16[2,384,128]{2,1,0:T(8,128)(2,1)S(1)} %pad_maximum_fusion.3), channel_id=1, source_target_pairs={{24,0},{32,8},{40,16},{48,24},{56,32},{64,40},{72,48},{80,56},{88,... | collective-permute-start | bytes 589832 | tf_op jit(solution)/shard_map/ppermute | solution.py:15
  64.3 1.5 %fusion.28 = f32[384,4,128]{2,0,1:T(8,128)S(1)} fusion(f32[384,4,128]{2,0,1:T(8,128)S(1)} %convolution_bitcast_fusion.3, bf16[4,384,384]{1,2,0:T(8,128)(2,1)S(1)} %fusion.8, bf16[2,384,128]{2,1,0:T(8,128)(2,1)} %collective-permute-done), kind=kOutput, calls=%fused_computation.48 | convolution fusion | flops 151191552 | bytes 2850816 | tf_op jit(solution)/shard_map/jtp,pd->tjd/dot_general | solution.py:90
  68.2 6.9 %all-to-all-start.1 = ((bf16[8,48,512]{2,1,0:T(8,128)(2,1)}), bf16[8,48,512]{2,1,0:T(8,128)(2,1)S(1)}, u32[]{:S(2)}, u32[]{:S(2)}) async-start(bf16[8,48,512]{2,1,0:T(8,128)(2,1)} %all_to_all.29), calls=%async_computation.1 | async-start | bytes 786432 | tf_op jit(solution)/shard_map/all_to_all | solution.py:103
  76.4 13.9 %all-to-all-done.1 = bf16[8,48,512]{2,1,0:T(8,128)(2,1)S(1)} async-done(((bf16[8,48,512]{2,1,0:T(8,128)(2,1)}), bf16[8,48,512]{2,1,0:T(8,128)(2,1)S(1)}, u32[]{:S(2)}, u32[]{:S(2)}) %all-to-all-start.1) | async-done | bytes 393248 | tf_op jit(solution)/shard_map/all_to_all | solution.py:103
  (81 shorter events, 17.7 us)
Async XLA Ops:
  0.6 14.3 %copy-start = (bf16[384,512]{1,0:T(8,128)(2,1)S(1)}, bf16[384,512]{1,0:T(8,128)(2,1)}, u32[]{:S(2)}) copy-start(bf16[384,512]{1,0:T(8,128)(2,1)} %param.5) | copy-start | bytes 1179652
  0.6 14.3 %copy-start.13 = (bf16[384,128]{1,0:T(8,128)(2,1)S(1)}, bf16[384,128]{1,0:T(8,128)(2,1)}, u32[]{:S(2)}) copy-start(bf16[384,128]{1,0:T(8,128)(2,1)} %param.6) | copy-start | bytes 294916
  1.7 14.4 %collective-permute-start = (bf16[2,384,128]{2,1,0:T(8,128)(2,1)S(1)}, bf16[2,384,128]{2,1,0:T(8,128)(2,1)}, u32[]{:S(2)}, u32[]{:S(2)}) collective-permute-start(bf16[2,384,128]{2,1,0:T(8,128)(2,1)S(1)} %pad_maximum_fusion), channel_id=1, source_target_pairs={{0,8},{8,16},{16,24},{24,32},{32,40},{40,48},{48,56},{56,64},{64,7... | collective-permute-start | bytes 589832 | tf_op jit(solution)/shard_map/ppermute | solution.py:15
  6.8 26.2 %all-to-all-start = ((bf16[48,8,512]{2,0,1:T(8,128)(2,1)}), bf16[48,8,512]{2,0,1:T(8,128)(2,1)S(1)}, u32[]{:S(2)}, u32[]{:S(2)}) async-start(bf16[48,8,512]{2,0,1:T(8,128)(2,1)} %bitcast.314), calls=%async_computation | async-start | bytes 786432 | tf_op jit(solution)/shard_map/all_to_all | solution.py:25
  14.9 13.7 %copy-start.9 = (pred[384,384]{0,1:T(8,128)(4,1)}, pred[384,384]{0,1:T(8,128)(4,1)S(1)}, u32[]{:S(2)}) copy-start(pred[384,384]{0,1:T(8,128)(4,1)S(1)} %get-tuple-element.7) | copy-start | bytes 442372
  14.9 14.3 %copy-start.11 = (pred[384,384]{0,1:T(8,128)(4,1)}, pred[384,384]{0,1:T(8,128)(4,1)S(1)}, u32[]{:S(2)}) copy-start(pred[384,384]{0,1:T(8,128)(4,1)S(1)} %get-tuple-element.5) | copy-start | bytes 442372
  15.5 13.7 %copy-start.3 = (f32[384,384,4]{1,0,2:T(8,128)}, f32[384,384,4]{1,0,2:T(8,128)S(1)}, u32[]{:S(2)}) copy-start(f32[384,384,4]{1,0,2:T(8,128)S(1)} %get-tuple-element.16) | copy-start | bytes 7077892
  16.1 5.1 %collective-permute-start.1 = (bf16[2,384,128]{2,1,0:T(8,128)(2,1)}, bf16[2,384,128]{2,1,0:T(8,128)(2,1)S(1)}, u32[]{:S(2)}, u32[]{:S(2)}) collective-permute-start(bf16[2,384,128]{2,1,0:T(8,128)(2,1)} %collective-permute-done), channel_id=1, source_target_pairs={{0,8},{8,16},{16,24},{24,32},{32,40},{40,48},{48,56},{56,64},{64,7... | collective-permute-start | bytes 589832 | tf_op jit(solution)/shard_map/ppermute | solution.py:15
  21.2 10.4 %copy-start.15 = (bf16[2,384,128]{2,1,0:T(8,128)(2,1)}, bf16[2,384,128]{2,1,0:T(8,128)(2,1)S(1)}, u32[]{:S(2)}) copy-start(bf16[2,384,128]{2,1,0:T(8,128)(2,1)S(1)} %collective-permute-done.1) | copy-start | bytes 589828
  21.2 6.9 %collective-permute-start.2 = (bf16[2,384,128]{2,1,0:T(8,128)(2,1)S(1)}, bf16[2,384,128]{2,1,0:T(8,128)(2,1)S(1)}, u32[]{:S(2)}, u32[]{:S(2)}) collective-permute-start(bf16[2,384,128]{2,1,0:T(8,128)(2,1)S(1)} %collective-permute-done.1), channel_id=1, source_target_pairs={{0,8},{8,16},{16,24},{24,32},{32,40},{40,48},{48,56},{56,64},{64,7... | collective-permute-start | bytes 589832 | tf_op jit(solution)/shard_map/ppermute | solution.py:15
  26.2 5.4 %copy-start.1 = (f32[384,384,4]{1,0,2:T(8,128)}, f32[384,384,4]{1,0,2:T(8,128)S(1)}, u32[]{:S(2)}) copy-start(f32[384,384,4]{1,0,2:T(8,128)S(1)} %get-tuple-element.12) | copy-start | bytes 7077892
  35.2 1.7 %copy-start.2 = (f32[384,384,4]{1,0,2:T(8,128)S(1)}, f32[384,384,4]{1,0,2:T(8,128)}, u32[]{:S(2)}) copy-start(f32[384,384,4]{1,0,2:T(8,128)} %copy-done.1) | copy-start | bytes 7077892
  36.8 1.7 %copy-start.6 = (f32[384,384,4]{1,0,2:T(8,128)S(1)}, f32[384,384,4]{1,0,2:T(8,128)}, u32[]{:S(2)}) copy-start(f32[384,384,4]{1,0,2:T(8,128)} %copy-done.5) | copy-start | bytes 7077892
  36.8 1.7 %copy-start.10 = (pred[384,384]{0,1:T(8,128)(4,1)S(1)}, pred[384,384]{0,1:T(8,128)(4,1)}, u32[]{:S(2)}) copy-start(pred[384,384]{0,1:T(8,128)(4,1)} %copy-done.9) | copy-start | bytes 442372
  38.5 1.7 %copy-start.4 = (f32[384,384,4]{1,0,2:T(8,128)S(1)}, f32[384,384,4]{1,0,2:T(8,128)}, u32[]{:S(2)}) copy-start(f32[384,384,4]{1,0,2:T(8,128)} %copy-done.3) | copy-start | bytes 7077892
  38.5 1.7 %copy-start.12 = (pred[384,384]{0,1:T(8,128)(4,1)S(1)}, pred[384,384]{0,1:T(8,128)(4,1)}, u32[]{:S(2)}) copy-start(pred[384,384]{0,1:T(8,128)(4,1)} %copy-done.11) | copy-start | bytes 442372
  43.3 20.4 %copy-start.7 = (bf16[4,384,384]{1,2,0:T(8,128)(2,1)}, bf16[4,384,384]{1,2,0:T(8,128)(2,1)S(1)}, u32[]{:S(2)}) copy-start(bf16[4,384,384]{1,2,0:T(8,128)(2,1)S(1)} %fusion.11) | copy-start | bytes 3538948
  43.3 6.1 %copy-start.16 = (bf16[2,384,128]{2,1,0:T(8,128)(2,1)S(1)}, bf16[2,384,128]{2,1,0:T(8,128)(2,1)}, u32[]{:S(2)}) copy-start(bf16[2,384,128]{2,1,0:T(8,128)(2,1)} %copy-done.15) | copy-start | bytes 589828
  45.8 29.8 %collective-permute-start.3 = (bf16[2,384,128]{2,1,0:T(8,128)(2,1)S(1)}, bf16[2,384,128]{2,1,0:T(8,128)(2,1)S(1)}, u32[]{:S(2)}, u32[]{:S(2)}) collective-permute-start(bf16[2,384,128]{2,1,0:T(8,128)(2,1)S(1)} %pad_maximum_fusion.1), channel_id=1, source_target_pairs={{8,0},{16,8},{24,16},{32,24},{40,32},{48,40},{56,48},{64,56},{72,6... | collective-permute-start | bytes 589832 | tf_op jit(solution)/shard_map/ppermute | solution.py:15
  50.9 24.7 %collective-permute-start.4 = (bf16[2,384,128]{2,1,0:T(8,128)(2,1)S(1)}, bf16[2,384,128]{2,1,0:T(8,128)(2,1)S(1)}, u32[]{:S(2)}, u32[]{:S(2)}) collective-permute-start(bf16[2,384,128]{2,1,0:T(8,128)(2,1)S(1)} %pad_maximum_fusion.2), channel_id=1, source_target_pairs={{16,0},{24,8},{32,16},{40,24},{48,32},{56,40},{64,48},{72,56},{80,... | collective-permute-start | bytes 589832 | tf_op jit(solution)/shard_map/ppermute | solution.py:15
  54.5 21.1 %collective-permute-start.5 = (bf16[2,384,128]{2,1,0:T(8,128)(2,1)S(1)}, bf16[2,384,128]{2,1,0:T(8,128)(2,1)S(1)}, u32[]{:S(2)}, u32[]{:S(2)}) collective-permute-start(bf16[2,384,128]{2,1,0:T(8,128)(2,1)S(1)} %pad_maximum_fusion.3), channel_id=1, source_target_pairs={{24,0},{32,8},{40,16},{48,24},{56,32},{64,40},{72,48},{80,56},{88,... | collective-permute-start | bytes 589832 | tf_op jit(solution)/shard_map/ppermute | solution.py:15
  66.4 8.8 %copy-start.8 = (bf16[4,384,384]{1,2,0:T(8,128)(2,1)S(1)}, bf16[4,384,384]{1,2,0:T(8,128)(2,1)}, u32[]{:S(2)}) copy-start(bf16[4,384,384]{1,2,0:T(8,128)(2,1)} %copy-done.7) | copy-start | bytes 3538948
  67.0 8.6 %copy-start.19 = (f32[1,384,128]{2,1,0:T(8,128)S(1)}, f32[1,384,128]{2,1,0:T(8,128)}, u32[]{:S(2)}) copy-start(f32[1,384,128]{2,1,0:T(8,128)} %convolution_bitcast_fusion.10) | copy-start | bytes 589828
  68.2 22.1 %all-to-all-start.1 = ((bf16[8,48,512]{2,1,0:T(8,128)(2,1)}), bf16[8,48,512]{2,1,0:T(8,128)(2,1)S(1)}, u32[]{:S(2)}, u32[]{:S(2)}) async-start(bf16[8,48,512]{2,1,0:T(8,128)(2,1)} %all_to_all.29), calls=%async_computation.1 | async-start | bytes 786432 | tf_op jit(solution)/shard_map/all_to_all | solution.py:103
  (6 other events, 7.1 us)
where the time goes:
time: 91.9 us; the launch traced here: 91.1 us
  starting transfers between devices  38.8 us (42%)
  matrix products  20.2 us (22%)
  waiting for transfers between devices  16.1 us (18%)
  local copies, waits for them, and re-layouts  11.1 us (12%)
  other arithmetic  3.84 us (4%)
  between operations  1.11 us (1%)
    ppermute x6, starting transfers between devices, passed_along(): return lax.ppermute(value, axis, pairs)  25 us
    all_to_all x1, waiting for transfers between devices, body(): lax.all_to_all(grad_query, 'kvh', split_axis=0, concat_axis=1, tiled=True)  13.9 us
    all_to_all x1, starting transfers between devices, body(): lax.all_to_all(grad_query, 'kvh', split_axis=0, concat_axis=1, tiled=True)  6.92 us
    all_to_all x1, starting transfers between devices, body(): lax.all_to_all(grad_output, 'kvh', split_axis=1, concat_axis=0, tiled=True)  6.82 us
    dot_general x4, matrix products, backward(): jnp.einsum('tjd,pd->jtp', grad_heads, key_value[1], preferred_element_typ...  4.81 us
    dot_general x4, matrix products, attend(): jnp.einsum('jtp,pd->jtd', weight_b, carried[distance][1], preferred_eleme...  4.24 us
    unnamed x44, local copies, waits for them, and re-layouts  3.81 us
    dot_general x4, matrix products, backward(): jnp.einsum('jtp,pd->tjd', dscore, key_value[0], preferred_element_type=jn...  3.2 us
  transfers between devices with their start and end apart: 8, of which 3 were waited for; matrix products, arithmetic and copies ran while one was open for 21% of the time, Pallas kernels for 0%

commit v1 on v0

v1 whole, which is shorter than its diff:
```python
import math

import jax
import jax.numpy as jnp
from jax import lax
from jax.experimental import pallas as pl
from jax.experimental.pallas import tpu as pltpu
from jax.sharding import PartitionSpec as P

HEAD = 128
GROUP = 4
BLOCK = 128
OWN = 3
REACH = 9
WINDOW = REACH + OWN - 1
WIDE = GROUP * BLOCK
SPAN = OWN * BLOCK
TAIL = 2 * BLOCK
INV_ROOT = HEAD ** (-0.5)
MIB = 2**20

NT = (((1,), (1,)), ((), ()))
NN = (((1,), (0,)), ((), ()))
VMEM = pl.BlockSpec(memory_space=pltpu.VMEM)
HBM = pl.BlockSpec(memory_space=pltpu.HBM)


def dot(a, b, dims):
    return lax.dot_general(a, b, dims, preferred_element_type=jnp.float32)


def block(index, count=1):
    return slice(index * BLOCK, (index + count) * BLOCK)


def heads_stacked(value):
    return jnp.concatenate([value[:, block(h)] for h in range(GROUP)], axis=0)


def started(pairs, sems):
    copies = [pltpu.make_async_copy(a, b, sems.at[n]) for n, (a, b) in enumerate(pairs)]
    for copy in copies:
        copy.start()
    return copies


def finish(copies):
    for copy in copies:
        copy.wait()


def peer_at(position, parts):
    return lax.rem(position + lax.rem(lax.axis_index("ctx"), 2) * (parts // 2), parts)


def on_odd_core():
    return lax.rem(lax.axis_index("ctx"), 2) == 1


def peer_cols(position, parts):
    return pl.ds(pl.multiple_of(peer_at(position, parts) * WIDE, WIDE), WIDE)


def prepare_kernel(grad_hbm, key_hbm, value_hbm, chunks, pair, tail, sems):
    parts = chunks.shape[0]
    last = slice(SPAN - TAIL, SPAN)
    moves = [
        (key_hbm, pair.at[:, :HEAD]),
        (value_hbm, pair.at[:, HEAD:]),
        (key_hbm.at[last, :], tail.at[:, :HEAD]),
        (value_hbm.at[last, :], tail.at[:, HEAD:]),
    ]
    for p in range(parts):
        moves.append((grad_hbm.at[:, peer_cols(p, parts)], chunks.at[p]))
    finish(started(moves, sems))


def put_window(part, win, own, beside, before, across, apart):
    cols = block(part)
    win[TAIL + 2 * SPAN :, :] = own[:, cols]
    win[TAIL : TAIL + SPAN, :] = before[:, cols]
    odd = on_odd_core()

    @pl.when(odd)
    def _():
        win[TAIL + SPAN : TAIL + 2 * SPAN, :] = beside[:, cols]
        win[0:TAIL, :] = across[SPAN - TAIL :, cols]

    @pl.when(jnp.logical_not(odd))
    def _():
        win[TAIL + SPAN : TAIL + 2 * SPAN, :] = across[:, cols]
        win[0:TAIL, :] = apart[:, cols]


def weight_copy(source, target, sems, i):
    mine = block(i * REACH, REACH)
    return pltpu.make_async_copy(source.at[mine, :], target.at[mine, :], sems.at[i])


def forward_kernel(
    start_hbm, query_hbm, own, beside, before, across, apart,
    weight_hbm, attended_ref, inverse_ref,
    start_ref, query_ref, key_win, value_win, value_t, held, weight_ref, sems, weight_sems
):
    arriving = started([(query_hbm, query_ref), (start_hbm, start_ref)], sems)
    put_window(0, key_win, own, beside, before, across, apart)
    put_window(1, value_win, own, beside, before, across, apart)
    value_t[...] = value_win[...].T
    first = lax.axis_index("ctx") * SPAN - (REACH - 1) * BLOCK
    to_exp2 = INV_ROOT * math.log2(math.e)
    key_at = lax.broadcasted_iota(jnp.int32, (BLOCK, WIDE), 0)
    query_at = lax.broadcasted_iota(jnp.int32, (BLOCK, WIDE), 1) & (BLOCK - 1)
    causal = key_at <= query_at
    finish(arriving)
    for i in range(OWN):
        queries_t = heads_stacked(query_ref[block(i), :]).T
        start = start_ref[i]
        best = jnp.full((8, WIDE), -jnp.inf, jnp.float32)
        for j in range(REACH):
            score = dot(key_win[block(i + j), :], queries_t, NN)
            allowed = causal if j == REACH - 1 else first + (i + j) * BLOCK >= start
            score = jnp.where(allowed, score, -jnp.inf)
            held[block(j), :] = score
            best = jnp.maximum(best, jnp.max(score.reshape(BLOCK // 8, 8, WIDE), axis=0))
        best = jnp.max(best, axis=0, keepdims=True)
        total = jnp.zeros((8, WIDE), jnp.float32)
        for j in range(REACH):
            part = jnp.exp2((held[block(j), :] - best) * to_exp2)
            total = total + jnp.sum(part.reshape(BLOCK // 8, 8, WIDE), axis=0)
            weight_ref[block(i * REACH + j), :] = part.astype(jnp.bfloat16)
        weight_copy(weight_ref, weight_hbm, weight_sems, i).start()
        inverse = 1.0 / jnp.sum(total, axis=0, keepdims=True)
        attended_ref[block(i), :] = (
            dot(value_t[:, block(i, REACH)], weight_ref[block(i * REACH, REACH), :], NN) * inverse
        ).astype(jnp.bfloat16)
        for h in range(GROUP):
            inverse_ref[block(i * GROUP + h), :] = jnp.broadcast_to(
                inverse[:, block(h)], (BLOCK, BLOCK)
            ).T
    for i in range(OWN):
        weight_copy(weight_ref, weight_hbm, weight_sems, i).wait()


def backward_kernel(
    query_hbm, weight_hbm, chunks, own, beside, before, across, apart, attended_ref, inverse_ref,
    dchunks, dnear_far, dmid, dfar, down,
    query_ref, weight_ref, grad_ref, key_win, value_win, key_t, held, dkey, dvalue, dquery,
    sems, weight_sems
):
    parts, share = chunks.shape[0], chunks.shape[1]

    def share_rows(p):
        return pl.ds(pl.multiple_of(peer_at(p, parts) * share, share), share)

    weights_in = [weight_copy(weight_hbm, weight_ref, weight_sems, i) for i in range(OWN)]
    query_in = started([(query_hbm, query_ref)], sems)
    for copy in weights_in:
        copy.start()
    for p in range(parts):
        grad_ref[share_rows(p), :] = chunks[p]
    put_window(1, value_win, own, beside, before, across, apart)
    put_window(0, key_win, own, beside, before, across, apart)
    key_t[...] = key_win[...].T
    finish(query_in)
    on_diagonal = lax.broadcasted_iota(jnp.int32, (BLOCK, BLOCK), 0) == lax.broadcasted_iota(
        jnp.int32, (BLOCK, BLOCK), 1
    )
    for i in range(OWN):
        queries = heads_stacked(query_ref[block(i), :])
        grads = (
            heads_stacked(grad_ref[block(i), :]).astype(jnp.float32)
            * inverse_ref[block(i * GROUP, GROUP), :]
        ).astype(jnp.bfloat16)
        grads_t = grads.T
        deltas = []
        for h in range(GROUP):
            cross = dot(grads[block(h), :], attended_ref[block(i), block(h)], NN)
            deltas.append(jnp.sum(jnp.where(on_diagonal, cross, 0.0), axis=0, keepdims=True))
        delta = jnp.concatenate(deltas, axis=1)
        weights_in[i].wait()
        for j in range(REACH):
            dweight = dot(value_win[block(i + j), :], grads_t, NN)
            weight = weight_ref[block(i * REACH + j), :]
            held[block(i * REACH + j), :] = (
                weight.astype(jnp.float32) * (dweight - delta)
            ).astype(jnp.bfloat16)
        mine = block(i * REACH, REACH)
        turned = dot(key_t[:, block(i, REACH)], held[mine, :], NN) * INV_ROOT
        for h in range(GROUP):
            dquery[block(i), block(h)] = turned[:, block(h)].T.astype(jnp.bfloat16)
        value_part = dot(weight_ref[mine, :], grads, NN)
        key_part = dot(held[mine, :], queries, NN)
        fresh = 0 if i == 0 else REACH - 1
        if fresh:
            seen = slice(0, fresh * BLOCK)
            dvalue[block(i, fresh), :] += value_part[seen, :]
            dkey[block(i, fresh), :] += key_part[seen, :]
        rest = slice(fresh * BLOCK, REACH * BLOCK)
        dvalue[block(i + fresh, REACH - fresh), :] = value_part[rest, :]
        dkey[block(i + fresh, REACH - fresh), :] = key_part[rest, :]
    for p in range(parts):
        dchunks[p] = dquery[share_rows(p), :]

    def put(ref, at, lo, count):
        to, span = slice(at, at + count), slice(lo, lo + count)
        ref[to, :HEAD] = (dkey[span, :] * INV_ROOT).astype(ref.dtype)
        ref[to, HEAD:] = dvalue[span, :].astype(ref.dtype)

    put(dnear_far, 0, TAIL + SPAN, SPAN)
    put(dnear_far, SPAN, 0, TAIL)
    put(dfar, 0, 0, TAIL)
    put(dmid, 0, TAIL, SPAN)
    put(down, 0, TAIL + 2 * SPAN, SPAN)


def merge_kernel(dmid, received, merged):
    odd = on_odd_core()
    f32 = jnp.float32

    @pl.when(odd)
    def _():
        merged[...] = (dmid[...].astype(f32) + received[:SPAN, :].astype(f32)).astype(merged.dtype)

    @pl.when(jnp.logical_not(odd))
    def _():
        head, last = slice(0, SPAN - TAIL), slice(SPAN - TAIL, SPAN)
        merged[head, :] = dmid[head, :]
        merged[last, :] = (
            dmid[last, :].astype(f32) + received[SPAN:, :].astype(f32)
        ).astype(merged.dtype)


def sum_kernel(down, received, shifted, apart, key_hbm, value_hbm, total, out, sems):
    odd = on_odd_core()
    f32 = jnp.float32
    total[...] = down[...] + shifted[...].astype(f32)

    @pl.when(odd)
    def _():
        total[SPAN - TAIL :, :] += apart[...].astype(f32)

    @pl.when(jnp.logical_not(odd))
    def _():
        total[...] += received[:SPAN, :].astype(f32)

    for part in range(2):
        out[part] = total[:, block(part)].astype(out.dtype)
    finish(started([(out.at[0], key_hbm), (out.at[1], value_hbm)], sems))


def place_kernel(chunks, out_hbm, sems):
    parts = chunks.shape[0]
    finish(
        started([(chunks.at[p], out_hbm.at[:, peer_cols(p, parts)]) for p in range(parts)], sems)
    )


def passed_along(value, by, parities=(0, 1)):
    length = lax.axis_size("ctx")
    pairs = [
        (i, i + by) for i in range(length) if 0 <= i + by < length and i % 2 in parities
    ]
    return lax.ppermute(value, "ctx", pairs)


def core_swapped(value):
    return lax.ppermute(value, "ctx", [(i, i ^ 1) for i in range(lax.axis_size("ctx"))])


def pinned(*arrays):
    return [pltpu.with_memory_space_constraint(x, pltpu.HBM) for x in arrays]


def cost(flops, exps=0):
    return pl.CostEstimate(flops=int(flops), bytes_accessed=8 * MIB, transcendentals=int(exps))


def params(mib):
    return pltpu.CompilerParams(vmem_limit_bytes=mib * MIB)


def body(query_states, key_states, value_states, grad_output, doc_start):
    parts, length = lax.axis_size("kvh"), lax.axis_size("ctx")
    share = SPAN // parts
    bf16, f32 = jnp.bfloat16, jnp.float32
    sds = jax.ShapeDtypeStruct
    dma = pltpu.SemaphoreType.DMA
    window = WINDOW * BLOCK
    pairs = OWN * REACH
    flops = 2 * pairs * BLOCK * BLOCK * WIDE
    chunked = sds((parts, share, WIDE), bf16)
    pair = sds((SPAN, 2 * HEAD), bf16)
    tail = sds((TAIL, 2 * HEAD), bf16)
    rings = [
        [c * parts + (p + (c % 2) * (parts // 2)) % parts for p in range(parts)]
        for c in range(length)
    ]

    def exchanged(value):
        return lax.all_to_all(
            value, ("ctx", "kvh"), split_axis=0, concat_axis=0, axis_index_groups=rings, tiled=True
        )

    start_hbm, query_hbm = pinned(doc_start, query_states)
    chunks, own, last = pl.pallas_call(
        prepare_kernel,
        out_shape=(chunked, pair, tail),
        in_specs=[HBM] * 3,
        out_specs=(VMEM,) * 3,
        scratch_shapes=[dma((parts + 4,))],
        compiler_params=params(4),
        name="prepare",
    )(*pinned(grad_output, key_states, value_states))
    grads = exchanged(chunks)
    before = passed_along(own, 2)
    apart = passed_along(last, 3, (1,))
    beside = passed_along(own, 1, (0,))
    across = core_swapped(before)
    halo = (own, beside, before, across, apart)

    weight, attended, inverse = pl.pallas_call(
        forward_kernel,
        out_shape=(
            sds((pairs * BLOCK, WIDE), bf16),
            sds((OWN * HEAD, WIDE), bf16),
            sds((OWN * WIDE, HEAD), f32),
        ),
        in_specs=[HBM, HBM] + [VMEM] * 5,
        out_specs=(HBM, VMEM, VMEM),
        scratch_shapes=[
            pltpu.SMEM(doc_start.shape, jnp.int32),
            pltpu.VMEM((SPAN, WIDE), bf16),
            pltpu.VMEM((window, HEAD), bf16),
            pltpu.VMEM((window, HEAD), bf16),
            pltpu.VMEM((HEAD, window), bf16),
            pltpu.VMEM((REACH * BLOCK, WIDE), f32),
            pltpu.VMEM((pairs * BLOCK, WIDE), bf16),
            dma((2,)),
            dma((OWN,)),
        ],
        cost_estimate=cost(2 * flops, pairs * BLOCK * WIDE),
        compiler_params=params(16),
        name="forward",
    )(start_hbm, query_hbm, *halo)

    dchunks, dnear_far, dmid, dfar, down = pl.pallas_call(
        backward_kernel,
        out_shape=(
            chunked,
            sds((SPAN + TAIL, 2 * HEAD), bf16),
            pair,
            tail,
            sds((SPAN, 2 * HEAD), f32),
        ),
        in_specs=[HBM, HBM] + [VMEM] * 8,
        out_specs=(VMEM,) * 5,
        scratch_shapes=[
            pltpu.VMEM((SPAN, WIDE), bf16),
            pltpu.VMEM((pairs * BLOCK, WIDE), bf16),
            pltpu.VMEM((SPAN, WIDE), bf16),
            pltpu.VMEM((window, HEAD), bf16),
            pltpu.VMEM((window, HEAD), bf16),
            pltpu.VMEM((HEAD, window), bf16),
            pltpu.VMEM((pairs * BLOCK, WIDE), bf16),
            pltpu.VMEM((window, HEAD), f32),
            pltpu.VMEM((window, HEAD), f32),
            pltpu.VMEM((SPAN, WIDE), bf16),
            dma((1,)),
            dma((OWN,)),
        ],
        cost_estimate=cost(4 * flops),
        compiler_params=params(24),
        name="backward",
    )(query_hbm, *pinned(weight), grads, *halo, attended, inverse)

    back = exchanged(dchunks)
    received = core_swapped(dnear_far)
    far_back = passed_along(dfar, -3, (0,))
    merged = pl.pallas_call(
        merge_kernel,
        out_shape=pair,
        in_specs=[VMEM] * 2,
        out_specs=VMEM,
        compiler_params=params(4),
        name="merge",
    )(dmid, received)
    shifted = passed_along(merged, -2)
    grad_key, grad_value = pl.pallas_call(
        sum_kernel,
        out_shape=(sds((SPAN, HEAD), bf16),) * 2,
        in_specs=[VMEM] * 4,
        out_specs=(HBM,) * 2,
        scratch_shapes=[
            pltpu.VMEM((SPAN, 2 * HEAD), f32), pltpu.VMEM((2, SPAN, HEAD), bf16), dma((2,))
        ],
        compiler_params=params(4),
        name="sum",
    )(down, received, shifted, far_back)
    grad_query = pl.pallas_call(
        place_kernel,
        out_shape=sds((share, parts * WIDE), bf16),
        in_specs=[VMEM],
        out_specs=HBM,
        scratch_shapes=[dma((parts,))],
        compiler_params=params(4),
        name="place",
    )(back)
    return grad_query, grad_key, grad_value


def solution(mesh):
    in_specs = (
        P("ctx", "kvh"),
        P("ctx", "kvh"),
        P("ctx", "kvh"),
        P(("ctx", "kvh"), None),
        P("ctx"),
    )
    out_specs = (P(("ctx", "kvh"), None), P("ctx", "kvh"), P("ctx", "kvh"))
    return jax.shard_map(body, mesh=mesh, in_specs=in_specs, out_specs=out_specs, check_vma=False)
```

time: 91.9 us -> 71 us (0.77)
  the two profiles are of different devices: /device:TPU:261 before, /device:TPU:205 now
where the time goes in v1:
time: 71 us; the launch traced here: 70.5 us
  starting transfers between devices  34.8 us (49%)
  waiting for transfers between devices  18.1 us (25%)
  Pallas kernels  15.1 us (21%)
  local copies, waits for them, and re-layouts  1.74 us (2%)
  between operations  0.75 us (1%)
    ppermute x5, waiting for transfers between devices, passed_along(): return lax.ppermute(value, 'ctx', pairs)  16.5 us
    ppermute x5, starting transfers between devices, passed_along(): return lax.ppermute(value, 'ctx', pairs)  15.7 us
    all_to_all x2, starting transfers between devices, exchanged(): lax.all_to_all(value, ('ctx', 'kvh'), split_axis=0, concat_axis=0, axis_i...  14.2 us
    pallas_call x1, Pallas kernels, body(): pl.pallas_call(backward_kernel, out_shape=(chunked, sds((SPAN + TAIL, 2 *...  6.5 us
    pallas_call x1, Pallas kernels, body(): pl.pallas_call(forward_kernel, out_shape=(sds((pairs * BLOCK, WIDE), bf16...  5.02 us
    ppermute x2, starting transfers between devices, core_swapped(): lax.ppermute(value, 'ctx', [(i, i ^ 1) for i in range(lax.axis_size('ctx'...  4.94 us
    pallas_call x1, Pallas kernels, body(): pl.pallas_call(prepare_kernel, out_shape=(chunked, pair, tail), in_specs=...  1.95 us
    unnamed x2, local copies, waits for them, and re-layouts  1.74 us
  transfers between devices with their start and end apart: 9, of which 4 were waited for; matrix products, arithmetic and copies ran while one was open for 0% of the time, Pallas kernels for 8%

profile of v1, /device:TPU:205, one launch (start us, length us, event | category | flops | bytes accessed | tf_op | source)
XLA Modules:
  0.0 70.5 jit_solution(16097989097774236751)
XLA Ops:
  0.6 1.9 %prepare.1 = (bf16[8,48,512]{2,1,0:T(8,128)(2,1)}, bf16[384,256]{1,0:T(8,128)(2,1)S(1)}, bf16[256,256]{1,0:T(8,128)(2,1)S(1)}) custom-call(bf16[48,4096]{1,0:T(8,128)(2,1)} %grad_hbm.1, bf16[384,128]{1,0:T(8,128)(2,1)} %key_hbm.1, bf16[384,128]{1,0:T(8,128)(2,1)} %value_hbm.1), custom_call_target="tpu_custom_call" | custom-call | tf_op jit(solution)/shard_map/prepare/pallas_call | solution.py:305
  2.6 7.9 %all-to-all-start = ((bf16[8,48,512]{2,1,0:T(8,128)(2,1)}), bf16[8,48,512]{2,1,0:T(8,128)(2,1)S(1)}, u32[]{:S(2)}, u32[]{:S(2)}) async-start(bf16[8,48,512]{2,1,0:T(8,128)(2,1)} %get-tuple-element.19), calls=%async_computation | async-start | bytes 786432 | tf_op jit(solution)/shard_map/all_to_all | solution.py:300
  10.5 2.8 %collective-permute-start.1 = (bf16[384,256]{1,0:T(8,128)(2,1)S(1)}, bf16[384,256]{1,0:T(8,128)(2,1)S(1)}, u32[]{:S(2)}, u32[]{:S(2)}) collective-permute-start(bf16[384,256]{1,0:T(8,128)(2,1)S(1)} %get-tuple-element.16.own), channel_id=1, source_target_pairs={{0,16},{8,24},{16,32},{24,40},{32,48},{40,56},{48,64},{56,72},{64,... | collective-permute-start | bytes 589832 | tf_op jit(solution)/shard_map/ppermute | solution.py:263
  13.3 1.3 %collective-permute-start = (bf16[384,256]{1,0:T(8,128)(2,1)S(1)}, bf16[384,256]{1,0:T(8,128)(2,1)S(1)}, u32[]{:S(2)}, u32[]{:S(2)}) collective-permute-start(bf16[384,256]{1,0:T(8,128)(2,1)S(1)} %get-tuple-element.16.own), channel_id=1, source_target_pairs={{0,8},{16,24},{32,40},{48,56},{64,72},{80,88},{96,104},{112,120},{... | collective-permute-start | bytes 589832 | tf_op jit(solution)/shard_map/ppermute | solution.py:263
  14.6 3.9 %collective-permute-done.1.before = bf16[384,256]{1,0:T(8,128)(2,1)S(1)} collective-permute-done((bf16[384,256]{1,0:T(8,128)(2,1)S(1)}, bf16[384,256]{1,0:T(8,128)(2,1)S(1)}, u32[]{:S(2)}, u32[]{:S(2)}) %collective-permute-start.1) | collective-permute-done | bytes 196640 | tf_op jit(solution)/shard_map/ppermute | solution.py:263
  18.6 3.0 %collective-permute-start.2 = (bf16[384,256]{1,0:T(8,128)(2,1)S(1)}, bf16[384,256]{1,0:T(8,128)(2,1)S(1)}, u32[]{:S(2)}, u32[]{:S(2)}) collective-permute-start(bf16[384,256]{1,0:T(8,128)(2,1)S(1)} %collective-permute-done.1.before), channel_id=1, source_target_pairs={{0,8},{8,0},{16,24},{24,16},{32,40},{40,32},{48,56},{56,48},{64,72... | collective-permute-start | bytes 589832 | tf_op jit(solution)/shard_map/ppermute | solution.py:267
  21.6 8.4 %collective-permute-start.3 = (bf16[256,256]{1,0:T(8,128)(2,1)S(1)}, bf16[256,256]{1,0:T(8,128)(2,1)S(1)}, u32[]{:S(2)}, u32[]{:S(2)}) collective-permute-start(bf16[256,256]{1,0:T(8,128)(2,1)S(1)} %get-tuple-element.17), channel_id=1, source_target_pairs={{8,32},{24,48},{40,64},{56,80},{72,96},{88,112},{104,128},{120,144... | collective-permute-start | bytes 393224 | tf_op jit(solution)/shard_map/ppermute | solution.py:263
  30.0 1.9 %collective-permute-done.3.apart = bf16[256,256]{1,0:T(8,128)(2,1)S(1)} collective-permute-done((bf16[256,256]{1,0:T(8,128)(2,1)S(1)}, bf16[256,256]{1,0:T(8,128)(2,1)S(1)}, u32[]{:S(2)}, u32[]{:S(2)}) %collective-permute-start.3) | collective-permute-done | bytes 131104 | tf_op jit(solution)/shard_map/ppermute | solution.py:263
  31.9 0.0 collective-permute-done.beside
  31.9 0.0 collective-permute-done.2.across
  31.9 5.0 %forward.1 = (bf16[3456,512]{1,0:T(8,128)(2,1)S(1)}, bf16[384,512]{1,0:T(8,128)(2,1)S(1)}, f32[1536,128]{1,0:T(8,128)S(1)}) custom-call(s32[3]{0:T(128)} %start_hbm.1, bf16[384,512]{1,0:T(8,128)(2,1)} %query_hbm.3, bf16[384,256]{1,0:T(8,128)(2,1)S(1)} %get-tuple-element.16.own, bf16[384,256]{1,0:T(8,128)(2,1)S(1)} %collective-permute-done.beside, ...), custom_call_target="tpu_custom_call" | custom-call | flops 905969664 | bytes 8388608 | tf_op jit(solution)/shard_map/forward/pallas_call | solution.py:321
  37.0 1.7 %copy-done = bf16[3456,512]{1,0:T(8,128)(2,1)} copy-done((bf16[3456,512]{1,0:T(8,128)(2,1)}, bf16[3456,512]{1,0:T(8,128)(2,1)S(1)}, u32[]{:S(2)}) %copy-start) | copy-done | bytes 3538968
  38.7 0.0 all-to-all-done.chunks
  38.7 6.5 %backward.1 = (bf16[8,48,512]{2,1,0:T(8,128)(2,1)}, bf16[640,256]{1,0:T(8,128)(2,1)S(1)}, bf16[384,256]{1,0:T(8,128)(2,1)S(1)}, bf16[256,256]{1,0:T(8,128)(2,1)S(1)}, f32[384,256]{1,0:T(8,128)S(1)}) custom-call(bf16[384,512]{1,0:T(8,128)(2,1)} %query_hbm.3, bf16[3456,512]{1,0:T(8,128)(2,1)} %copy-done, bf16[8,48,512]{2,1,0:T(8,128)(2,1)S(1)} %all-to-all-done.chunks, ...), custom_call_target="tpu_custom_call" | custom-call | flops 1811939328 | bytes 8388608 | tf_op jit(solution)/shard_map/backward/pallas_call | solution.py:346
  45.2 6.2 %all-to-all-start.1 = ((bf16[8,48,512]{2,1,0:T(8,128)(2,1)}), bf16[8,48,512]{2,1,0:T(8,128)(2,1)S(1)}, u32[]{:S(2)}, u32[]{:S(2)}) async-start(bf16[8,48,512]{2,1,0:T(8,128)(2,1)} %get-tuple-element.22), calls=%async_computation.1 | async-start | bytes 786432 | tf_op jit(solution)/shard_map/all_to_all | solution.py:300
  51.5 1.9 %collective-permute-start.4 = (bf16[640,256]{1,0:T(8,128)(2,1)S(1)}, bf16[640,256]{1,0:T(8,128)(2,1)S(1)}, u32[]{:S(2)}, u32[]{:S(2)}) collective-permute-start(bf16[640,256]{1,0:T(8,128)(2,1)S(1)} %get-tuple-element.24), channel_id=1, source_target_pairs={{0,8},{8,0},{16,24},{24,16},{32,40},{40,32},{48,56},{56,48},{64,72... | collective-permute-start | bytes 983048 | tf_op jit(solution)/shard_map/ppermute | solution.py:267
  53.4 1.6 %collective-permute-done.4.received = bf16[640,256]{1,0:T(8,128)(2,1)S(1)} collective-permute-done((bf16[640,256]{1,0:T(8,128)(2,1)S(1)}, bf16[640,256]{1,0:T(8,128)(2,1)S(1)}, u32[]{:S(2)}, u32[]{:S(2)}) %collective-permute-start.4) | collective-permute-done | bytes 327712 | tf_op jit(solution)/shard_map/ppermute | solution.py:267
  55.0 1.9 %collective-permute-start.5 = (bf16[384,256]{1,0:T(8,128)(2,1)S(1)}, bf16[384,256]{1,0:T(8,128)(2,1)S(1)}, u32[]{:S(2)}, u32[]{:S(2)}) collective-permute-start(bf16[384,256]{1,0:T(8,128)(2,1)S(1)} %merge.1), channel_id=1, source_target_pairs={{16,0},{24,8},{32,16},{40,24},{48,32},{56,40},{64,48},{72,56},{80,... | collective-permute-start | bytes 589832 | tf_op jit(solution)/shard_map/ppermute | solution.py:263
  57.0 1.3 %collective-permute-start.6 = (bf16[256,256]{1,0:T(8,128)(2,1)S(1)}, bf16[256,256]{1,0:T(8,128)(2,1)S(1)}, u32[]{:S(2)}, u32[]{:S(2)}) collective-permute-start(bf16[256,256]{1,0:T(8,128)(2,1)S(1)} %get-tuple-element.26), channel_id=1, source_target_pairs={{32,8},{48,24},{64,40},{80,56},{96,72},{112,88},{128,104},{144,120... | collective-permute-start | bytes 393224 | tf_op jit(solution)/shard_map/ppermute | solution.py:263
  58.3 10.7 %collective-permute-done.6.apart = bf16[256,256]{1,0:T(8,128)(2,1)S(1)} collective-permute-done((bf16[256,256]{1,0:T(8,128)(2,1)S(1)}, bf16[256,256]{1,0:T(8,128)(2,1)S(1)}, u32[]{:S(2)}, u32[]{:S(2)}) %collective-permute-start.6) | collective-permute-done | bytes 131104 | tf_op jit(solution)/shard_map/ppermute | solution.py:263
  68.9 0.0 collective-permute-done.5.shifted
  68.9 0.8 %sum.1 = (bf16[384,128]{1,0:T(8,128)(2,1)}, bf16[384,128]{1,0:T(8,128)(2,1)}) custom-call(f32[384,256]{1,0:T(8,128)S(1)} %get-tuple-element.23.down, bf16[640,256]{1,0:T(8,128)(2,1)S(1)} %collective-permute-done.4.received, bf16[384,256]{1,0:T(8,128)(2,1)S(1)} %collective-permute-done.5.shifted, bf16[256,256]{1,0:T(8,128)(2,1)S(1)} %collective-permute-done.6.apart), custom_call_target="tpu_custom_call" | custom-call | tf_op jit(solution)/shard_map/sum/pallas_call | solution.py:388
  69.7 0.0 all-to-all-done.1.chunks
  69.7 0.8 %place.1 = bf16[48,4096]{1,0:T(8,128)(2,1)} custom-call(bf16[8,48,512]{2,1,0:T(8,128)(2,1)S(1)} %all-to-all-done.1.chunks), custom_call_target="tpu_custom_call" | custom-call | tf_op jit(solution)/shard_map/place/pallas_call | solution.py:399
  (2 shorter events, 0.1 us)
Async XLA Ops:
  2.6 36.1 %all-to-all-start = ((bf16[8,48,512]{2,1,0:T(8,128)(2,1)}), bf16[8,48,512]{2,1,0:T(8,128)(2,1)S(1)}, u32[]{:S(2)}, u32[]{:S(2)}) async-start(bf16[8,48,512]{2,1,0:T(8,128)(2,1)} %get-tuple-element.19), calls=%async_computation | async-start | bytes 786432 | tf_op jit(solution)/shard_map/all_to_all | solution.py:300
  10.5 8.1 %collective-permute-start.1 = (bf16[384,256]{1,0:T(8,128)(2,1)S(1)}, bf16[384,256]{1,0:T(8,128)(2,1)S(1)}, u32[]{:S(2)}, u32[]{:S(2)}) collective-permute-start(bf16[384,256]{1,0:T(8,128)(2,1)S(1)} %get-tuple-element.16.own), channel_id=1, source_target_pairs={{0,16},{8,24},{16,32},{24,40},{32,48},{40,56},{48,64},{56,72},{64,... | collective-permute-start | bytes 589832 | tf_op jit(solution)/shard_map/ppermute | solution.py:263
  13.3 18.6 %collective-permute-start = (bf16[384,256]{1,0:T(8,128)(2,1)S(1)}, bf16[384,256]{1,0:T(8,128)(2,1)S(1)}, u32[]{:S(2)}, u32[]{:S(2)}) collective-permute-start(bf16[384,256]{1,0:T(8,128)(2,1)S(1)} %get-tuple-element.16.own), channel_id=1, source_target_pairs={{0,8},{16,24},{32,40},{48,56},{64,72},{80,88},{96,104},{112,120},{... | collective-permute-start | bytes 589832 | tf_op jit(solution)/shard_map/ppermute | solution.py:263
  18.6 13.3 %collective-permute-start.2 = (bf16[384,256]{1,0:T(8,128)(2,1)S(1)}, bf16[384,256]{1,0:T(8,128)(2,1)S(1)}, u32[]{:S(2)}, u32[]{:S(2)}) collective-permute-start(bf16[384,256]{1,0:T(8,128)(2,1)S(1)} %collective-permute-done.1.before), channel_id=1, source_target_pairs={{0,8},{8,0},{16,24},{24,16},{32,40},{40,32},{48,56},{56,48},{64,72... | collective-permute-start | bytes 589832 | tf_op jit(solution)/shard_map/ppermute | solution.py:267
  21.6 10.3 %collective-permute-start.3 = (bf16[256,256]{1,0:T(8,128)(2,1)S(1)}, bf16[256,256]{1,0:T(8,128)(2,1)S(1)}, u32[]{:S(2)}, u32[]{:S(2)}) collective-permute-start(bf16[256,256]{1,0:T(8,128)(2,1)S(1)} %get-tuple-element.17), channel_id=1, source_target_pairs={{8,32},{24,48},{40,64},{56,80},{72,96},{88,112},{104,128},{120,144... | collective-permute-start | bytes 393224 | tf_op jit(solution)/shard_map/ppermute | solution.py:263
  37.0 1.7 %copy-start = (bf16[3456,512]{1,0:T(8,128)(2,1)}, bf16[3456,512]{1,0:T(8,128)(2,1)S(1)}, u32[]{:S(2)}) copy-start(bf16[3456,512]{1,0:T(8,128)(2,1)S(1)} %get-tuple-element.18.weight_hbm) | copy-start | bytes 10616836
  45.2 24.5 %all-to-all-start.1 = ((bf16[8,48,512]{2,1,0:T(8,128)(2,1)}), bf16[8,48,512]{2,1,0:T(8,128)(2,1)S(1)}, u32[]{:S(2)}, u32[]{:S(2)}) async-start(bf16[8,48,512]{2,1,0:T(8,128)(2,1)} %get-tuple-element.22), calls=%async_computation.1 | async-start | bytes 786432 | tf_op jit(solution)/shard_map/all_to_all | solution.py:300
  51.5 3.5 %collective-permute-start.4 = (bf16[640,256]{1,0:T(8,128)(2,1)S(1)}, bf16[640,256]{1,0:T(8,128)(2,1)S(1)}, u32[]{:S(2)}, u32[]{:S(2)}) collective-permute-start(bf16[640,256]{1,0:T(8,128)(2,1)S(1)} %get-tuple-element.24), channel_id=1, source_target_pairs={{0,8},{8,0},{16,24},{24,16},{32,40},{40,32},{48,56},{56,48},{64,72... | collective-permute-start | bytes 983048 | tf_op jit(solution)/shard_map/ppermute | solution.py:267
  55.0 13.9 %collective-permute-start.5 = (bf16[384,256]{1,0:T(8,128)(2,1)S(1)}, bf16[384,256]{1,0:T(8,128)(2,1)S(1)}, u32[]{:S(2)}, u32[]{:S(2)}) collective-permute-start(bf16[384,256]{1,0:T(8,128)(2,1)S(1)} %merge.1), channel_id=1, source_target_pairs={{16,0},{24,8},{32,16},{40,24},{48,32},{56,40},{64,48},{72,56},{80,... | collective-permute-start | bytes 589832 | tf_op jit(solution)/shard_map/ppermute | solution.py:263
  57.0 12.0 %collective-permute-start.6 = (bf16[256,256]{1,0:T(8,128)(2,1)S(1)}, bf16[256,256]{1,0:T(8,128)(2,1)S(1)}, u32[]{:S(2)}, u32[]{:S(2)}) collective-permute-start(bf16[256,256]{1,0:T(8,128)(2,1)S(1)} %get-tuple-element.26), channel_id=1, source_target_pairs={{32,8},{48,24},{64,40},{80,56},{96,72},{112,88},{128,104},{144,120... | collective-permute-start | bytes 393224 | tf_op jit(solution)/shard_map/ppermute | solution.py:263

commit v2 on v1

--- a/solution.py
+++ b/solution.py
@@ -61,8 +61,7 @@
     return pl.ds(pl.multiple_of(peer_at(position, parts) * WIDE, WIDE), WIDE)
 
 
-def prepare_kernel(grad_hbm, key_hbm, value_hbm, chunks, pair, tail, sems):
-    parts = chunks.shape[0]
+def pair_kernel(key_hbm, value_hbm, pair, tail, sems):
     last = slice(SPAN - TAIL, SPAN)
     moves = [
         (key_hbm, pair.at[:, :HEAD]),
@@ -70,9 +69,14 @@
         (key_hbm.at[last, :], tail.at[:, :HEAD]),
         (value_hbm.at[last, :], tail.at[:, HEAD:]),
     ]
-    for p in range(parts):
-        moves.append((grad_hbm.at[:, peer_cols(p, parts)], chunks.at[p]))
     finish(started(moves, sems))
+
+
+def chunk_kernel(grad_hbm, before, apart, chunks, sems):
+    parts = chunks.shape[0]
+    finish(
+        started([(grad_hbm.at[:, peer_cols(p, parts)], chunks.at[p]) for p in range(parts)], sems)
+    )
 
 
 def put_window(part, win, own, beside, before, across, apart):
@@ -99,13 +103,14 @@
 
 def forward_kernel(
     start_hbm, query_hbm, own, beside, before, across, apart,
-    weight_hbm, attended_ref, inverse_ref,
-    start_ref, query_ref, key_win, value_win, value_t, held, weight_ref, sems, weight_sems
+    weight_hbm, attended_ref, inverse_ref, value_win, key_t,
+    start_ref, query_ref, key_win, value_t, held, weight_ref, sems, weight_sems
 ):
     arriving = started([(query_hbm, query_ref), (start_hbm, start_ref)], sems)
     put_window(0, key_win, own, beside, before, across, apart)
     put_window(1, value_win, own, beside, before, across, apart)
     value_t[...] = value_win[...].T
+    key_t[...] = key_win[...].T
     first = lax.axis_index("ctx") * SPAN - (REACH - 1) * BLOCK
     to_exp2 = INV_ROOT * math.log2(math.e)
     key_at = lax.broadcasted_iota(jnp.int32, (BLOCK, WIDE), 0)
@@ -142,10 +147,9 @@
 
 
 def backward_kernel(
-    query_hbm, weight_hbm, chunks, own, beside, before, across, apart, attended_ref, inverse_ref,
+    query_hbm, weight_hbm, chunks, value_win, key_t, attended_ref, inverse_ref,
     dchunks, dnear_far, dmid, dfar, down,
-    query_ref, weight_ref, grad_ref, key_win, value_win, key_t, held, dkey, dvalue, dquery,
-    sems, weight_sems
+    query_ref, weight_ref, grad_ref, wide, held, dkey, dvalue, dquery, sems, weight_sems
 ):
     parts, share = chunks.shape[0], chunks.shape[1]
 
@@ -153,20 +157,15 @@
         return pl.ds(pl.multiple_of(peer_at(p, parts) * share, share), share)
 
     weights_in = [weight_copy(weight_hbm, weight_ref, weight_sems, i) for i in range(OWN)]
-    query_in = started([(query_hbm, query_ref)], sems)
     for copy in weights_in:
         copy.start()
+    query_in = started([(query_hbm, query_ref)], sems)
     for p in range(parts):
         grad_ref[share_rows(p), :] = chunks[p]
-    put_window(1, value_win, own, beside, before, across, apart)
-    put_window(0, key_win, own, beside, before, across, apart)
-    key_t[...] = key_win[...].T
-    finish(query_in)
     on_diagonal = lax.broadcasted_iota(jnp.int32, (BLOCK, BLOCK), 0) == lax.broadcasted_iota(
         jnp.int32, (BLOCK, BLOCK), 1
     )
     for i in range(OWN):
-        queries = heads_stacked(query_ref[block(i), :])
         grads = (
             heads_stacked(grad_ref[block(i), :]).astype(jnp.float32)
             * inverse_ref[block(i * GROUP, GROUP), :]
@@ -177,13 +176,21 @@
             cross = dot(grads[block(h), :], attended_ref[block(i), block(h)], NN)
             deltas.append(jnp.sum(jnp.where(on_diagonal, cross, 0.0), axis=0, keepdims=True))
         delta = jnp.concatenate(deltas, axis=1)
+
+        def slope(j):
+            return dot(value_win[block(i + j), :], grads_t, NN) - delta
+
+        if i == 0:
+            for j in range(REACH):
+                wide[block(j), :] = slope(j)
+            finish(query_in)
         weights_in[i].wait()
         for j in range(REACH):
-            dweight = dot(value_win[block(i + j), :], grads_t, NN)
-            weight = weight_ref[block(i * REACH + j), :]
+            weight = weight_ref[block(i * REACH + j), :].astype(jnp.float32)
             held[block(i * REACH + j), :] = (
-                weight.astype(jnp.float32) * (dweight - delta)
+                weight * (wide[block(j), :] if i == 0 else slope(j))
             ).astype(jnp.bfloat16)
+        queries = heads_stacked(query_ref[block(i), :])
         mine = block(i * REACH, REACH)
         turned = dot(key_t[:, block(i, REACH)], held[mine, :], NN) * INV_ROOT
         for h in range(GROUP):
@@ -230,19 +237,23 @@
         ).astype(merged.dtype)
 
 
-def sum_kernel(down, received, shifted, apart, key_hbm, value_hbm, total, out, sems):
+def fold_kernel(down, received, apart, folded):
     odd = on_odd_core()
     f32 = jnp.float32
-    total[...] = down[...] + shifted[...].astype(f32)
 
     @pl.when(odd)
     def _():
-        total[SPAN - TAIL :, :] += apart[...].astype(f32)
+        head, last = slice(0, SPAN - TAIL), slice(SPAN - TAIL, SPAN)
+        folded[head, :] = down[head, :]
+        folded[last, :] = down[last, :] + apart[...].astype(f32)
 
     @pl.when(jnp.logical_not(odd))
     def _():
-        total[...] += received[:SPAN, :].astype(f32)
-
+        folded[...] = down[...] + received[:SPAN, :].astype(f32)
+
+
+def sum_kernel(folded, shifted, key_hbm, value_hbm, out, sems):
+    total = folded[...] + shifted[...].astype(jnp.float32)
     for part in range(2):
         out[part] = total[:, block(part)].astype(out.dtype)
     finish(started([(out.at[0], key_hbm), (out.at[1], value_hbm)], sems))
@@ -302,35 +313,45 @@
         )
 
     start_hbm, query_hbm = pinned(doc_start, query_states)
-    chunks, own, last = pl.pallas_call(
-        prepare_kernel,
-        out_shape=(chunked, pair, tail),
-        in_specs=[HBM] * 3,
-        out_specs=(VMEM,) * 3,
-        scratch_shapes=[dma((parts + 4,))],
-        compiler_params=params(4),
-        name="prepare",
-    )(*pinned(grad_output, key_states, value_states))
-    grads = exchanged(chunks)
+    own, last = pl.pallas_call(
+        pair_kernel,
+        out_shape=(pair, tail),
+        in_specs=[HBM] * 2,
+        out_specs=(VMEM,) * 2,
+        scratch_shapes=[dma((4,))],
+        compiler_params=params(4),
+        name="pair",
+    )(*pinned(key_states, value_states))
     before = passed_along(own, 2)
     apart = passed_along(last, 3, (1,))
     beside = passed_along(own, 1, (0,))
     across = core_swapped(before)
     halo = (own, beside, before, across, apart)
-
-    weight, attended, inverse = pl.pallas_call(
+    chunks = pl.pallas_call(
+        chunk_kernel,
+        out_shape=chunked,
+        in_specs=[HBM, VMEM, VMEM],
+        out_specs=VMEM,
+        scratch_shapes=[dma((parts,))],
+        compiler_params=params(4),
+        name="chunk",
+    )(*pinned(grad_output), before, apart)
+    grads = exchanged(chunks)
+
+    weight, attended, inverse, value_win, key_t = pl.pallas_call(
         forward_kernel,
         out_shape=(
             sds((pairs * BLOCK, WIDE), bf16),
             sds((OWN * HEAD, WIDE), bf16),
             sds((OWN * WIDE, HEAD), f32),
+            sds((window, HEAD), bf16),
+            sds((HEAD, window), bf16),
         ),
         in_specs=[HBM, HBM] + [VMEM] * 5,
-        out_specs=(HBM, VMEM, VMEM),
+        out_specs=(HBM,) + (VMEM,) * 4,
         scratch_shapes=[
             pltpu.SMEM(doc_start.shape, jnp.int32),
             pltpu.VMEM((SPAN, WIDE), bf16),
-            pltpu.VMEM((window, HEAD), bf16),
             pltpu.VMEM((window, HEAD), bf16),
             pltpu.VMEM((HEAD, window), bf16),
             pltpu.VMEM((REACH * BLOCK, WIDE), f32),
@@ -352,15 +373,13 @@
             tail,
             sds((SPAN, 2 * HEAD), f32),
         ),
-        in_specs=[HBM, HBM] + [VMEM] * 8,
+        in_specs=[HBM, HBM] + [VMEM] * 5,
         out_specs=(VMEM,) * 5,
         scratch_shapes=[
             pltpu.VMEM((SPAN, WIDE), bf16),
             pltpu.VMEM((pairs * BLOCK, WIDE), bf16),
             pltpu.VMEM((SPAN, WIDE), bf16),
-            pltpu.VMEM((window, HEAD), bf16),
-            pltpu.VMEM((window, HEAD), bf16),
-            pltpu.VMEM((HEAD, window), bf16),
+            pltpu.VMEM((REACH * BLOCK, WIDE), f32),
             pltpu.VMEM((pairs * BLOCK, WIDE), bf16),
             pltpu.VMEM((window, HEAD), f32),
             pltpu.VMEM((window, HEAD), f32),
@@ -371,7 +390,7 @@
         cost_estimate=cost(4 * flops),
         compiler_params=params(24),
         name="backward",
-    )(query_hbm, *pinned(weight), grads, *halo, attended, inverse)
+    )(query_hbm, *pinned(weight), grads, value_win, key_t, attended, inverse)
 
     back = exchanged(dchunks)
     received = core_swapped(dnear_far)
@@ -385,17 +404,23 @@
         name="merge",
     )(dmid, received)
     shifted = passed_along(merged, -2)
+    folded = pl.pallas_call(
+        fold_kernel,
+        out_shape=sds((SPAN, 2 * HEAD), f32),
+        in_specs=[VMEM] * 3,
+        out_specs=VMEM,
+        compiler_params=params(4),
+        name="fold",
+    )(down, received, far_back)
     grad_key, grad_value = pl.pallas_call(
         sum_kernel,
         out_shape=(sds((SPAN, HEAD), bf16),) * 2,
-        in_specs=[VMEM] * 4,
+        in_specs=[VMEM] * 2,
         out_specs=(HBM,) * 2,
-        scratch_shapes=[
-            pltpu.VMEM((SPAN, 2 * HEAD), f32), pltpu.VMEM((2, SPAN, HEAD), bf16), dma((2,))
-        ],
+        scratch_shapes=[pltpu.VMEM((2, SPAN, HEAD), bf16), dma((2,))],
         compiler_params=params(4),
         name="sum",
-    )(down, received, shifted, far_back)
+    )(folded, shifted)
     grad_query = pl.pallas_call(
         place_kernel,
         out_shape=sds((share, parts * WIDE), bf16),

time: 71 us -> 70.1 us (0.987)
  the two profiles are of different devices: /device:TPU:205 before, /device:TPU:198 now
where the time goes in v2:
time: 70.1 us; the launch traced here: 69.3 us
  starting transfers between devices  32.5 us (46%)
  waiting for transfers between devices  18.4 us (26%)
  Pallas kernels  16 us (23%)
  local copies, waits for them, and re-layouts  1.74 us (2%)
  between operations  0.76 us (1%)
    ppermute x5, waiting for transfers between devices, passed_along(): return lax.ppermute(value, 'ctx', pairs)  15.7 us
    ppermute x5, starting transfers between devices, passed_along(): return lax.ppermute(value, 'ctx', pairs)  13.4 us
    all_to_all x2, starting transfers between devices, exchanged(): lax.all_to_all(value, ('ctx', 'kvh'), split_axis=0, concat_axis=0, axis_i...  13.3 us
    pallas_call x1, Pallas kernels, body(): pl.pallas_call(backward_kernel, out_shape=(chunked, sds((SPAN + TAIL, 2 *...  6.58 us
    ppermute x2, starting transfers between devices, core_swapped(): lax.ppermute(value, 'ctx', [(i, i ^ 1) for i in range(lax.axis_size('ctx'...  5.77 us
    pallas_call x1, Pallas kernels, body(): pl.pallas_call(forward_kernel, out_shape=(sds((pairs * BLOCK, WIDE), bf16...  5.01 us
    ppermute x2, waiting for transfers between devices, core_swapped(): lax.ppermute(value, 'ctx', [(i, i ^ 1) for i in range(lax.axis_size('ctx'...  2.63 us
    pallas_call x1, Pallas kernels, body(): pl.pallas_call(chunk_kernel, out_shape=chunked, in_specs=[HBM, VMEM, VMEM...  1.78 us
  transfers between devices with their start and end apart: 9, of which 5 were waited for; matrix products, arithmetic and copies ran while one was open for 0% of the time, Pallas kernels for 8%

profile of v2, /device:TPU:198, one launch (start us, length us, event | category | flops | bytes accessed | tf_op | source)
XLA Modules:
  0.0 69.3 jit_solution(7430391406491572537)
XLA Ops:
  0.6 1.0 %pair.1 = (bf16[384,256]{1,0:T(8,128)(2,1)S(1)}, bf16[256,256]{1,0:T(8,128)(2,1)S(1)}) custom-call(bf16[384,128]{1,0:T(8,128)(2,1)} %key_hbm.1, bf16[384,128]{1,0:T(8,128)(2,1)} %value_hbm.1), custom_call_target="tpu_custom_call" | custom-call | tf_op jit(solution)/shard_map/pair/pallas_call | solution.py:316
  1.6 5.4 %collective-permute-start.1 = (bf16[384,256]{1,0:T(8,128)(2,1)S(1)}, bf16[384,256]{1,0:T(8,128)(2,1)S(1)}, u32[]{:S(2)}, u32[]{:S(2)}) collective-permute-start(bf16[384,256]{1,0:T(8,128)(2,1)S(1)} %get-tuple-element.17.own), channel_id=1, source_target_pairs={{0,16},{8,24},{16,32},{24,40},{32,48},{40,56},{48,64},{56,72},{64,... | collective-permute-start | bytes 589832 | tf_op jit(solution)/shard_map/ppermute | solution.py:274
  7.1 1.3 %collective-permute-start.3 = (bf16[256,256]{1,0:T(8,128)(2,1)S(1)}, bf16[256,256]{1,0:T(8,128)(2,1)S(1)}, u32[]{:S(2)}, u32[]{:S(2)}) collective-permute-start(bf16[256,256]{1,0:T(8,128)(2,1)S(1)} %get-tuple-element.18), channel_id=1, source_target_pairs={{8,32},{24,48},{40,64},{56,80},{72,96},{88,112},{104,128},{120,144... | collective-permute-start | bytes 393224 | tf_op jit(solution)/shard_map/ppermute | solution.py:274
  8.4 6.5 %collective-permute-done.3.apart = bf16[256,256]{1,0:T(8,128)(2,1)S(1)} collective-permute-done((bf16[256,256]{1,0:T(8,128)(2,1)S(1)}, bf16[256,256]{1,0:T(8,128)(2,1)S(1)}, u32[]{:S(2)}, u32[]{:S(2)}) %collective-permute-start.3) | collective-permute-done | bytes 131104 | tf_op jit(solution)/shard_map/ppermute | solution.py:274
  14.8 0.0 collective-permute-done.1.before
  14.8 1.8 %chunk.1 = bf16[8,48,512]{2,1,0:T(8,128)(2,1)} custom-call(bf16[48,4096]{1,0:T(8,128)(2,1)} %grad_hbm.1, bf16[384,256]{1,0:T(8,128)(2,1)S(1)} %collective-permute-done.1.before, bf16[256,256]{1,0:T(8,128)(2,1)S(1)} %collective-permute-done.3.apart), custom_call_target="tpu_custom_call" | custom-call | tf_op jit(solution)/shard_map/chunk/pallas_call | solution.py:330
  16.6 7.1 %all-to-all-start = ((bf16[8,48,512]{2,1,0:T(8,128)(2,1)}), bf16[8,48,512]{2,1,0:T(8,128)(2,1)S(1)}, u32[]{:S(2)}, u32[]{:S(2)}) async-start(bf16[8,48,512]{2,1,0:T(8,128)(2,1)} %chunk.1), calls=%async_computation | async-start | bytes 786432 | tf_op jit(solution)/shard_map/all_to_all | solution.py:311
  23.7 2.3 %collective-permute-start = (bf16[384,256]{1,0:T(8,128)(2,1)S(1)}, bf16[384,256]{1,0:T(8,128)(2,1)S(1)}, u32[]{:S(2)}, u32[]{:S(2)}) collective-permute-start(bf16[384,256]{1,0:T(8,128)(2,1)S(1)} %get-tuple-element.17.own), channel_id=1, source_target_pairs={{0,8},{16,24},{32,40},{48,56},{64,72},{80,88},{96,104},{112,120},{... | collective-permute-start | bytes 589832 | tf_op jit(solution)/shard_map/ppermute | solution.py:274
  26.1 1.9 %collective-permute-start.2 = (bf16[384,256]{1,0:T(8,128)(2,1)S(1)}, bf16[384,256]{1,0:T(8,128)(2,1)S(1)}, u32[]{:S(2)}, u32[]{:S(2)}) collective-permute-start(bf16[384,256]{1,0:T(8,128)(2,1)S(1)} %collective-permute-done.1.before), channel_id=1, source_target_pairs={{0,8},{8,0},{16,24},{24,16},{32,40},{40,32},{48,56},{56,48},{64,72... | collective-permute-start | bytes 589832 | tf_op jit(solution)/shard_map/ppermute | solution.py:278
  28.0 1.4 %collective-permute-done.2.across = bf16[384,256]{1,0:T(8,128)(2,1)S(1)} collective-permute-done((bf16[384,256]{1,0:T(8,128)(2,1)S(1)}, bf16[384,256]{1,0:T(8,128)(2,1)S(1)}, u32[]{:S(2)}, u32[]{:S(2)}) %collective-permute-start.2) | collective-permute-done | bytes 196640 | tf_op jit(solution)/shard_map/ppermute | solution.py:278
  29.4 5.0 %forward.1 = (bf16[3456,512]{1,0:T(8,128)(2,1)S(1)}, bf16[384,512]{1,0:T(8,128)(2,1)S(1)}, f32[1536,128]{1,0:T(8,128)S(1)}, bf16[1408,128]{1,0:T(8,128)(2,1)S(1)}, bf16[128,1408]{1,0:T(8,128)(2,1)S(1)}) custom-call(s32[3]{0:T(128)} %start_hbm.1, bf16[384,512]{1,0:T(8,128)(2,1)} %query_hbm.3, bf16[384,256]{1,0:T(8,128)(2,1)S(1)} %get-tuple-element.17.own, ...), custom_call_target="tpu_custom_call" | custom-call | flops 905969664 | bytes 8388608 | tf_op jit(solution)/shard_map/forward/pallas_call | solution.py:341
  34.4 1.7 %copy-done = bf16[3456,512]{1,0:T(8,128)(2,1)} copy-done((bf16[3456,512]{1,0:T(8,128)(2,1)}, bf16[3456,512]{1,0:T(8,128)(2,1)S(1)}, u32[]{:S(2)}) %copy-start) | copy-done | bytes 3538968
  36.2 0.0 all-to-all-done.chunks
  36.2 6.6 %backward.1 = (bf16[8,48,512]{2,1,0:T(8,128)(2,1)}, bf16[640,256]{1,0:T(8,128)(2,1)S(1)}, bf16[384,256]{1,0:T(8,128)(2,1)S(1)}, bf16[256,256]{1,0:T(8,128)(2,1)S(1)}, f32[384,256]{1,0:T(8,128)S(1)}) custom-call(bf16[384,512]{1,0:T(8,128)(2,1)} %query_hbm.3, bf16[3456,512]{1,0:T(8,128)(2,1)} %copy-done, bf16[8,48,512]{2,1,0:T(8,128)(2,1)S(1)} %all-to-all-done.chunks, ...), custom_call_target="tpu_custom_call" | custom-call | flops 1811939328 | bytes 8388608 | tf_op jit(solution)/shard_map/backward/pallas_call | solution.py:367
  42.8 6.2 %all-to-all-start.1 = ((bf16[8,48,512]{2,1,0:T(8,128)(2,1)}), bf16[8,48,512]{2,1,0:T(8,128)(2,1)S(1)}, u32[]{:S(2)}, u32[]{:S(2)}) async-start(bf16[8,48,512]{2,1,0:T(8,128)(2,1)} %get-tuple-element.24), calls=%async_computation.1 | async-start | bytes 786432 | tf_op jit(solution)/shard_map/all_to_all | solution.py:311
  49.0 3.9 %collective-permute-start.4 = (bf16[640,256]{1,0:T(8,128)(2,1)S(1)}, bf16[640,256]{1,0:T(8,128)(2,1)S(1)}, u32[]{:S(2)}, u32[]{:S(2)}) collective-permute-start(bf16[640,256]{1,0:T(8,128)(2,1)S(1)} %get-tuple-element.26), channel_id=1, source_target_pairs={{0,8},{8,0},{16,24},{24,16},{32,40},{40,32},{48,56},{56,48},{64,72... | collective-permute-start | bytes 983048 | tf_op jit(solution)/shard_map/ppermute | solution.py:278
  52.8 1.2 %collective-permute-done.4.received = bf16[640,256]{1,0:T(8,128)(2,1)S(1)} collective-permute-done((bf16[640,256]{1,0:T(8,128)(2,1)S(1)}, bf16[640,256]{1,0:T(8,128)(2,1)S(1)}, u32[]{:S(2)}, u32[]{:S(2)}) %collective-permute-start.4) | collective-permute-done | bytes 327712 | tf_op jit(solution)/shard_map/ppermute | solution.py:278
  54.1 1.9 %collective-permute-start.6 = (bf16[384,256]{1,0:T(8,128)(2,1)S(1)}, bf16[384,256]{1,0:T(8,128)(2,1)S(1)}, u32[]{:S(2)}, u32[]{:S(2)}) collective-permute-start(bf16[384,256]{1,0:T(8,128)(2,1)S(1)} %merge.1), channel_id=1, source_target_pairs={{16,0},{24,8},{32,16},{40,24},{48,32},{56,40},{64,48},{72,56},{80,... | collective-permute-start | bytes 589832 | tf_op jit(solution)/shard_map/ppermute | solution.py:274
  56.0 2.5 %collective-permute-start.5 = (bf16[256,256]{1,0:T(8,128)(2,1)S(1)}, bf16[256,256]{1,0:T(8,128)(2,1)S(1)}, u32[]{:S(2)}, u32[]{:S(2)}) collective-permute-start(bf16[256,256]{1,0:T(8,128)(2,1)S(1)} %get-tuple-element.27), channel_id=1, source_target_pairs={{32,8},{48,24},{64,40},{80,56},{96,72},{112,88},{128,104},{144,120... | collective-permute-start | bytes 393224 | tf_op jit(solution)/shard_map/ppermute | solution.py:274
  58.5 3.9 %collective-permute-done.5.apart = bf16[256,256]{1,0:T(8,128)(2,1)S(1)} collective-permute-done((bf16[256,256]{1,0:T(8,128)(2,1)S(1)}, bf16[256,256]{1,0:T(8,128)(2,1)S(1)}, u32[]{:S(2)}, u32[]{:S(2)}) %collective-permute-start.5) | collective-permute-done | bytes 131104 | tf_op jit(solution)/shard_map/ppermute | solution.py:274
  62.4 5.3 %collective-permute-done.6.shifted = bf16[384,256]{1,0:T(8,128)(2,1)S(1)} collective-permute-done((bf16[384,256]{1,0:T(8,128)(2,1)S(1)}, bf16[384,256]{1,0:T(8,128)(2,1)S(1)}, u32[]{:S(2)}, u32[]{:S(2)}) %collective-permute-start.6) | collective-permute-done | bytes 196640 | tf_op jit(solution)/shard_map/ppermute | solution.py:274
  67.8 0.7 %sum.1 = (bf16[384,128]{1,0:T(8,128)(2,1)}, bf16[384,128]{1,0:T(8,128)(2,1)}) custom-call(f32[384,256]{1,0:T(8,128)S(1)} %fold.1.folded, bf16[384,256]{1,0:T(8,128)(2,1)S(1)} %collective-permute-done.6.shifted), custom_call_target="tpu_custom_call" | custom-call | tf_op jit(solution)/shard_map/sum/pallas_call | solution.py:415
  68.5 0.0 all-to-all-done.1.chunks
  68.5 0.8 %place.1 = bf16[48,4096]{1,0:T(8,128)(2,1)} custom-call(bf16[8,48,512]{2,1,0:T(8,128)(2,1)S(1)} %all-to-all-done.1.chunks), custom_call_target="tpu_custom_call" | custom-call | tf_op jit(solution)/shard_map/place/pallas_call | solution.py:424
  (4 shorter events, 0.1 us)
Async XLA Ops:
  1.6 13.2 %collective-permute-start.1 = (bf16[384,256]{1,0:T(8,128)(2,1)S(1)}, bf16[384,256]{1,0:T(8,128)(2,1)S(1)}, u32[]{:S(2)}, u32[]{:S(2)}) collective-permute-start(bf16[384,256]{1,0:T(8,128)(2,1)S(1)} %get-tuple-element.17.own), channel_id=1, source_target_pairs={{0,16},{8,24},{16,32},{24,40},{32,48},{40,56},{48,64},{56,72},{64,... | collective-permute-start | bytes 589832 | tf_op jit(solution)/shard_map/ppermute | solution.py:274
  7.1 7.8 %collective-permute-start.3 = (bf16[256,256]{1,0:T(8,128)(2,1)S(1)}, bf16[256,256]{1,0:T(8,128)(2,1)S(1)}, u32[]{:S(2)}, u32[]{:S(2)}) collective-permute-start(bf16[256,256]{1,0:T(8,128)(2,1)S(1)} %get-tuple-element.18), channel_id=1, source_target_pairs={{8,32},{24,48},{40,64},{56,80},{72,96},{88,112},{104,128},{120,144... | collective-permute-start | bytes 393224 | tf_op jit(solution)/shard_map/ppermute | solution.py:274
  16.6 19.5 %all-to-all-start = ((bf16[8,48,512]{2,1,0:T(8,128)(2,1)}), bf16[8,48,512]{2,1,0:T(8,128)(2,1)S(1)}, u32[]{:S(2)}, u32[]{:S(2)}) async-start(bf16[8,48,512]{2,1,0:T(8,128)(2,1)} %chunk.1), calls=%async_computation | async-start | bytes 786432 | tf_op jit(solution)/shard_map/all_to_all | solution.py:311
  23.7 4.2 %collective-permute-start = (bf16[384,256]{1,0:T(8,128)(2,1)S(1)}, bf16[384,256]{1,0:T(8,128)(2,1)S(1)}, u32[]{:S(2)}, u32[]{:S(2)}) collective-permute-start(bf16[384,256]{1,0:T(8,128)(2,1)S(1)} %get-tuple-element.17.own), channel_id=1, source_target_pairs={{0,8},{16,24},{32,40},{48,56},{64,72},{80,88},{96,104},{112,120},{... | collective-permute-start | bytes 589832 | tf_op jit(solution)/shard_map/ppermute | solution.py:274
  26.1 3.3 %collective-permute-start.2 = (bf16[384,256]{1,0:T(8,128)(2,1)S(1)}, bf16[384,256]{1,0:T(8,128)(2,1)S(1)}, u32[]{:S(2)}, u32[]{:S(2)}) collective-permute-start(bf16[384,256]{1,0:T(8,128)(2,1)S(1)} %collective-permute-done.1.before), channel_id=1, source_target_pairs={{0,8},{8,0},{16,24},{24,16},{32,40},{40,32},{48,56},{56,48},{64,72... | collective-permute-start | bytes 589832 | tf_op jit(solution)/shard_map/ppermute | solution.py:278
  34.4 1.7 %copy-start = (bf16[3456,512]{1,0:T(8,128)(2,1)}, bf16[3456,512]{1,0:T(8,128)(2,1)S(1)}, u32[]{:S(2)}) copy-start(bf16[3456,512]{1,0:T(8,128)(2,1)S(1)} %get-tuple-element.19.weight_hbm) | copy-start | bytes 10616836
  42.8 25.8 %all-to-all-start.1 = ((bf16[8,48,512]{2,1,0:T(8,128)(2,1)}), bf16[8,48,512]{2,1,0:T(8,128)(2,1)S(1)}, u32[]{:S(2)}, u32[]{:S(2)}) async-start(bf16[8,48,512]{2,1,0:T(8,128)(2,1)} %get-tuple-element.24), calls=%async_computation.1 | async-start | bytes 786432 | tf_op jit(solution)/shard_map/all_to_all | solution.py:311
  49.0 5.1 %collective-permute-start.4 = (bf16[640,256]{1,0:T(8,128)(2,1)S(1)}, bf16[640,256]{1,0:T(8,128)(2,1)S(1)}, u32[]{:S(2)}, u32[]{:S(2)}) collective-permute-start(bf16[640,256]{1,0:T(8,128)(2,1)S(1)} %get-tuple-element.26), channel_id=1, source_target_pairs={{0,8},{8,0},{16,24},{24,16},{32,40},{40,32},{48,56},{56,48},{64,72... | collective-permute-start | bytes 983048 | tf_op jit(solution)/shard_map/ppermute | solution.py:278
  54.1 13.7 %collective-permute-start.6 = (bf16[384,256]{1,0:T(8,128)(2,1)S(1)}, bf16[384,256]{1,0:T(8,128)(2,1)S(1)}, u32[]{:S(2)}, u32[]{:S(2)}) collective-permute-start(bf16[384,256]{1,0:T(8,128)(2,1)S(1)} %merge.1), channel_id=1, source_target_pairs={{16,0},{24,8},{32,16},{40,24},{48,32},{56,40},{64,48},{72,56},{80,... | collective-permute-start | bytes 589832 | tf_op jit(solution)/shard_map/ppermute | solution.py:274
  56.0 6.4 %collective-permute-start.5 = (bf16[256,256]{1,0:T(8,128)(2,1)S(1)}, bf16[256,256]{1,0:T(8,128)(2,1)S(1)}, u32[]{:S(2)}, u32[]{:S(2)}) collective-permute-start(bf16[256,256]{1,0:T(8,128)(2,1)S(1)} %get-tuple-element.27), channel_id=1, source_target_pairs={{32,8},{48,24},{64,40},{80,56},{96,72},{112,88},{128,104},{144,120... | collective-permute-start | bytes 393224 | tf_op jit(solution)/shard_map/ppermute | solution.py:274

commit v3 on v2

--- a/solution.py
+++ b/solution.py
@@ -17,6 +17,7 @@
 SPAN = OWN * BLOCK
 TAIL = 2 * BLOCK
 INV_ROOT = HEAD ** (-0.5)
+TO_EXP2 = INV_ROOT * math.log2(math.e)
 MIB = 2**20
 
 NT = (((1,), (1,)), ((), ()))
@@ -61,9 +62,11 @@
     return pl.ds(pl.multiple_of(peer_at(position, parts) * WIDE, WIDE), WIDE)
 
 
-def pair_kernel(key_hbm, value_hbm, pair, tail, sems):
+def prepare_kernel(grad_hbm, key_hbm, value_hbm, chunks, pair, tail, sems):
+    parts = chunks.shape[0]
     last = slice(SPAN - TAIL, SPAN)
-    moves = [
+    moves = [(grad_hbm.at[:, peer_cols(p, parts)], chunks.at[p]) for p in range(parts)]
+    moves += [
         (key_hbm, pair.at[:, :HEAD]),
         (value_hbm, pair.at[:, HEAD:]),
         (key_hbm.at[last, :], tail.at[:, :HEAD]),
@@ -72,57 +75,77 @@
     finish(started(moves, sems))
 
 
-def chunk_kernel(grad_hbm, before, apart, chunks, sems):
-    parts = chunks.shape[0]
-    finish(
-        started([(grad_hbm.at[:, peer_cols(p, parts)], chunks.at[p]) for p in range(parts)], sems)
-    )
-
-
-def put_window(part, win, own, beside, before, across, apart):
+def halo_kernel(own, beside, apart, keys, values):
+    odd = on_odd_core()
+    for part, win in enumerate((keys, values)):
+        cols = block(part)
+        win[TAIL + 2 * SPAN :, :] = own[:, cols]
+
+        @pl.when(odd)
+        def _():
+            win[0:TAIL, :] = jnp.zeros((TAIL, HEAD), win.dtype)
+            win[TAIL + SPAN : TAIL + 2 * SPAN, :] = beside[:, cols]
+
+        @pl.when(jnp.logical_not(odd))
+        def _():
+            win[0:TAIL, :] = apart[:, cols]
+            win[TAIL + SPAN : TAIL + 2 * SPAN, :] = jnp.zeros((SPAN, HEAD), win.dtype)
+
+        win[TAIL : TAIL + SPAN, :] = jnp.zeros((SPAN, HEAD), win.dtype)
+
+
+def complete(win, part, partial, before, across):
     cols = block(part)
-    win[TAIL + 2 * SPAN :, :] = own[:, cols]
+    win[...] = partial[...]
     win[TAIL : TAIL + SPAN, :] = before[:, cols]
     odd = on_odd_core()
 
     @pl.when(odd)
     def _():
-        win[TAIL + SPAN : TAIL + 2 * SPAN, :] = beside[:, cols]
         win[0:TAIL, :] = across[SPAN - TAIL :, cols]
 
     @pl.when(jnp.logical_not(odd))
     def _():
         win[TAIL + SPAN : TAIL + 2 * SPAN, :] = across[:, cols]
-        win[0:TAIL, :] = apart[:, cols]
-
-
-def weight_copy(source, target, sems, i):
-    mine = block(i * REACH, REACH)
-    return pltpu.make_async_copy(source.at[mine, :], target.at[mine, :], sems.at[i])
+
+
+def causal_mask():
+    key_at = lax.broadcasted_iota(jnp.int32, (BLOCK, WIDE), 0)
+    query_at = lax.broadcasted_iota(jnp.int32, (BLOCK, WIDE), 1) & (BLOCK - 1)
+    return key_at <= query_at
+
+
+def first_key():
+    return lax.axis_index("ctx") * SPAN - (REACH - 1) * BLOCK
+
+
+def row8(i):
+    return slice(8 * i, 8 * i + 8)
 
 
 def forward_kernel(
-    start_hbm, query_hbm, own, beside, before, across, apart,
-    weight_hbm, attended_ref, inverse_ref, value_win, key_t,
-    start_ref, query_ref, key_win, value_t, held, weight_ref, sems, weight_sems
+    start_hbm, query_hbm, keys, values, before, across,
+    queries, queries_t, key_win, value_win, key_t, attended_ref, norm_ref, starts,
+    start_ref, query_ref, value_t, held, weights, sems
 ):
     arriving = started([(query_hbm, query_ref), (start_hbm, start_ref)], sems)
-    put_window(0, key_win, own, beside, before, across, apart)
-    put_window(1, value_win, own, beside, before, across, apart)
+    complete(key_win, 0, keys, before, across)
+    complete(value_win, 1, values, before, across)
     value_t[...] = value_win[...].T
     key_t[...] = key_win[...].T
-    first = lax.axis_index("ctx") * SPAN - (REACH - 1) * BLOCK
-    to_exp2 = INV_ROOT * math.log2(math.e)
-    key_at = lax.broadcasted_iota(jnp.int32, (BLOCK, WIDE), 0)
-    query_at = lax.broadcasted_iota(jnp.int32, (BLOCK, WIDE), 1) & (BLOCK - 1)
-    causal = key_at <= query_at
+    causal = causal_mask()
+    first = first_key()
     finish(arriving)
     for i in range(OWN):
-        queries_t = heads_stacked(query_ref[block(i), :]).T
+        stacked = heads_stacked(query_ref[block(i), :])
+        queries[block(i * GROUP, GROUP), :] = stacked
+        turned = stacked.T
+        queries_t[block(i), :] = turned
         start = start_ref[i]
+        starts[row8(i), :] = jnp.full((8, WIDE), start, jnp.int32)
         best = jnp.full((8, WIDE), -jnp.inf, jnp.float32)
         for j in range(REACH):
-            score = dot(key_win[block(i + j), :], queries_t, NN)
+            score = dot(key_win[block(i + j), :], turned, NN)
             allowed = causal if j == REACH - 1 else first + (i + j) * BLOCK >= start
             score = jnp.where(allowed, score, -jnp.inf)
             held[block(j), :] = score
@@ -130,73 +153,60 @@
         best = jnp.max(best, axis=0, keepdims=True)
         total = jnp.zeros((8, WIDE), jnp.float32)
         for j in range(REACH):
-            part = jnp.exp2((held[block(j), :] - best) * to_exp2)
+            part = jnp.exp2((held[block(j), :] - best) * TO_EXP2)
             total = total + jnp.sum(part.reshape(BLOCK // 8, 8, WIDE), axis=0)
-            weight_ref[block(i * REACH + j), :] = part.astype(jnp.bfloat16)
-        weight_copy(weight_ref, weight_hbm, weight_sems, i).start()
-        inverse = 1.0 / jnp.sum(total, axis=0, keepdims=True)
+            weights[block(i * REACH + j), :] = part.astype(jnp.bfloat16)
+        total = jnp.sum(total, axis=0, keepdims=True)
+        norm_ref[row8(i), :] = jnp.broadcast_to(best * TO_EXP2 + jnp.log2(total), (8, WIDE))
         attended_ref[block(i), :] = (
-            dot(value_t[:, block(i, REACH)], weight_ref[block(i * REACH, REACH), :], NN) * inverse
+            dot(value_t[:, block(i, REACH)], weights[block(i * REACH, REACH), :], NN)
+            * (1.0 / total)
         ).astype(jnp.bfloat16)
-        for h in range(GROUP):
-            inverse_ref[block(i * GROUP + h), :] = jnp.broadcast_to(
-                inverse[:, block(h)], (BLOCK, BLOCK)
-            ).T
-    for i in range(OWN):
-        weight_copy(weight_ref, weight_hbm, weight_sems, i).wait()
 
 
 def backward_kernel(
-    query_hbm, weight_hbm, chunks, value_win, key_t, attended_ref, inverse_ref,
+    chunks, queries, queries_t, key_win, value_win, key_t, attended_ref, norm_ref, starts,
     dchunks, dnear_far, dmid, dfar, down,
-    query_ref, weight_ref, grad_ref, wide, held, dkey, dvalue, dquery, sems, weight_sems
+    grad_ref, weights, held, dkey, dvalue, dquery
 ):
     parts, share = chunks.shape[0], chunks.shape[1]
 
     def share_rows(p):
         return pl.ds(pl.multiple_of(peer_at(p, parts) * share, share), share)
 
-    weights_in = [weight_copy(weight_hbm, weight_ref, weight_sems, i) for i in range(OWN)]
-    for copy in weights_in:
-        copy.start()
-    query_in = started([(query_hbm, query_ref)], sems)
     for p in range(parts):
         grad_ref[share_rows(p), :] = chunks[p]
+    causal = causal_mask()
+    first = first_key()
     on_diagonal = lax.broadcasted_iota(jnp.int32, (BLOCK, BLOCK), 0) == lax.broadcasted_iota(
         jnp.int32, (BLOCK, BLOCK), 1
     )
     for i in range(OWN):
-        grads = (
-            heads_stacked(grad_ref[block(i), :]).astype(jnp.float32)
-            * inverse_ref[block(i * GROUP, GROUP), :]
-        ).astype(jnp.bfloat16)
+        grads = heads_stacked(grad_ref[block(i), :])
         grads_t = grads.T
         deltas = []
         for h in range(GROUP):
             cross = dot(grads[block(h), :], attended_ref[block(i), block(h)], NN)
             deltas.append(jnp.sum(jnp.where(on_diagonal, cross, 0.0), axis=0, keepdims=True))
         delta = jnp.concatenate(deltas, axis=1)
-
-        def slope(j):
-            return dot(value_win[block(i + j), :], grads_t, NN) - delta
-
-        if i == 0:
-            for j in range(REACH):
-                wide[block(j), :] = slope(j)
-            finish(query_in)
-        weights_in[i].wait()
+        norm = norm_ref[8 * i : 8 * i + 1, :]
+        start = starts[8 * i : 8 * i + 1, :]
         for j in range(REACH):
-            weight = weight_ref[block(i * REACH + j), :].astype(jnp.float32)
-            held[block(i * REACH + j), :] = (
-                weight * (wide[block(j), :] if i == 0 else slope(j))
-            ).astype(jnp.bfloat16)
-        queries = heads_stacked(query_ref[block(i), :])
+            score = dot(key_win[block(i + j), :], queries_t[block(i), :], NN)
+            if j == REACH - 1:
+                weight = jnp.where(causal, jnp.exp2(score * TO_EXP2 - norm), 0.0)
+            else:
+                allowed = first + (i + j) * BLOCK >= start
+                weight = jnp.exp2(score * TO_EXP2 - jnp.where(allowed, norm, jnp.inf))
+            dweight = dot(value_win[block(i + j), :], grads_t, NN)
+            weights[block(i * REACH + j), :] = weight.astype(jnp.bfloat16)
+            held[block(i * REACH + j), :] = (weight * (dweight - delta)).astype(jnp.bfloat16)
         mine = block(i * REACH, REACH)
         turned = dot(key_t[:, block(i, REACH)], held[mine, :], NN) * INV_ROOT
         for h in range(GROUP):
             dquery[block(i), block(h)] = turned[:, block(h)].T.astype(jnp.bfloat16)
-        value_part = dot(weight_ref[mine, :], grads, NN)
-        key_part = dot(held[mine, :], queries, NN)
+        value_part = dot(weights[mine, :], grads, NN)
+        key_part = dot(held[mine, :], queries[block(i * GROUP, GROUP), :], NN)
         fresh = 0 if i == 0 else REACH - 1
         if fresh:
             seen = slice(0, fresh * BLOCK)
@@ -313,56 +323,56 @@
         )
 
     start_hbm, query_hbm = pinned(doc_start, query_states)
-    own, last = pl.pallas_call(
-        pair_kernel,
-        out_shape=(pair, tail),
-        in_specs=[HBM] * 2,
-        out_specs=(VMEM,) * 2,
-        scratch_shapes=[dma((4,))],
-        compiler_params=params(4),
-        name="pair",
-    )(*pinned(key_states, value_states))
+    chunks, own, last = pl.pallas_call(
+        prepare_kernel,
+        out_shape=(chunked, pair, tail),
+        in_specs=[HBM] * 3,
+        out_specs=(VMEM,) * 3,
+        scratch_shapes=[dma((parts + 4,))],
+        compiler_params=params(4),
+        name="prepare",
+    )(*pinned(grad_output, key_states, value_states))
+    grads = exchanged(chunks)
     before = passed_along(own, 2)
     apart = passed_along(last, 3, (1,))
     beside = passed_along(own, 1, (0,))
     across = core_swapped(before)
-    halo = (own, beside, before, across, apart)
-    chunks = pl.pallas_call(
-        chunk_kernel,
-        out_shape=chunked,
-        in_specs=[HBM, VMEM, VMEM],
-        out_specs=VMEM,
-        scratch_shapes=[dma((parts,))],
-        compiler_params=params(4),
-        name="chunk",
-    )(*pinned(grad_output), before, apart)
-    grads = exchanged(chunks)
-
-    weight, attended, inverse, value_win, key_t = pl.pallas_call(
+    keys, values = pl.pallas_call(
+        halo_kernel,
+        out_shape=(sds((window, HEAD), bf16),) * 2,
+        in_specs=[VMEM] * 3,
+        out_specs=(VMEM,) * 2,
+        cost_estimate=cost(flops),
+        compiler_params=params(4),
+        name="halo",
+    )(own, beside, apart)
+
+    kept = pl.pallas_call(
         forward_kernel,
         out_shape=(
-            sds((pairs * BLOCK, WIDE), bf16),
+            sds((OWN * WIDE, HEAD), bf16),
             sds((OWN * HEAD, WIDE), bf16),
-            sds((OWN * WIDE, HEAD), f32),
+            sds((window, HEAD), bf16),
             sds((window, HEAD), bf16),
             sds((HEAD, window), bf16),
+            sds((OWN * HEAD, WIDE), bf16),
+            sds((8 * OWN, WIDE), f32),
+            sds((8 * OWN, WIDE), jnp.int32),
         ),
-        in_specs=[HBM, HBM] + [VMEM] * 5,
-        out_specs=(HBM,) + (VMEM,) * 4,
+        in_specs=[HBM, HBM] + [VMEM] * 4,
+        out_specs=(VMEM,) * 8,
         scratch_shapes=[
             pltpu.SMEM(doc_start.shape, jnp.int32),
             pltpu.VMEM((SPAN, WIDE), bf16),
-            pltpu.VMEM((window, HEAD), bf16),
             pltpu.VMEM((HEAD, window), bf16),
             pltpu.VMEM((REACH * BLOCK, WIDE), f32),
             pltpu.VMEM((pairs * BLOCK, WIDE), bf16),
             dma((2,)),
-            dma((OWN,)),
         ],
         cost_estimate=cost(2 * flops, pairs * BLOCK * WIDE),
         compiler_params=params(16),
         name="forward",
-    )(start_hbm, query_hbm, *halo)
+    )(start_hbm, query_hbm, keys, values, before, across)
 
     dchunks, dnear_far, dmid, dfar, down = pl.pallas_call(
         backward_kernel,
@@ -373,24 +383,20 @@
             tail,
             sds((SPAN, 2 * HEAD), f32),
         ),
-        in_specs=[HBM, HBM] + [VMEM] * 5,
+        in_specs=[VMEM] * 9,
         out_specs=(VMEM,) * 5,
         scratch_shapes=[
             pltpu.VMEM((SPAN, WIDE), bf16),
             pltpu.VMEM((pairs * BLOCK, WIDE), bf16),
-            pltpu.VMEM((SPAN, WIDE), bf16),
-            pltpu.VMEM((REACH * BLOCK, WIDE), f32),
             pltpu.VMEM((pairs * BLOCK, WIDE), bf16),
             pltpu.VMEM((window, HEAD), f32),
             pltpu.VMEM((window, HEAD), f32),
             pltpu.VMEM((SPAN, WIDE), bf16),
-            dma((1,)),
-            dma((OWN,)),
         ],
-        cost_estimate=cost(4 * flops),
+        cost_estimate=cost(5 * flops, pairs * BLOCK * WIDE),
         compiler_params=params(24),
         name="backward",
-    )(query_hbm, *pinned(weight), grads, value_win, key_t, attended, inverse)
+    )(grads, *kept)
 
     back = exchanged(dchunks)
     received = core_swapped(dnear_far)
@@ -409,6 +415,7 @@
         out_shape=sds((SPAN, 2 * HEAD), f32),
         in_specs=[VMEM] * 3,
         out_specs=VMEM,
+        cost_estimate=cost(flops),
         compiler_params=params(4),
         name="fold",
     )(down, received, far_back)

time: 70.1 us -> 69.1 us (0.986)
  the two profiles are of different devices: /device:TPU:198 before, /device:TPU:205 now
where the time goes in v3:
time: 69.1 us; the launch traced here: 68.6 us
  starting transfers between devices  34.8 us (50%)
  waiting for transfers between devices  18.1 us (26%)
  Pallas kernels  13.1 us (19%)
  local copies, waits for them, and re-layouts  1.71 us (2%)
  between operations  0.77 us (1%)
    ppermute x5, waiting for transfers between devices, passed_along(): return lax.ppermute(value, 'ctx', pairs)  16.5 us
    ppermute x5, starting transfers between devices, passed_along(): return lax.ppermute(value, 'ctx', pairs)  15.7 us
    all_to_all x2, starting transfers between devices, exchanged(): lax.all_to_all(value, ('ctx', 'kvh'), split_axis=0, concat_axis=0, axis_i...  14.2 us
    pallas_call x1, Pallas kernels, body(): pl.pallas_call(backward_kernel, out_shape=(chunked, sds((SPAN + TAIL, 2 *...  5.18 us
    ppermute x2, starting transfers between devices, core_swapped(): lax.ppermute(value, 'ctx', [(i, i ^ 1) for i in range(lax.axis_size('ctx'...  4.94 us
    pallas_call x1, Pallas kernels, body(): pl.pallas_call(forward_kernel, out_shape=(sds((OWN * WIDE, HEAD), bf16),...  4.19 us
    pallas_call x1, Pallas kernels, body(): pl.pallas_call(prepare_kernel, out_shape=(chunked, pair, tail), in_specs=...  2.03 us
    unnamed x4, local copies, waits for them, and re-layouts  1.71 us
  transfers between devices with their start and end apart: 9, of which 4 were waited for; matrix products, arithmetic and copies ran while one was open for 0% of the time, Pallas kernels for 7%

profile of v3, /device:TPU:205, one launch (start us, length us, event | category | flops | bytes accessed | tf_op | source)
XLA Modules:
  0.0 68.6 jit_solution(3904969527923261812)
XLA Ops:
  0.6 2.0 %prepare.1 = (bf16[8,48,512]{2,1,0:T(8,128)(2,1)}, bf16[384,256]{1,0:T(8,128)(2,1)S(1)}, bf16[256,256]{1,0:T(8,128)(2,1)S(1)}) custom-call(bf16[48,4096]{1,0:T(8,128)(2,1)} %grad_hbm.1, bf16[384,128]{1,0:T(8,128)(2,1)} %key_hbm.1, bf16[384,128]{1,0:T(8,128)(2,1)} %value_hbm.1), custom_call_target="tpu_custom_call" | custom-call | tf_op jit(solution)/shard_map/prepare/pallas_call | solution.py:326
  2.7 7.9 %all-to-all-start = ((bf16[8,48,512]{2,1,0:T(8,128)(2,1)}), bf16[8,48,512]{2,1,0:T(8,128)(2,1)S(1)}, u32[]{:S(2)}, u32[]{:S(2)}) async-start(bf16[8,48,512]{2,1,0:T(8,128)(2,1)} %get-tuple-element.23), calls=%async_computation | async-start | bytes 786432 | tf_op jit(solution)/shard_map/all_to_all | solution.py:321
  10.6 2.8 %collective-permute-start.2 = (bf16[384,256]{1,0:T(8,128)(2,1)S(1)}, bf16[384,256]{1,0:T(8,128)(2,1)S(1)}, u32[]{:S(2)}, u32[]{:S(2)}) collective-permute-start(bf16[384,256]{1,0:T(8,128)(2,1)S(1)} %get-tuple-element.24.own), channel_id=1, source_target_pairs={{0,16},{8,24},{16,32},{24,40},{32,48},{40,56},{48,64},{56,72},{64,... | collective-permute-start | bytes 589832 | tf_op jit(solution)/shard_map/ppermute | solution.py:284
  13.4 1.3 %collective-permute-start = (bf16[384,256]{1,0:T(8,128)(2,1)S(1)}, bf16[384,256]{1,0:T(8,128)(2,1)S(1)}, u32[]{:S(2)}, u32[]{:S(2)}) collective-permute-start(bf16[384,256]{1,0:T(8,128)(2,1)S(1)} %get-tuple-element.24.own), channel_id=1, source_target_pairs={{0,8},{16,24},{32,40},{48,56},{64,72},{80,88},{96,104},{112,120},{... | collective-permute-start | bytes 589832 | tf_op jit(solution)/shard_map/ppermute | solution.py:284
  14.7 3.9 %collective-permute-done.2.before = bf16[384,256]{1,0:T(8,128)(2,1)S(1)} collective-permute-done((bf16[384,256]{1,0:T(8,128)(2,1)S(1)}, bf16[384,256]{1,0:T(8,128)(2,1)S(1)}, u32[]{:S(2)}, u32[]{:S(2)}) %collective-permute-start.2) | collective-permute-done | bytes 196640 | tf_op jit(solution)/shard_map/ppermute | solution.py:284
  18.7 3.0 %collective-permute-start.3 = (bf16[384,256]{1,0:T(8,128)(2,1)S(1)}, bf16[384,256]{1,0:T(8,128)(2,1)S(1)}, u32[]{:S(2)}, u32[]{:S(2)}) collective-permute-start(bf16[384,256]{1,0:T(8,128)(2,1)S(1)} %collective-permute-done.2.before), channel_id=1, source_target_pairs={{0,8},{8,0},{16,24},{24,16},{32,40},{40,32},{48,56},{56,48},{64,72... | collective-permute-start | bytes 589832 | tf_op jit(solution)/shard_map/ppermute | solution.py:288
  21.7 8.4 %collective-permute-start.1 = (bf16[256,256]{1,0:T(8,128)(2,1)S(1)}, bf16[256,256]{1,0:T(8,128)(2,1)S(1)}, u32[]{:S(2)}, u32[]{:S(2)}) collective-permute-start(bf16[256,256]{1,0:T(8,128)(2,1)S(1)} %get-tuple-element.25), channel_id=1, source_target_pairs={{8,32},{24,48},{40,64},{56,80},{72,96},{88,112},{104,128},{120,144... | collective-permute-start | bytes 393224 | tf_op jit(solution)/shard_map/ppermute | solution.py:284
  30.1 1.9 %collective-permute-done.1.apart = bf16[256,256]{1,0:T(8,128)(2,1)S(1)} collective-permute-done((bf16[256,256]{1,0:T(8,128)(2,1)S(1)}, bf16[256,256]{1,0:T(8,128)(2,1)S(1)}, u32[]{:S(2)}, u32[]{:S(2)}) %collective-permute-start.1) | collective-permute-done | bytes 131104 | tf_op jit(solution)/shard_map/ppermute | solution.py:284
  32.0 0.0 collective-permute-done.beside
  32.0 0.1 halo.1
  32.1 0.0 collective-permute-done.3.across
  32.1 4.2 %forward.1 = (bf16[1536,128]{1,0:T(8,128)(2,1)S(1)}, bf16[384,512]{1,0:T(8,128)(2,1)S(1)}, bf16[1408,128]{1,0:T(8,128)(2,1)S(1)}, bf16[1408,128]{1,0:T(8,128)(2,...) custom-call(s32[3]{0:T(128)} %start_hbm.1, ...), custom_call_target="tpu_custom_call" | custom-call | flops 905969664 | bytes 8388608 | tf_op jit(solution)/shard_map/forward/pallas_call | solution.py:350
  36.3 0.7 %copy-done = bf16[128,1408]{1,0:T(8,128)(2,1)} copy-done((bf16[128,1408]{1,0:T(8,128)(2,1)}, bf16[128,1408]{1,0:T(8,128)(2,1)S(1)}, u32[]{:S(2)}) %copy-start) | copy-done | bytes 360472
  37.1 1.0 %copy-done.1 = bf16[128,1408]{1,0:T(8,128)(2,1)S(1)} copy-done((bf16[128,1408]{1,0:T(8,128)(2,1)S(1)}, bf16[128,1408]{1,0:T(8,128)(2,1)}, u32[]{:S(2)}) %copy-start.1) | copy-done | bytes 360472
  38.1 5.2 %backward.1 = (bf16[8,48,512]{2,1,0:T(8,128)(2,1)}, bf16[640,256]{1,0:T(8,128)(2,1)S(1)}, bf16[384,256]{1,0:T(8,128)(2,1)S(1)}, bf16[256,256]{1,0:T(8,128)(2,1)S(1)}, f32[384,256]{1,0:T(8,128)S(1)}) custom-call(bf16[8,48,512]{2,1,0:T(8,128)(2,1)S(1)} %all-to-all-done.chunks, bf16[1536,128]{1,0:T(8,128)(2,1)S(1)} %get-tuple-element.28.queries, ...), custom_call_target="tpu_custom_call" | custom-call | flops 2264924160 | bytes 8388608 | tf_op jit(solution)/shard_map/backward/pallas_call | solution.py:377
  43.2 6.2 %all-to-all-start.1 = ((bf16[8,48,512]{2,1,0:T(8,128)(2,1)}), bf16[8,48,512]{2,1,0:T(8,128)(2,1)S(1)}, u32[]{:S(2)}, u32[]{:S(2)}) async-start(bf16[8,48,512]{2,1,0:T(8,128)(2,1)} %get-tuple-element.36), calls=%async_computation.1 | async-start | bytes 786432 | tf_op jit(solution)/shard_map/all_to_all | solution.py:321
  49.5 1.9 %collective-permute-start.4 = (bf16[640,256]{1,0:T(8,128)(2,1)S(1)}, bf16[640,256]{1,0:T(8,128)(2,1)S(1)}, u32[]{:S(2)}, u32[]{:S(2)}) collective-permute-start(bf16[640,256]{1,0:T(8,128)(2,1)S(1)} %get-tuple-element.38), channel_id=1, source_target_pairs={{0,8},{8,0},{16,24},{24,16},{32,40},{40,32},{48,56},{56,48},{64,72... | collective-permute-start | bytes 983048 | tf_op jit(solution)/shard_map/ppermute | solution.py:288
  51.4 1.6 %collective-permute-done.4.received = bf16[640,256]{1,0:T(8,128)(2,1)S(1)} collective-permute-done((bf16[640,256]{1,0:T(8,128)(2,1)S(1)}, bf16[640,256]{1,0:T(8,128)(2,1)S(1)}, u32[]{:S(2)}, u32[]{:S(2)}) %collective-permute-start.4) | collective-permute-done | bytes 327712 | tf_op jit(solution)/shard_map/ppermute | solution.py:288
  53.0 1.9 %collective-permute-start.6 = (bf16[384,256]{1,0:T(8,128)(2,1)S(1)}, bf16[384,256]{1,0:T(8,128)(2,1)S(1)}, u32[]{:S(2)}, u32[]{:S(2)}) collective-permute-start(bf16[384,256]{1,0:T(8,128)(2,1)S(1)} %merge.1), channel_id=1, source_target_pairs={{16,0},{24,8},{32,16},{40,24},{48,32},{56,40},{64,48},{72,56},{80,... | collective-permute-start | bytes 589832 | tf_op jit(solution)/shard_map/ppermute | solution.py:284
  55.0 1.3 %collective-permute-start.5 = (bf16[256,256]{1,0:T(8,128)(2,1)S(1)}, bf16[256,256]{1,0:T(8,128)(2,1)S(1)}, u32[]{:S(2)}, u32[]{:S(2)}) collective-permute-start(bf16[256,256]{1,0:T(8,128)(2,1)S(1)} %get-tuple-element.39), channel_id=1, source_target_pairs={{32,8},{48,24},{64,40},{80,56},{96,72},{112,88},{128,104},{144,120... | collective-permute-start | bytes 393224 | tf_op jit(solution)/shard_map/ppermute | solution.py:284
  56.3 10.7 %collective-permute-done.5.apart = bf16[256,256]{1,0:T(8,128)(2,1)S(1)} collective-permute-done((bf16[256,256]{1,0:T(8,128)(2,1)S(1)}, bf16[256,256]{1,0:T(8,128)(2,1)S(1)}, u32[]{:S(2)}, u32[]{:S(2)}) %collective-permute-start.5) | collective-permute-done | bytes 131104 | tf_op jit(solution)/shard_map/ppermute | solution.py:284
  67.0 0.0 collective-permute-done.6.shifted
  67.0 0.7 %sum.1 = (bf16[384,128]{1,0:T(8,128)(2,1)}, bf16[384,128]{1,0:T(8,128)(2,1)}) custom-call(f32[384,256]{1,0:T(8,128)S(1)} %fold.1.folded, bf16[384,256]{1,0:T(8,128)(2,1)S(1)} %collective-permute-done.6.shifted), custom_call_target="tpu_custom_call" | custom-call | tf_op jit(solution)/shard_map/sum/pallas_call | solution.py:422
  67.7 0.8 %place.1 = bf16[48,4096]{1,0:T(8,128)(2,1)} custom-call(bf16[8,48,512]{2,1,0:T(8,128)(2,1)S(1)} %all-to-all-done.1.chunks), custom_call_target="tpu_custom_call" | custom-call | tf_op jit(solution)/shard_map/place/pallas_call | solution.py:431
  (6 shorter events, 0.1 us)
Async XLA Ops:
  2.7 34.4 %all-to-all-start = ((bf16[8,48,512]{2,1,0:T(8,128)(2,1)}), bf16[8,48,512]{2,1,0:T(8,128)(2,1)S(1)}, u32[]{:S(2)}, u32[]{:S(2)}) async-start(bf16[8,48,512]{2,1,0:T(8,128)(2,1)} %get-tuple-element.23), calls=%async_computation | async-start | bytes 786432 | tf_op jit(solution)/shard_map/all_to_all | solution.py:321
  10.6 8.1 %collective-permute-start.2 = (bf16[384,256]{1,0:T(8,128)(2,1)S(1)}, bf16[384,256]{1,0:T(8,128)(2,1)S(1)}, u32[]{:S(2)}, u32[]{:S(2)}) collective-permute-start(bf16[384,256]{1,0:T(8,128)(2,1)S(1)} %get-tuple-element.24.own), channel_id=1, source_target_pairs={{0,16},{8,24},{16,32},{24,40},{32,48},{40,56},{48,64},{56,72},{64,... | collective-permute-start | bytes 589832 | tf_op jit(solution)/shard_map/ppermute | solution.py:284
  13.4 18.6 %collective-permute-start = (bf16[384,256]{1,0:T(8,128)(2,1)S(1)}, bf16[384,256]{1,0:T(8,128)(2,1)S(1)}, u32[]{:S(2)}, u32[]{:S(2)}) collective-permute-start(bf16[384,256]{1,0:T(8,128)(2,1)S(1)} %get-tuple-element.24.own), channel_id=1, source_target_pairs={{0,8},{16,24},{32,40},{48,56},{64,72},{80,88},{96,104},{112,120},{... | collective-permute-start | bytes 589832 | tf_op jit(solution)/shard_map/ppermute | solution.py:284
  18.7 13.5 %collective-permute-start.3 = (bf16[384,256]{1,0:T(8,128)(2,1)S(1)}, bf16[384,256]{1,0:T(8,128)(2,1)S(1)}, u32[]{:S(2)}, u32[]{:S(2)}) collective-permute-start(bf16[384,256]{1,0:T(8,128)(2,1)S(1)} %collective-permute-done.2.before), channel_id=1, source_target_pairs={{0,8},{8,0},{16,24},{24,16},{32,40},{40,32},{48,56},{56,48},{64,72... | collective-permute-start | bytes 589832 | tf_op jit(solution)/shard_map/ppermute | solution.py:288
  21.7 10.3 %collective-permute-start.1 = (bf16[256,256]{1,0:T(8,128)(2,1)S(1)}, bf16[256,256]{1,0:T(8,128)(2,1)S(1)}, u32[]{:S(2)}, u32[]{:S(2)}) collective-permute-start(bf16[256,256]{1,0:T(8,128)(2,1)S(1)} %get-tuple-element.25), channel_id=1, source_target_pairs={{8,32},{24,48},{40,64},{56,80},{72,96},{88,112},{104,128},{120,144... | collective-permute-start | bytes 393224 | tf_op jit(solution)/shard_map/ppermute | solution.py:284
  36.3 0.7 %copy-start = (bf16[128,1408]{1,0:T(8,128)(2,1)}, bf16[128,1408]{1,0:T(8,128)(2,1)S(1)}, u32[]{:S(2)}) copy-start(bf16[128,1408]{1,0:T(8,128)(2,1)S(1)} %get-tuple-element.32.key_t) | copy-start | bytes 1081348
  37.1 1.0 %copy-start.1 = (bf16[128,1408]{1,0:T(8,128)(2,1)S(1)}, bf16[128,1408]{1,0:T(8,128)(2,1)}, u32[]{:S(2)}) copy-start(bf16[128,1408]{1,0:T(8,128)(2,1)} %copy-done) | copy-start | bytes 1081348
  43.2 24.5 %all-to-all-start.1 = ((bf16[8,48,512]{2,1,0:T(8,128)(2,1)}), bf16[8,48,512]{2,1,0:T(8,128)(2,1)S(1)}, u32[]{:S(2)}, u32[]{:S(2)}) async-start(bf16[8,48,512]{2,1,0:T(8,128)(2,1)} %get-tuple-element.36), calls=%async_computation.1 | async-start | bytes 786432 | tf_op jit(solution)/shard_map/all_to_all | solution.py:321
  49.5 3.5 %collective-permute-start.4 = (bf16[640,256]{1,0:T(8,128)(2,1)S(1)}, bf16[640,256]{1,0:T(8,128)(2,1)S(1)}, u32[]{:S(2)}, u32[]{:S(2)}) collective-permute-start(bf16[640,256]{1,0:T(8,128)(2,1)S(1)} %get-tuple-element.38), channel_id=1, source_target_pairs={{0,8},{8,0},{16,24},{24,16},{32,40},{40,32},{48,56},{56,48},{64,72... | collective-permute-start | bytes 983048 | tf_op jit(solution)/shard_map/ppermute | solution.py:288
  53.0 13.9 %collective-permute-start.6 = (bf16[384,256]{1,0:T(8,128)(2,1)S(1)}, bf16[384,256]{1,0:T(8,128)(2,1)S(1)}, u32[]{:S(2)}, u32[]{:S(2)}) collective-permute-start(bf16[384,256]{1,0:T(8,128)(2,1)S(1)} %merge.1), channel_id=1, source_target_pairs={{16,0},{24,8},{32,16},{40,24},{48,32},{56,40},{64,48},{72,56},{80,... | collective-permute-start | bytes 589832 | tf_op jit(solution)/shard_map/ppermute | solution.py:284
  55.0 12.0 %collective-permute-start.5 = (bf16[256,256]{1,0:T(8,128)(2,1)S(1)}, bf16[256,256]{1,0:T(8,128)(2,1)S(1)}, u32[]{:S(2)}, u32[]{:S(2)}) collective-permute-start(bf16[256,256]{1,0:T(8,128)(2,1)S(1)} %get-tuple-element.39), channel_id=1, source_target_pairs={{32,8},{48,24},{64,40},{80,56},{96,72},{112,88},{128,104},{144,120... | collective-permute-start | bytes 393224 | tf_op jit(solution)/shard_map/ppermute | solution.py:284

commit v4 on v3

--- a/solution.py
+++ b/solution.py
@@ -75,38 +75,9 @@
     finish(started(moves, sems))
 
 
-def halo_kernel(own, beside, apart, keys, values):
-    odd = on_odd_core()
-    for part, win in enumerate((keys, values)):
-        cols = block(part)
-        win[TAIL + 2 * SPAN :, :] = own[:, cols]
-
-        @pl.when(odd)
-        def _():
-            win[0:TAIL, :] = jnp.zeros((TAIL, HEAD), win.dtype)
-            win[TAIL + SPAN : TAIL + 2 * SPAN, :] = beside[:, cols]
-
-        @pl.when(jnp.logical_not(odd))
-        def _():
-            win[0:TAIL, :] = apart[:, cols]
-            win[TAIL + SPAN : TAIL + 2 * SPAN, :] = jnp.zeros((SPAN, HEAD), win.dtype)
-
-        win[TAIL : TAIL + SPAN, :] = jnp.zeros((SPAN, HEAD), win.dtype)
-
-
-def complete(win, part, partial, before, across):
+def window_of(part, far, mid, near, own):
     cols = block(part)
-    win[...] = partial[...]
-    win[TAIL : TAIL + SPAN, :] = before[:, cols]
-    odd = on_odd_core()
-
-    @pl.when(odd)
-    def _():
-        win[0:TAIL, :] = across[SPAN - TAIL :, cols]
-
-    @pl.when(jnp.logical_not(odd))
-    def _():
-        win[TAIL + SPAN : TAIL + 2 * SPAN, :] = across[:, cols]
+    return jnp.concatenate([far[:, cols], mid[:, cols], near[:, cols], own[:, cols]], axis=0)
 
 
 def causal_mask():
@@ -124,15 +95,15 @@
 
 
 def forward_kernel(
-    start_hbm, query_hbm, keys, values, before, across,
-    queries, queries_t, key_win, value_win, key_t, attended_ref, norm_ref, starts,
+    start_hbm, query_hbm, own, near, mid, far,
+    queries, key_win, value_win, attended_ref, norm_ref, starts,
     start_ref, query_ref, value_t, held, weights, sems
 ):
     arriving = started([(query_hbm, query_ref), (start_hbm, start_ref)], sems)
-    complete(key_win, 0, keys, before, across)
-    complete(value_win, 1, values, before, across)
-    value_t[...] = value_win[...].T
-    key_t[...] = key_win[...].T
+    key_win[...] = window_of(0, far, mid, near, own)
+    turned_values = window_of(1, far, mid, near, own)
+    value_win[...] = turned_values
+    value_t[...] = turned_values.T
     causal = causal_mask()
     first = first_key()
     finish(arriving)
@@ -140,7 +111,6 @@
         stacked = heads_stacked(query_ref[block(i), :])
         queries[block(i * GROUP, GROUP), :] = stacked
         turned = stacked.T
-        queries_t[block(i), :] = turned
         start = start_ref[i]
         starts[row8(i), :] = jnp.full((8, WIDE), start, jnp.int32)
         best = jnp.full((8, WIDE), -jnp.inf, jnp.float32)
@@ -165,9 +135,9 @@
 
 
 def backward_kernel(
-    chunks, queries, queries_t, key_win, value_win, key_t, attended_ref, norm_ref, starts,
+    chunks, queries, key_win, value_win, attended_ref, norm_ref, starts,
     dchunks, dnear_far, dmid, dfar, down,
-    grad_ref, weights, held, dkey, dvalue, dquery
+    key_t, grad_ref, weights, held, dkey, dvalue, dquery
 ):
     parts, share = chunks.shape[0], chunks.shape[1]
 
@@ -176,6 +146,7 @@
 
     for p in range(parts):
         grad_ref[share_rows(p), :] = chunks[p]
+    key_t[...] = key_win[...].T
     causal = causal_mask()
     first = first_key()
     on_diagonal = lax.broadcasted_iota(jnp.int32, (BLOCK, BLOCK), 0) == lax.broadcasted_iota(
@@ -184,6 +155,7 @@
     for i in range(OWN):
         grads = heads_stacked(grad_ref[block(i), :])
         grads_t = grads.T
+        queries_t = queries[block(i * GROUP, GROUP), :].T
         deltas = []
         for h in range(GROUP):
             cross = dot(grads[block(h), :], attended_ref[block(i), block(h)], NN)
@@ -192,7 +164,7 @@
         norm = norm_ref[8 * i : 8 * i + 1, :]
         start = starts[8 * i : 8 * i + 1, :]
         for j in range(REACH):
-            score = dot(key_win[block(i + j), :], queries_t[block(i), :], NN)
+            score = dot(key_win[block(i + j), :], queries_t, NN)
             if j == REACH - 1:
                 weight = jnp.where(causal, jnp.exp2(score * TO_EXP2 - norm), 0.0)
             else:
@@ -333,34 +305,22 @@
         name="prepare",
     )(*pinned(grad_output, key_states, value_states))
     grads = exchanged(chunks)
-    before = passed_along(own, 2)
-    apart = passed_along(last, 3, (1,))
-    beside = passed_along(own, 1, (0,))
-    across = core_swapped(before)
-    keys, values = pl.pallas_call(
-        halo_kernel,
-        out_shape=(sds((window, HEAD), bf16),) * 2,
-        in_specs=[VMEM] * 3,
-        out_specs=(VMEM,) * 2,
-        cost_estimate=cost(flops),
-        compiler_params=params(4),
-        name="halo",
-    )(own, beside, apart)
+    far = passed_along(last, 3)
+    mid = passed_along(own, 2)
+    near = passed_along(own, 1)
 
     kept = pl.pallas_call(
         forward_kernel,
         out_shape=(
             sds((OWN * WIDE, HEAD), bf16),
-            sds((OWN * HEAD, WIDE), bf16),
             sds((window, HEAD), bf16),
             sds((window, HEAD), bf16),
-            sds((HEAD, window), bf16),
             sds((OWN * HEAD, WIDE), bf16),
             sds((8 * OWN, WIDE), f32),
             sds((8 * OWN, WIDE), jnp.int32),
         ),
         in_specs=[HBM, HBM] + [VMEM] * 4,
-        out_specs=(VMEM,) * 8,
+        out_specs=(VMEM,) * 6,
         scratch_shapes=[
             pltpu.SMEM(doc_start.shape, jnp.int32),
             pltpu.VMEM((SPAN, WIDE), bf16),
@@ -372,7 +332,7 @@
         cost_estimate=cost(2 * flops, pairs * BLOCK * WIDE),
         compiler_params=params(16),
         name="forward",
-    )(start_hbm, query_hbm, keys, values, before, across)
+    )(start_hbm, query_hbm, own, near, mid, far)
 
     dchunks, dnear_far, dmid, dfar, down = pl.pallas_call(
         backward_kernel,
@@ -383,9 +343,10 @@
             tail,
             sds((SPAN, 2 * HEAD), f32),
         ),
-        in_specs=[VMEM] * 9,
+        in_specs=[VMEM] * 7,
         out_specs=(VMEM,) * 5,
         scratch_shapes=[
+            pltpu.VMEM((HEAD, window), bf16),
             pltpu.VMEM((SPAN, WIDE), bf16),
             pltpu.VMEM((pairs * BLOCK, WIDE), bf16),
             pltpu.VMEM((pairs * BLOCK, WIDE), bf16),

time: 69.1 us -> 62.9 us (0.910)
  the two profiles are of different devices: /device:TPU:205 before, /device:TPU:198 now
where the time goes in v4:
time: 62.9 us; the launch traced here: 62.1 us
  starting transfers between devices  34.8 us (55%)
  waiting for transfers between devices  13.4 us (21%)
  Pallas kernels  13.1 us (21%)
  between operations  0.73 us (1%)
    ppermute x5, starting transfers between devices, passed_along(): return lax.ppermute(value, 'ctx', pairs)  18 us
    all_to_all x2, starting transfers between devices, exchanged(): lax.all_to_all(value, ('ctx', 'kvh'), split_axis=0, concat_axis=0, axis_i...  13 us
    ppermute x5, waiting for transfers between devices, passed_along(): return lax.ppermute(value, 'ctx', pairs)  12.2 us
    pallas_call x1, Pallas kernels, body(): pl.pallas_call(backward_kernel, out_shape=(chunked, sds((SPAN + TAIL, 2 *...  5.35 us
    pallas_call x1, Pallas kernels, body(): pl.pallas_call(forward_kernel, out_shape=(sds((OWN * WIDE, HEAD), bf16),...  4.13 us
    ppermute x1, starting transfers between devices, core_swapped(): lax.ppermute(value, 'ctx', [(i, i ^ 1) for i in range(lax.axis_size('ctx'...  3.83 us
    pallas_call x1, Pallas kernels, body(): pl.pallas_call(prepare_kernel, out_shape=(chunked, pair, tail), in_specs=...  2.03 us
  transfers between devices with their start and end apart: 8, of which 4 were waited for; matrix products, arithmetic and copies ran while one was open for 0% of the time, Pallas kernels for 8%

profile of v4, /device:TPU:198, one launch (start us, length us, event | category | flops | bytes accessed | tf_op | source)
XLA Modules:
  0.0 62.1 jit_solution(1304320416444938982)
XLA Ops:
  0.6 2.0 %prepare.1 = (bf16[8,48,512]{2,1,0:T(8,128)(2,1)}, bf16[384,256]{1,0:T(8,128)(2,1)S(1)}, bf16[256,256]{1,0:T(8,128)(2,1)S(1)}) custom-call(bf16[48,4096]{1,0:T(8,128)(2,1)} %grad_hbm.1, bf16[384,128]{1,0:T(8,128)(2,1)} %key_hbm.1, bf16[384,128]{1,0:T(8,128)(2,1)} %value_hbm.1), custom_call_target="tpu_custom_call" | custom-call | tf_op jit(solution)/shard_map/prepare/pallas_call | solution.py:298
  2.7 7.1 %all-to-all-start = ((bf16[8,48,512]{2,1,0:T(8,128)(2,1)}), bf16[8,48,512]{2,1,0:T(8,128)(2,1)S(1)}, u32[]{:S(2)}, u32[]{:S(2)}) async-start(bf16[8,48,512]{2,1,0:T(8,128)(2,1)} %get-tuple-element.19), calls=%async_computation | async-start | bytes 786432 | tf_op jit(solution)/shard_map/all_to_all | solution.py:293
  9.8 5.4 %collective-permute-start.1 = (bf16[384,256]{1,0:T(8,128)(2,1)S(1)}, bf16[384,256]{1,0:T(8,128)(2,1)S(1)}, u32[]{:S(2)}, u32[]{:S(2)}) collective-permute-start(bf16[384,256]{1,0:T(8,128)(2,1)S(1)} %get-tuple-element.20.own), channel_id=1, source_target_pairs={{0,16},{8,24},{16,32},{24,40},{32,48},{40,56},{48,64},{56,72},{64,... | collective-permute-start | bytes 589832 | tf_op jit(solution)/shard_map/ppermute | solution.py:256
  15.2 3.3 %collective-permute-start = (bf16[384,256]{1,0:T(8,128)(2,1)S(1)}, bf16[384,256]{1,0:T(8,128)(2,1)S(1)}, u32[]{:S(2)}, u32[]{:S(2)}) collective-permute-start(bf16[384,256]{1,0:T(8,128)(2,1)S(1)} %get-tuple-element.20.own), channel_id=1, source_target_pairs={{0,8},{8,16},{16,24},{24,32},{32,40},{40,48},{48,56},{56,64},{64,7... | collective-permute-start | bytes 589832 | tf_op jit(solution)/shard_map/ppermute | solution.py:256
  18.5 3.2 %collective-permute-start.2 = (bf16[256,256]{1,0:T(8,128)(2,1)S(1)}, bf16[256,256]{1,0:T(8,128)(2,1)S(1)}, u32[]{:S(2)}, u32[]{:S(2)}) collective-permute-start(bf16[256,256]{1,0:T(8,128)(2,1)S(1)} %get-tuple-element.21), channel_id=1, source_target_pairs={{0,24},{8,32},{16,40},{24,48},{32,56},{40,64},{48,72},{56,80},{64,... | collective-permute-start | bytes 393224 | tf_op jit(solution)/shard_map/ppermute | solution.py:256
  21.7 4.5 %collective-permute-done.2.far = bf16[256,256]{1,0:T(8,128)(2,1)S(1)} collective-permute-done((bf16[256,256]{1,0:T(8,128)(2,1)S(1)}, bf16[256,256]{1,0:T(8,128)(2,1)S(1)}, u32[]{:S(2)}, u32[]{:S(2)}) %collective-permute-start.2) | collective-permute-done | bytes 131104 | tf_op jit(solution)/shard_map/ppermute | solution.py:256
  26.3 0.0 collective-permute-done.1.mid
  26.3 0.0 collective-permute-done.near
  26.3 4.1 %forward.1 = (bf16[1536,128]{1,0:T(8,128)(2,1)S(1)}, bf16[1408,128]{1,0:T(8,128)(2,1)S(1)}, bf16[1408,128]{1,0:T(8,128)(2,1)S(1)}, bf16[384,512]{1,0:T(8,128)(2,...) custom-call(s32[3]{0:T(128)} %start_hbm.1, bf16[384,512]{1,0:T(8,128)(2,1)} %query_hbm.1, ...), custom_call_target="tpu_custom_call" | custom-call | flops 905969664 | bytes 8388608 | tf_op jit(solution)/shard_map/forward/pallas_call | solution.py:312
  30.4 0.0 all-to-all-done.chunks
  30.4 5.4 %backward.1 = (bf16[8,48,512]{2,1,0:T(8,128)(2,1)}, bf16[640,256]{1,0:T(8,128)(2,1)S(1)}, bf16[384,256]{1,0:T(8,128)(2,1)S(1)}, bf16[256,256]{1,0:T(8,128)(2,1)S(1)}, f32[384,256]{1,0:T(8,128)S(1)}) custom-call(bf16[8,48,512]{2,1,0:T(8,128)(2,1)S(1)} %all-to-all-done.chunks, bf16[1536,128]{1,0:T(8,128)(2,1)S(1)} %get-tuple-element.22.queries, ...), custom_call_target="tpu_custom_call" | custom-call | flops 2264924160 | bytes 8388608 | tf_op jit(solution)/shard_map/backward/pallas_call | solution.py:337
  35.8 5.8 %all-to-all-start.1 = ((bf16[8,48,512]{2,1,0:T(8,128)(2,1)}), bf16[8,48,512]{2,1,0:T(8,128)(2,1)S(1)}, u32[]{:S(2)}, u32[]{:S(2)}) async-start(bf16[8,48,512]{2,1,0:T(8,128)(2,1)} %get-tuple-element.28), calls=%async_computation.1 | async-start | bytes 786432 | tf_op jit(solution)/shard_map/all_to_all | solution.py:293
  41.6 3.8 %collective-permute-start.3 = (bf16[640,256]{1,0:T(8,128)(2,1)S(1)}, bf16[640,256]{1,0:T(8,128)(2,1)S(1)}, u32[]{:S(2)}, u32[]{:S(2)}) collective-permute-start(bf16[640,256]{1,0:T(8,128)(2,1)S(1)} %get-tuple-element.30), channel_id=1, source_target_pairs={{0,8},{8,0},{16,24},{24,16},{32,40},{40,32},{48,56},{56,48},{64,72... | collective-permute-start | bytes 983048 | tf_op jit(solution)/shard_map/ppermute | solution.py:260
  45.5 1.2 %collective-permute-done.3.received = bf16[640,256]{1,0:T(8,128)(2,1)S(1)} collective-permute-done((bf16[640,256]{1,0:T(8,128)(2,1)S(1)}, bf16[640,256]{1,0:T(8,128)(2,1)S(1)}, u32[]{:S(2)}, u32[]{:S(2)}) %collective-permute-start.3) | collective-permute-done | bytes 327712 | tf_op jit(solution)/shard_map/ppermute | solution.py:260
  46.7 2.6 %collective-permute-start.5 = (bf16[384,256]{1,0:T(8,128)(2,1)S(1)}, bf16[384,256]{1,0:T(8,128)(2,1)S(1)}, u32[]{:S(2)}, u32[]{:S(2)}) collective-permute-start(bf16[384,256]{1,0:T(8,128)(2,1)S(1)} %merge.1), channel_id=1, source_target_pairs={{16,0},{24,8},{32,16},{40,24},{48,32},{56,40},{64,48},{72,56},{80,... | collective-permute-start | bytes 589832 | tf_op jit(solution)/shard_map/ppermute | solution.py:256
  49.3 3.5 %collective-permute-start.4 = (bf16[256,256]{1,0:T(8,128)(2,1)S(1)}, bf16[256,256]{1,0:T(8,128)(2,1)S(1)}, u32[]{:S(2)}, u32[]{:S(2)}) collective-permute-start(bf16[256,256]{1,0:T(8,128)(2,1)S(1)} %get-tuple-element.31), channel_id=1, source_target_pairs={{32,8},{48,24},{64,40},{80,56},{96,72},{112,88},{128,104},{144,120... | collective-permute-start | bytes 393224 | tf_op jit(solution)/shard_map/ppermute | solution.py:256
  52.9 2.5 %collective-permute-done.4.apart = bf16[256,256]{1,0:T(8,128)(2,1)S(1)} collective-permute-done((bf16[256,256]{1,0:T(8,128)(2,1)S(1)}, bf16[256,256]{1,0:T(8,128)(2,1)S(1)}, u32[]{:S(2)}, u32[]{:S(2)}) %collective-permute-start.4) | collective-permute-done | bytes 131104 | tf_op jit(solution)/shard_map/ppermute | solution.py:256
  55.4 5.1 %collective-permute-done.5.shifted = bf16[384,256]{1,0:T(8,128)(2,1)S(1)} collective-permute-done((bf16[384,256]{1,0:T(8,128)(2,1)S(1)}, bf16[384,256]{1,0:T(8,128)(2,1)S(1)}, u32[]{:S(2)}, u32[]{:S(2)}) %collective-permute-start.5) | collective-permute-done | bytes 196640 | tf_op jit(solution)/shard_map/ppermute | solution.py:256
  60.5 0.7 %sum.1 = (bf16[384,128]{1,0:T(8,128)(2,1)}, bf16[384,128]{1,0:T(8,128)(2,1)}) custom-call(f32[384,256]{1,0:T(8,128)S(1)} %fold.1.folded, bf16[384,256]{1,0:T(8,128)(2,1)S(1)} %collective-permute-done.5.shifted), custom_call_target="tpu_custom_call" | custom-call | tf_op jit(solution)/shard_map/sum/pallas_call | solution.py:383
  61.3 0.0 all-to-all-done.1.chunks
  61.3 0.8 %place.1 = bf16[48,4096]{1,0:T(8,128)(2,1)} custom-call(bf16[8,48,512]{2,1,0:T(8,128)(2,1)S(1)} %all-to-all-done.1.chunks), custom_call_target="tpu_custom_call" | custom-call | tf_op jit(solution)/shard_map/place/pallas_call | solution.py:392
  (2 shorter events, 0.1 us)
Async XLA Ops:
  2.7 27.7 %all-to-all-start = ((bf16[8,48,512]{2,1,0:T(8,128)(2,1)}), bf16[8,48,512]{2,1,0:T(8,128)(2,1)S(1)}, u32[]{:S(2)}, u32[]{:S(2)}) async-start(bf16[8,48,512]{2,1,0:T(8,128)(2,1)} %get-tuple-element.19), calls=%async_computation | async-start | bytes 786432 | tf_op jit(solution)/shard_map/all_to_all | solution.py:293
  9.8 16.5 %collective-permute-start.1 = (bf16[384,256]{1,0:T(8,128)(2,1)S(1)}, bf16[384,256]{1,0:T(8,128)(2,1)S(1)}, u32[]{:S(2)}, u32[]{:S(2)}) collective-permute-start(bf16[384,256]{1,0:T(8,128)(2,1)S(1)} %get-tuple-element.20.own), channel_id=1, source_target_pairs={{0,16},{8,24},{16,32},{24,40},{32,48},{40,56},{48,64},{56,72},{64,... | collective-permute-start | bytes 589832 | tf_op jit(solution)/shard_map/ppermute | solution.py:256
  15.2 11.1 %collective-permute-start = (bf16[384,256]{1,0:T(8,128)(2,1)S(1)}, bf16[384,256]{1,0:T(8,128)(2,1)S(1)}, u32[]{:S(2)}, u32[]{:S(2)}) collective-permute-start(bf16[384,256]{1,0:T(8,128)(2,1)S(1)} %get-tuple-element.20.own), channel_id=1, source_target_pairs={{0,8},{8,16},{16,24},{24,32},{32,40},{40,48},{48,56},{56,64},{64,7... | collective-permute-start | bytes 589832 | tf_op jit(solution)/shard_map/ppermute | solution.py:256
  18.5 7.8 %collective-permute-start.2 = (bf16[256,256]{1,0:T(8,128)(2,1)S(1)}, bf16[256,256]{1,0:T(8,128)(2,1)S(1)}, u32[]{:S(2)}, u32[]{:S(2)}) collective-permute-start(bf16[256,256]{1,0:T(8,128)(2,1)S(1)} %get-tuple-element.21), channel_id=1, source_target_pairs={{0,24},{8,32},{16,40},{24,48},{32,56},{40,64},{48,72},{56,80},{64,... | collective-permute-start | bytes 393224 | tf_op jit(solution)/shard_map/ppermute | solution.py:256
  35.8 25.5 %all-to-all-start.1 = ((bf16[8,48,512]{2,1,0:T(8,128)(2,1)}), bf16[8,48,512]{2,1,0:T(8,128)(2,1)S(1)}, u32[]{:S(2)}, u32[]{:S(2)}) async-start(bf16[8,48,512]{2,1,0:T(8,128)(2,1)} %get-tuple-element.28), calls=%async_computation.1 | async-start | bytes 786432 | tf_op jit(solution)/shard_map/all_to_all | solution.py:293
  41.6 5.1 %collective-permute-start.3 = (bf16[640,256]{1,0:T(8,128)(2,1)S(1)}, bf16[640,256]{1,0:T(8,128)(2,1)S(1)}, u32[]{:S(2)}, u32[]{:S(2)}) collective-permute-start(bf16[640,256]{1,0:T(8,128)(2,1)S(1)} %get-tuple-element.30), channel_id=1, source_target_pairs={{0,8},{8,0},{16,24},{24,16},{32,40},{40,32},{48,56},{56,48},{64,72... | collective-permute-start | bytes 983048 | tf_op jit(solution)/shard_map/ppermute | solution.py:260
  46.7 13.8 %collective-permute-start.5 = (bf16[384,256]{1,0:T(8,128)(2,1)S(1)}, bf16[384,256]{1,0:T(8,128)(2,1)S(1)}, u32[]{:S(2)}, u32[]{:S(2)}) collective-permute-start(bf16[384,256]{1,0:T(8,128)(2,1)S(1)} %merge.1), channel_id=1, source_target_pairs={{16,0},{24,8},{32,16},{40,24},{48,32},{56,40},{64,48},{72,56},{80,... | collective-permute-start | bytes 589832 | tf_op jit(solution)/shard_map/ppermute | solution.py:256
  49.3 6.1 %collective-permute-start.4 = (bf16[256,256]{1,0:T(8,128)(2,1)S(1)}, bf16[256,256]{1,0:T(8,128)(2,1)S(1)}, u32[]{:S(2)}, u32[]{:S(2)}) collective-permute-start(bf16[256,256]{1,0:T(8,128)(2,1)S(1)} %get-tuple-element.31), channel_id=1, source_target_pairs={{32,8},{48,24},{64,40},{80,56},{96,72},{112,88},{128,104},{144,120... | collective-permute-start | bytes 393224 | tf_op jit(solution)/shard_map/ppermute | solution.py:256

commit v5 on v4

--- a/solution.py
+++ b/solution.py
@@ -73,6 +73,10 @@
         (value_hbm.at[last, :], tail.at[:, HEAD:]),
     ]
     finish(started(moves, sems))
+
+
+def later_kernel(own, later):
+    later[...] = own[...]
 
 
 def window_of(part, far, mid, near, own):
@@ -306,6 +310,15 @@
     )(*pinned(grad_output, key_states, value_states))
     grads = exchanged(chunks)
     far = passed_along(last, 3)
+    own = pl.pallas_call(
+        later_kernel,
+        out_shape=pair,
+        in_specs=[VMEM],
+        out_specs=VMEM,
+        cost_estimate=cost(12 * flops),
+        compiler_params=params(4),
+        name="later",
+    )(own)
     mid = passed_along(own, 2)
     near = passed_along(own, 1)
 
@@ -376,7 +389,7 @@
         out_shape=sds((SPAN, 2 * HEAD), f32),
         in_specs=[VMEM] * 3,
         out_specs=VMEM,
-        cost_estimate=cost(flops),
+        cost_estimate=cost(12 * flops),
         compiler_params=params(4),
         name="fold",
     )(down, received, far_back)

time: 62.9 us -> 62.3 us (level)
  starting transfers between devices: 34.8 us -> 34.1 us
    ppermute x1, starting transfers between devices: 3.83 us -> 1.91 us  [core_swapped(): lax.ppermute(value, 'ctx', [(i, i ^ 1) for i in range(lax.axis_size('ctx'...]
    ppermute x5, waiting for transfers between devices: 12.2 us -> 13.8 us  [passed_along(): return lax.ppermute(value, 'ctx', pairs)]
    ppermute x1, waiting for transfers between devices: 1.23 us -> 0.01 us  [core_swapped(): lax.ppermute(value, 'ctx', [(i, i ^ 1) for i in range(lax.axis_size('ctx'...]
    ppermute x5, starting transfers between devices: 18 us -> 19.1 us  [passed_along(): return lax.ppermute(value, 'ctx', pairs)]
  transfers between devices with their start and end apart: 8 -> 8, of which waited for: 4 -> 3; matrix products, arithmetic and copies ran while one was open for 0% -> 0% of each run, Pallas kernels for 8% -> 8%
where the time goes in v5:
time: 62.3 us; the launch traced here: 61.8 us
  starting transfers between devices  34.1 us (55%)
  waiting for transfers between devices  13.8 us (22%)
  Pallas kernels  13.2 us (21%)
  between operations  0.74 us (1%)
    ppermute x5, starting transfers between devices, passed_along(): return lax.ppermute(value, 'ctx', pairs)  19.1 us
    ppermute x5, waiting for transfers between devices, passed_along(): return lax.ppermute(value, 'ctx', pairs)  13.8 us
    all_to_all x2, starting transfers between devices, exchanged(): lax.all_to_all(value, ('ctx', 'kvh'), split_axis=0, concat_axis=0, axis_i...  13.1 us
    pallas_call x1, Pallas kernels, body(): pl.pallas_call(backward_kernel, out_shape=(chunked, sds((SPAN + TAIL, 2 *...  5.35 us
    pallas_call x1, Pallas kernels, body(): pl.pallas_call(forward_kernel, out_shape=(sds((OWN * WIDE, HEAD), bf16),...  4.13 us
    pallas_call x1, Pallas kernels, body(): pl.pallas_call(prepare_kernel, out_shape=(chunked, pair, tail), in_specs=...  2.03 us
    ppermute x1, starting transfers between devices, core_swapped(): lax.ppermute(value, 'ctx', [(i, i ^ 1) for i in range(lax.axis_size('ctx'...  1.91 us
  transfers between devices with their start and end apart: 8, of which 3 were waited for; matrix products, arithmetic and copies ran while one was open for 0% of the time, Pallas kernels for 8%

profile of v5, /device:TPU:198, one launch (start us, length us, event | category | flops | bytes accessed | tf_op | source)
XLA Modules:
  0.0 61.8 jit_solution(6566640206881154593)
XLA Ops:
  0.6 2.0 %prepare.1 = (bf16[8,48,512]{2,1,0:T(8,128)(2,1)}, bf16[384,256]{1,0:T(8,128)(2,1)S(1)}, bf16[256,256]{1,0:T(8,128)(2,1)S(1)}) custom-call(bf16[48,4096]{1,0:T(8,128)(2,1)} %grad_hbm.1, bf16[384,128]{1,0:T(8,128)(2,1)} %key_hbm.1, bf16[384,128]{1,0:T(8,128)(2,1)} %value_hbm.1), custom_call_target="tpu_custom_call" | custom-call | tf_op jit(solution)/shard_map/prepare/pallas_call | solution.py:302
  2.7 7.1 %all-to-all-start = ((bf16[8,48,512]{2,1,0:T(8,128)(2,1)}), bf16[8,48,512]{2,1,0:T(8,128)(2,1)S(1)}, u32[]{:S(2)}, u32[]{:S(2)}) async-start(bf16[8,48,512]{2,1,0:T(8,128)(2,1)} %get-tuple-element.19), calls=%async_computation | async-start | bytes 786432 | tf_op jit(solution)/shard_map/all_to_all | solution.py:297
  9.8 5.4 %collective-permute-start.1 = (bf16[384,256]{1,0:T(8,128)(2,1)S(1)}, bf16[384,256]{1,0:T(8,128)(2,1)S(1)}, u32[]{:S(2)}, u32[]{:S(2)}) collective-permute-start(bf16[384,256]{1,0:T(8,128)(2,1)S(1)} %later.1.own), channel_id=1, source_target_pairs={{0,16},{8,24},{16,32},{24,40},{32,48},{40,56},{48,64},{56,72},{64,... | collective-permute-start | bytes 589832 | tf_op jit(solution)/shard_map/ppermute | solution.py:260
  15.2 3.3 %collective-permute-start = (bf16[384,256]{1,0:T(8,128)(2,1)S(1)}, bf16[384,256]{1,0:T(8,128)(2,1)S(1)}, u32[]{:S(2)}, u32[]{:S(2)}) collective-permute-start(bf16[384,256]{1,0:T(8,128)(2,1)S(1)} %later.1.own), channel_id=1, source_target_pairs={{0,8},{8,16},{16,24},{24,32},{32,40},{40,48},{48,56},{56,64},{64,7... | collective-permute-start | bytes 589832 | tf_op jit(solution)/shard_map/ppermute | solution.py:260
  18.5 3.2 %collective-permute-start.2 = (bf16[256,256]{1,0:T(8,128)(2,1)S(1)}, bf16[256,256]{1,0:T(8,128)(2,1)S(1)}, u32[]{:S(2)}, u32[]{:S(2)}) collective-permute-start(bf16[256,256]{1,0:T(8,128)(2,1)S(1)} %get-tuple-element.21), channel_id=1, source_target_pairs={{0,24},{8,32},{16,40},{24,48},{32,56},{40,64},{48,72},{56,80},{64,... | collective-permute-start | bytes 393224 | tf_op jit(solution)/shard_map/ppermute | solution.py:260
  21.7 4.5 %collective-permute-done.2.far = bf16[256,256]{1,0:T(8,128)(2,1)S(1)} collective-permute-done((bf16[256,256]{1,0:T(8,128)(2,1)S(1)}, bf16[256,256]{1,0:T(8,128)(2,1)S(1)}, u32[]{:S(2)}, u32[]{:S(2)}) %collective-permute-start.2) | collective-permute-done | bytes 131104 | tf_op jit(solution)/shard_map/ppermute | solution.py:260
  26.3 0.0 collective-permute-done.1.mid
  26.3 0.0 collective-permute-done.near
  26.3 4.1 %forward.1 = (bf16[1536,128]{1,0:T(8,128)(2,1)S(1)}, bf16[1408,128]{1,0:T(8,128)(2,1)S(1)}, bf16[1408,128]{1,0:T(8,128)(2,1)S(1)}, bf16[384,512]{1,0:T(8,128)(2,...) custom-call(s32[3]{0:T(128)} %start_hbm.1, bf16[384,512]{1,0:T(8,128)(2,1)} %query_hbm.1, ...), custom_call_target="tpu_custom_call" | custom-call | flops 905969664 | bytes 8388608 | tf_op jit(solution)/shard_map/forward/pallas_call | solution.py:325
  30.4 0.0 all-to-all-done.chunks
  30.4 5.4 %backward.1 = (bf16[8,48,512]{2,1,0:T(8,128)(2,1)}, bf16[640,256]{1,0:T(8,128)(2,1)S(1)}, bf16[384,256]{1,0:T(8,128)(2,1)S(1)}, bf16[256,256]{1,0:T(8,128)(2,1)S(1)}, f32[384,256]{1,0:T(8,128)S(1)}) custom-call(bf16[8,48,512]{2,1,0:T(8,128)(2,1)S(1)} %all-to-all-done.chunks, bf16[1536,128]{1,0:T(8,128)(2,1)S(1)} %get-tuple-element.22.queries, ...), custom_call_target="tpu_custom_call" | custom-call | flops 2264924160 | bytes 8388608 | tf_op jit(solution)/shard_map/backward/pallas_call | solution.py:350
  35.8 1.9 %collective-permute-start.3 = (bf16[640,256]{1,0:T(8,128)(2,1)S(1)}, bf16[640,256]{1,0:T(8,128)(2,1)S(1)}, u32[]{:S(2)}, u32[]{:S(2)}) collective-permute-start(bf16[640,256]{1,0:T(8,128)(2,1)S(1)} %get-tuple-element.30), channel_id=1, source_target_pairs={{0,8},{8,0},{16,24},{24,16},{32,40},{40,32},{48,56},{56,48},{64,72... | collective-permute-start | bytes 983048 | tf_op jit(solution)/shard_map/ppermute | solution.py:264
  37.7 6.0 %all-to-all-start.1 = ((bf16[8,48,512]{2,1,0:T(8,128)(2,1)}), bf16[8,48,512]{2,1,0:T(8,128)(2,1)S(1)}, u32[]{:S(2)}, u32[]{:S(2)}) async-start(bf16[8,48,512]{2,1,0:T(8,128)(2,1)} %get-tuple-element.28), calls=%async_computation.1 | async-start | bytes 786432 | tf_op jit(solution)/shard_map/all_to_all | solution.py:297
  43.7 4.6 %collective-permute-start.4 = (bf16[256,256]{1,0:T(8,128)(2,1)S(1)}, bf16[256,256]{1,0:T(8,128)(2,1)S(1)}, u32[]{:S(2)}, u32[]{:S(2)}) collective-permute-start(bf16[256,256]{1,0:T(8,128)(2,1)S(1)} %get-tuple-element.31), channel_id=1, source_target_pairs={{32,8},{48,24},{64,40},{80,56},{96,72},{112,88},{128,104},{144,120... | collective-permute-start | bytes 393224 | tf_op jit(solution)/shard_map/ppermute | solution.py:260
  48.3 0.0 collective-permute-done.3.received
  48.3 0.1 merge.1
  48.4 2.6 %collective-permute-start.5 = (bf16[384,256]{1,0:T(8,128)(2,1)S(1)}, bf16[384,256]{1,0:T(8,128)(2,1)S(1)}, u32[]{:S(2)}, u32[]{:S(2)}) collective-permute-start(bf16[384,256]{1,0:T(8,128)(2,1)S(1)} %merge.1), channel_id=1, source_target_pairs={{16,0},{24,8},{32,16},{40,24},{48,32},{56,40},{64,48},{72,56},{80,... | collective-permute-start | bytes 589832 | tf_op jit(solution)/shard_map/ppermute | solution.py:260
  51.0 0.9 %collective-permute-done.4.apart = bf16[256,256]{1,0:T(8,128)(2,1)S(1)} collective-permute-done((bf16[256,256]{1,0:T(8,128)(2,1)S(1)}, bf16[256,256]{1,0:T(8,128)(2,1)S(1)}, u32[]{:S(2)}, u32[]{:S(2)}) %collective-permute-start.4) | collective-permute-done | bytes 131104 | tf_op jit(solution)/shard_map/ppermute | solution.py:260
  52.0 8.3 %collective-permute-done.5.shifted = bf16[384,256]{1,0:T(8,128)(2,1)S(1)} collective-permute-done((bf16[384,256]{1,0:T(8,128)(2,1)S(1)}, bf16[384,256]{1,0:T(8,128)(2,1)S(1)}, u32[]{:S(2)}, u32[]{:S(2)}) %collective-permute-start.5) | collective-permute-done | bytes 196640 | tf_op jit(solution)/shard_map/ppermute | solution.py:260
  60.3 0.7 %sum.1 = (bf16[384,128]{1,0:T(8,128)(2,1)}, bf16[384,128]{1,0:T(8,128)(2,1)}) custom-call(f32[384,256]{1,0:T(8,128)S(1)} %fold.1.folded, bf16[384,256]{1,0:T(8,128)(2,1)S(1)} %collective-permute-done.5.shifted), custom_call_target="tpu_custom_call" | custom-call | tf_op jit(solution)/shard_map/sum/pallas_call | solution.py:396
  61.0 0.0 all-to-all-done.1.chunks
  61.0 0.8 %place.1 = bf16[48,4096]{1,0:T(8,128)(2,1)} custom-call(bf16[8,48,512]{2,1,0:T(8,128)(2,1)S(1)} %all-to-all-done.1.chunks), custom_call_target="tpu_custom_call" | custom-call | tf_op jit(solution)/shard_map/place/pallas_call | solution.py:405
  (2 shorter events, 0.0 us)
Async XLA Ops:
  2.7 27.8 %all-to-all-start = ((bf16[8,48,512]{2,1,0:T(8,128)(2,1)}), bf16[8,48,512]{2,1,0:T(8,128)(2,1)S(1)}, u32[]{:S(2)}, u32[]{:S(2)}) async-start(bf16[8,48,512]{2,1,0:T(8,128)(2,1)} %get-tuple-element.19), calls=%async_computation | async-start | bytes 786432 | tf_op jit(solution)/shard_map/all_to_all | solution.py:297
  9.8 16.5 %collective-permute-start.1 = (bf16[384,256]{1,0:T(8,128)(2,1)S(1)}, bf16[384,256]{1,0:T(8,128)(2,1)S(1)}, u32[]{:S(2)}, u32[]{:S(2)}) collective-permute-start(bf16[384,256]{1,0:T(8,128)(2,1)S(1)} %later.1.own), channel_id=1, source_target_pairs={{0,16},{8,24},{16,32},{24,40},{32,48},{40,56},{48,64},{56,72},{64,... | collective-permute-start | bytes 589832 | tf_op jit(solution)/shard_map/ppermute | solution.py:260
  15.2 11.1 %collective-permute-start = (bf16[384,256]{1,0:T(8,128)(2,1)S(1)}, bf16[384,256]{1,0:T(8,128)(2,1)S(1)}, u32[]{:S(2)}, u32[]{:S(2)}) collective-permute-start(bf16[384,256]{1,0:T(8,128)(2,1)S(1)} %later.1.own), channel_id=1, source_target_pairs={{0,8},{8,16},{16,24},{24,32},{32,40},{40,48},{48,56},{56,64},{64,7... | collective-permute-start | bytes 589832 | tf_op jit(solution)/shard_map/ppermute | solution.py:260
  18.5 7.8 %collective-permute-start.2 = (bf16[256,256]{1,0:T(8,128)(2,1)S(1)}, bf16[256,256]{1,0:T(8,128)(2,1)S(1)}, u32[]{:S(2)}, u32[]{:S(2)}) collective-permute-start(bf16[256,256]{1,0:T(8,128)(2,1)S(1)} %get-tuple-element.21), channel_id=1, source_target_pairs={{0,24},{8,32},{16,40},{24,48},{32,56},{40,64},{48,72},{56,80},{64,... | collective-permute-start | bytes 393224 | tf_op jit(solution)/shard_map/ppermute | solution.py:260
  35.8 12.5 %collective-permute-start.3 = (bf16[640,256]{1,0:T(8,128)(2,1)S(1)}, bf16[640,256]{1,0:T(8,128)(2,1)S(1)}, u32[]{:S(2)}, u32[]{:S(2)}) collective-permute-start(bf16[640,256]{1,0:T(8,128)(2,1)S(1)} %get-tuple-element.30), channel_id=1, source_target_pairs={{0,8},{8,0},{16,24},{24,16},{32,40},{40,32},{48,56},{56,48},{64,72... | collective-permute-start | bytes 983048 | tf_op jit(solution)/shard_map/ppermute | solution.py:264
  37.7 23.3 %all-to-all-start.1 = ((bf16[8,48,512]{2,1,0:T(8,128)(2,1)}), bf16[8,48,512]{2,1,0:T(8,128)(2,1)S(1)}, u32[]{:S(2)}, u32[]{:S(2)}) async-start(bf16[8,48,512]{2,1,0:T(8,128)(2,1)} %get-tuple-element.28), calls=%async_computation.1 | async-start | bytes 786432 | tf_op jit(solution)/shard_map/all_to_all | solution.py:297
  43.7 8.2 %collective-permute-start.4 = (bf16[256,256]{1,0:T(8,128)(2,1)S(1)}, bf16[256,256]{1,0:T(8,128)(2,1)S(1)}, u32[]{:S(2)}, u32[]{:S(2)}) collective-permute-start(bf16[256,256]{1,0:T(8,128)(2,1)S(1)} %get-tuple-element.31), channel_id=1, source_target_pairs={{32,8},{48,24},{64,40},{80,56},{96,72},{112,88},{128,104},{144,120... | collective-permute-start | bytes 393224 | tf_op jit(solution)/shard_map/ppermute | solution.py:260
  48.4 11.9 %collective-permute-start.5 = (bf16[384,256]{1,0:T(8,128)(2,1)S(1)}, bf16[384,256]{1,0:T(8,128)(2,1)S(1)}, u32[]{:S(2)}, u32[]{:S(2)}) collective-permute-start(bf16[384,256]{1,0:T(8,128)(2,1)S(1)} %merge.1), channel_id=1, source_target_pairs={{16,0},{24,8},{32,16},{40,24},{48,32},{56,40},{64,48},{72,56},{80,... | collective-permute-start | bytes 589832 | tf_op jit(solution)/shard_map/ppermute | solution.py:260

commit v6 on v5

--- a/solution.py
+++ b/solution.py
@@ -62,17 +62,26 @@
     return pl.ds(pl.multiple_of(peer_at(position, parts) * WIDE, WIDE), WIDE)
 
 
-def prepare_kernel(grad_hbm, key_hbm, value_hbm, chunks, pair, tail, sems):
+def prepare_kernel(
+    start_hbm, query_hbm, grad_hbm, key_hbm, value_hbm,
+    chunks, pair, tail, query, starts, start_ref, sems
+):
     parts = chunks.shape[0]
     last = slice(SPAN - TAIL, SPAN)
-    moves = [(grad_hbm.at[:, peer_cols(p, parts)], chunks.at[p]) for p in range(parts)]
+    moves = [(start_hbm, start_ref)]
+    moves += [(grad_hbm.at[:, peer_cols(p, parts)], chunks.at[p]) for p in range(parts)]
     moves += [
         (key_hbm, pair.at[:, :HEAD]),
         (value_hbm, pair.at[:, HEAD:]),
         (key_hbm.at[last, :], tail.at[:, :HEAD]),
         (value_hbm.at[last, :], tail.at[:, HEAD:]),
+        (query_hbm, query),
     ]
-    finish(started(moves, sems))
+    copies = started(moves, sems)
+    finish(copies[:1])
+    for i in range(OWN):
+        starts[row8(i), :] = jnp.full((8, WIDE), start_ref[i], jnp.int32)
+    finish(copies[1:])
 
 
 def later_kernel(own, later):
@@ -98,50 +107,10 @@
     return slice(8 * i, 8 * i + 8)
 
 
-def forward_kernel(
-    start_hbm, query_hbm, own, near, mid, far,
-    queries, key_win, value_win, attended_ref, norm_ref, starts,
-    start_ref, query_ref, value_t, held, weights, sems
-):
-    arriving = started([(query_hbm, query_ref), (start_hbm, start_ref)], sems)
-    key_win[...] = window_of(0, far, mid, near, own)
-    turned_values = window_of(1, far, mid, near, own)
-    value_win[...] = turned_values
-    value_t[...] = turned_values.T
-    causal = causal_mask()
-    first = first_key()
-    finish(arriving)
-    for i in range(OWN):
-        stacked = heads_stacked(query_ref[block(i), :])
-        queries[block(i * GROUP, GROUP), :] = stacked
-        turned = stacked.T
-        start = start_ref[i]
-        starts[row8(i), :] = jnp.full((8, WIDE), start, jnp.int32)
-        best = jnp.full((8, WIDE), -jnp.inf, jnp.float32)
-        for j in range(REACH):
-            score = dot(key_win[block(i + j), :], turned, NN)
-            allowed = causal if j == REACH - 1 else first + (i + j) * BLOCK >= start
-            score = jnp.where(allowed, score, -jnp.inf)
-            held[block(j), :] = score
-            best = jnp.maximum(best, jnp.max(score.reshape(BLOCK // 8, 8, WIDE), axis=0))
-        best = jnp.max(best, axis=0, keepdims=True)
-        total = jnp.zeros((8, WIDE), jnp.float32)
-        for j in range(REACH):
-            part = jnp.exp2((held[block(j), :] - best) * TO_EXP2)
-            total = total + jnp.sum(part.reshape(BLOCK // 8, 8, WIDE), axis=0)
-            weights[block(i * REACH + j), :] = part.astype(jnp.bfloat16)
-        total = jnp.sum(total, axis=0, keepdims=True)
-        norm_ref[row8(i), :] = jnp.broadcast_to(best * TO_EXP2 + jnp.log2(total), (8, WIDE))
-        attended_ref[block(i), :] = (
-            dot(value_t[:, block(i, REACH)], weights[block(i * REACH, REACH), :], NN)
-            * (1.0 / total)
-        ).astype(jnp.bfloat16)
-
-
-def backward_kernel(
-    chunks, queries, key_win, value_win, attended_ref, norm_ref, starts,
+def attention_kernel(
+    chunks, query_ref, starts, own, near, mid, far,
     dchunks, dnear_far, dmid, dfar, down,
-    key_t, grad_ref, weights, held, dkey, dvalue, dquery
+    key_win, value_win, value_t, key_t, scores, grad_ref, weights, held, dkey, dvalue, dquery
 ):
     parts, share = chunks.shape[0], chunks.shape[1]
 
@@ -150,39 +119,60 @@
 
     for p in range(parts):
         grad_ref[share_rows(p), :] = chunks[p]
-    key_t[...] = key_win[...].T
+    keys = window_of(0, far, mid, near, own)
+    key_win[...] = keys
+    key_t[...] = keys.T
+    values = window_of(1, far, mid, near, own)
+    value_win[...] = values
+    value_t[...] = values.T
     causal = causal_mask()
     first = first_key()
     on_diagonal = lax.broadcasted_iota(jnp.int32, (BLOCK, BLOCK), 0) == lax.broadcasted_iota(
         jnp.int32, (BLOCK, BLOCK), 1
     )
     for i in range(OWN):
-        grads = heads_stacked(grad_ref[block(i), :])
+        mine = block(i * REACH, REACH)
+        queries = heads_stacked(query_ref[block(i), :])
+        queries_t = queries.T
+        start = starts[8 * i : 8 * i + 1, :]
+        best = jnp.full((8, WIDE), -jnp.inf, jnp.float32)
+        for j in range(REACH):
+            score = dot(key_win[block(i + j), :], queries_t, NN)
+            allowed = causal if j == REACH - 1 else first + (i + j) * BLOCK >= start
+            score = jnp.where(allowed, score, -jnp.inf)
+            scores[block(i * REACH + j), :] = score
+            best = jnp.maximum(best, jnp.max(score.reshape(BLOCK // 8, 8, WIDE), axis=0))
+        best = jnp.max(best, axis=0, keepdims=True)
+        total = jnp.zeros((8, WIDE), jnp.float32)
+        for j in range(REACH):
+            part = jnp.exp2((scores[block(i * REACH + j), :] - best) * TO_EXP2)
+            total = total + jnp.sum(part.reshape(BLOCK // 8, 8, WIDE), axis=0)
+            weights[block(i * REACH + j), :] = part.astype(jnp.bfloat16)
+        inverse = 1.0 / jnp.sum(total, axis=0, keepdims=True)
+        attended = (
+            dot(value_t[:, block(i, REACH)], weights[mine, :], NN) * inverse
+        ).astype(jnp.bfloat16)
+        per_row = jnp.concatenate(
+            [jnp.broadcast_to(inverse[:, block(h)], (BLOCK, BLOCK)).T for h in range(GROUP)], axis=0
+        )
+        grads = (heads_stacked(grad_ref[block(i), :]).astype(jnp.float32) * per_row).astype(
+            jnp.bfloat16
+        )
         grads_t = grads.T
-        queries_t = queries[block(i * GROUP, GROUP), :].T
         deltas = []
         for h in range(GROUP):
-            cross = dot(grads[block(h), :], attended_ref[block(i), block(h)], NN)
+            cross = dot(grads[block(h), :], attended[:, block(h)], NN)
             deltas.append(jnp.sum(jnp.where(on_diagonal, cross, 0.0), axis=0, keepdims=True))
         delta = jnp.concatenate(deltas, axis=1)
-        norm = norm_ref[8 * i : 8 * i + 1, :]
-        start = starts[8 * i : 8 * i + 1, :]
         for j in range(REACH):
-            score = dot(key_win[block(i + j), :], queries_t, NN)
-            if j == REACH - 1:
-                weight = jnp.where(causal, jnp.exp2(score * TO_EXP2 - norm), 0.0)
-            else:
-                allowed = first + (i + j) * BLOCK >= start
-                weight = jnp.exp2(score * TO_EXP2 - jnp.where(allowed, norm, jnp.inf))
             dweight = dot(value_win[block(i + j), :], grads_t, NN)
-            weights[block(i * REACH + j), :] = weight.astype(jnp.bfloat16)
+            weight = weights[block(i * REACH + j), :].astype(jnp.float32)
             held[block(i * REACH + j), :] = (weight * (dweight - delta)).astype(jnp.bfloat16)
-        mine = block(i * REACH, REACH)
         turned = dot(key_t[:, block(i, REACH)], held[mine, :], NN) * INV_ROOT
         for h in range(GROUP):
             dquery[block(i), block(h)] = turned[:, block(h)].T.astype(jnp.bfloat16)
         value_part = dot(weights[mine, :], grads, NN)
-        key_part = dot(held[mine, :], queries[block(i * GROUP, GROUP), :], NN)
+        key_part = dot(held[mine, :], queries, NN)
         fresh = 0 if i == 0 else REACH - 1
         if fresh:
             seen = slice(0, fresh * BLOCK)
@@ -298,16 +288,17 @@
             value, ("ctx", "kvh"), split_axis=0, concat_axis=0, axis_index_groups=rings, tiled=True
         )
 
-    start_hbm, query_hbm = pinned(doc_start, query_states)
-    chunks, own, last = pl.pallas_call(
+    chunks, own, last, queries, starts = pl.pallas_call(
         prepare_kernel,
-        out_shape=(chunked, pair, tail),
-        in_specs=[HBM] * 3,
-        out_specs=(VMEM,) * 3,
-        scratch_shapes=[dma((parts + 4,))],
+        out_shape=(
+            chunked, pair, tail, sds((SPAN, WIDE), bf16), sds((8 * OWN, WIDE), jnp.int32)
+        ),
+        in_specs=[HBM] * 5,
+        out_specs=(VMEM,) * 5,
+        scratch_shapes=[pltpu.SMEM(doc_start.shape, jnp.int32), dma((parts + 6,))],
         compiler_params=params(4),
         name="prepare",
-    )(*pinned(grad_output, key_states, value_states))
+    )(*pinned(doc_start, query_states, grad_output, key_states, value_states))
     grads = exchanged(chunks)
     far = passed_along(last, 3)
     own = pl.pallas_call(
@@ -322,33 +313,8 @@
     mid = passed_along(own, 2)
     near = passed_along(own, 1)
 
-    kept = pl.pallas_call(
-        forward_kernel,
-        out_shape=(
-            sds((OWN * WIDE, HEAD), bf16),
-            sds((window, HEAD), bf16),
-            sds((window, HEAD), bf16),
-            sds((OWN * HEAD, WIDE), bf16),
-            sds((8 * OWN, WIDE), f32),
-            sds((8 * OWN, WIDE), jnp.int32),
-        ),
-        in_specs=[HBM, HBM] + [VMEM] * 4,
-        out_specs=(VMEM,) * 6,
-        scratch_shapes=[
-            pltpu.SMEM(doc_start.shape, jnp.int32),
-            pltpu.VMEM((SPAN, WIDE), bf16),
-            pltpu.VMEM((HEAD, window), bf16),
-            pltpu.VMEM((REACH * BLOCK, WIDE), f32),
-            pltpu.VMEM((pairs * BLOCK, WIDE), bf16),
-            dma((2,)),
-        ],
-        cost_estimate=cost(2 * flops, pairs * BLOCK * WIDE),
-        compiler_params=params(16),
-        name="forward",
-    )(start_hbm, query_hbm, own, near, mid, far)
-
     dchunks, dnear_far, dmid, dfar, down = pl.pallas_call(
-        backward_kernel,
+        attention_kernel,
         out_shape=(
             chunked,
             sds((SPAN + TAIL, 2 * HEAD), bf16),
@@ -359,7 +325,11 @@
         in_specs=[VMEM] * 7,
         out_specs=(VMEM,) * 5,
         scratch_shapes=[
+            pltpu.VMEM((window, HEAD), bf16),
+            pltpu.VMEM((window, HEAD), bf16),
             pltpu.VMEM((HEAD, window), bf16),
+            pltpu.VMEM((HEAD, window), bf16),
+            pltpu.VMEM((pairs * BLOCK, WIDE), f32),
             pltpu.VMEM((SPAN, WIDE), bf16),
             pltpu.VMEM((pairs * BLOCK, WIDE), bf16),
             pltpu.VMEM((pairs * BLOCK, WIDE), bf16),
@@ -367,10 +337,10 @@
             pltpu.VMEM((window, HEAD), f32),
             pltpu.VMEM((SPAN, WIDE), bf16),
         ],
-        cost_estimate=cost(5 * flops, pairs * BLOCK * WIDE),
-        compiler_params=params(24),
-        name="backward",
-    )(grads, *kept)
+        cost_estimate=cost(6 * flops, pairs * BLOCK * WIDE),
+        compiler_params=params(36),
+        name="attention",
+    )(grads, queries, starts, own, near, mid, far)
 
     back = exchanged(dchunks)
     received = core_swapped(dnear_far)

time: 62.3 us -> 61.2 us (0.982)
  Pallas kernels: 13.2 us -> 12.1 us
    pallas_call x3 -> x2, Pallas kernels: 11.5 us -> 10.4 us  [the longest x1 8.17 us: body(): pl.pallas_call(attention_kernel, out_shape=(chunked, sds((SPAN + TAIL, 2...]
  transfers between devices with their start and end apart: 8 -> 8, of which waited for: 3 -> 3; matrix products, arithmetic and copies ran while one was open for 0% -> 0% of each run, Pallas kernels for 8% -> 1%
where the time goes in v6:
time: 61.2 us; the launch traced here: 60.7 us
  starting transfers between devices  34.1 us (56%)
  waiting for transfers between devices  13.8 us (23%)
  Pallas kernels  12.1 us (20%)
  between operations  0.73 us (1%)
    ppermute x5, starting transfers between devices, passed_along(): return lax.ppermute(value, 'ctx', pairs)  19.1 us
    ppermute x5, waiting for transfers between devices, passed_along(): return lax.ppermute(value, 'ctx', pairs)  13.8 us
    all_to_all x2, starting transfers between devices, exchanged(): lax.all_to_all(value, ('ctx', 'kvh'), split_axis=0, concat_axis=0, axis_i...  13.1 us
    pallas_call x1, Pallas kernels, body(): pl.pallas_call(attention_kernel, out_shape=(chunked, sds((SPAN + TAIL, 2...  8.17 us
    pallas_call x1, Pallas kernels, body(): pl.pallas_call(prepare_kernel, out_shape=(chunked, pair, tail, sds((SPAN,...  2.24 us
    ppermute x1, starting transfers between devices, core_swapped(): lax.ppermute(value, 'ctx', [(i, i ^ 1) for i in range(lax.axis_size('ctx'...  1.91 us
  transfers between devices with their start and end apart: 8, of which 3 were waited for; matrix products, arithmetic and copies ran while one was open for 0% of the time, Pallas kernels for 1%

profile of v6, /device:TPU:198, one launch (start us, length us, event | category | flops | bytes accessed | tf_op | source)
XLA Modules:
  0.0 60.7 jit_solution(17320531470260291334)
XLA Ops:
  0.6 2.2 %prepare.1 = (bf16[8,48,512]{2,1,0:T(8,128)(2,1)}, bf16[384,256]{1,0:T(8,128)(2,1)S(1)}, bf16[256,256]{1,0:T(8,128)(2,1)S(1)}, bf16[384,512]{1,0:T(8,128)(2,1)S(1)}, s32[24,512]{1,0:T(8,128)S(1)}) custom-call(s32[3]{0:T(128)} %start_hbm.1, bf16[384,512]{1,0:T(8,128)(2,1)} %query_hbm.1, bf16[48,4096]{1,0:T(8,128)(2,1)} %grad_hbm.1, bf16[384,128]{1,0:T(8,128)(2,1)} %key_hbm.1, ...), custom_call_target="tpu_custom_call" | custom-call | tf_op jit(solution)/shard_map/prepare/pallas_call | solution.py:291
  2.9 7.1 %all-to-all-start = ((bf16[8,48,512]{2,1,0:T(8,128)(2,1)}), bf16[8,48,512]{2,1,0:T(8,128)(2,1)S(1)}, u32[]{:S(2)}, u32[]{:S(2)}) async-start(bf16[8,48,512]{2,1,0:T(8,128)(2,1)} %get-tuple-element.15), calls=%async_computation | async-start | bytes 786432 | tf_op jit(solution)/shard_map/all_to_all | solution.py:287
  10.0 5.4 %collective-permute-start.1 = (bf16[384,256]{1,0:T(8,128)(2,1)S(1)}, bf16[384,256]{1,0:T(8,128)(2,1)S(1)}, u32[]{:S(2)}, u32[]{:S(2)}) collective-permute-start(bf16[384,256]{1,0:T(8,128)(2,1)S(1)} %later.1.own), channel_id=1, source_target_pairs={{0,16},{8,24},{16,32},{24,40},{32,48},{40,56},{48,64},{56,72},{64,... | collective-permute-start | bytes 589832 | tf_op jit(solution)/shard_map/ppermute | solution.py:250
  15.4 3.3 %collective-permute-start = (bf16[384,256]{1,0:T(8,128)(2,1)S(1)}, bf16[384,256]{1,0:T(8,128)(2,1)S(1)}, u32[]{:S(2)}, u32[]{:S(2)}) collective-permute-start(bf16[384,256]{1,0:T(8,128)(2,1)S(1)} %later.1.own), channel_id=1, source_target_pairs={{0,8},{8,16},{16,24},{24,32},{32,40},{40,48},{48,56},{56,64},{64,7... | collective-permute-start | bytes 589832 | tf_op jit(solution)/shard_map/ppermute | solution.py:250
  18.7 3.2 %collective-permute-start.2 = (bf16[256,256]{1,0:T(8,128)(2,1)S(1)}, bf16[256,256]{1,0:T(8,128)(2,1)S(1)}, u32[]{:S(2)}, u32[]{:S(2)}) collective-permute-start(bf16[256,256]{1,0:T(8,128)(2,1)S(1)} %get-tuple-element.19), channel_id=1, source_target_pairs={{0,24},{8,32},{16,40},{24,48},{32,56},{40,64},{48,72},{56,80},{64,... | collective-permute-start | bytes 393224 | tf_op jit(solution)/shard_map/ppermute | solution.py:250
  22.0 4.5 %collective-permute-done.2.far = bf16[256,256]{1,0:T(8,128)(2,1)S(1)} collective-permute-done((bf16[256,256]{1,0:T(8,128)(2,1)S(1)}, bf16[256,256]{1,0:T(8,128)(2,1)S(1)}, u32[]{:S(2)}, u32[]{:S(2)}) %collective-permute-start.2) | collective-permute-done | bytes 131104 | tf_op jit(solution)/shard_map/ppermute | solution.py:250
  26.5 0.0 collective-permute-done.1.mid
  26.5 0.0 collective-permute-done.near
  26.5 0.0 all-to-all-done.chunks
  26.5 8.2 %attention.1 = (bf16[8,48,512]{2,1,0:T(8,128)(2,1)}, bf16[640,256]{1,0:T(8,128)(2,1)S(1)}, bf16[384,256]{1,0:T(8,128)(2,1)S(1)}, bf16[256,256]{1,0:T(8,128)(2,1)S(1)}, f32[384,256]{1,0:T(8,128)S(1)}) custom-call(bf16[8,48,512]{2,1,0:T(8,128)(2,1)S(1)} %all-to-all-done.chunks, bf16[384,512]{1,0:T(8,128)(2,1)S(1)} %get-tuple-element.16.query_ref, ...), custom_call_target="tpu_custom_call" | custom-call | flops 2717908992 | bytes 8388608 | tf_op jit(solution)/shard_map/attention/pallas_call | solution.py:316
  34.7 1.9 %collective-permute-start.3 = (bf16[640,256]{1,0:T(8,128)(2,1)S(1)}, bf16[640,256]{1,0:T(8,128)(2,1)S(1)}, u32[]{:S(2)}, u32[]{:S(2)}) collective-permute-start(bf16[640,256]{1,0:T(8,128)(2,1)S(1)} %get-tuple-element.22), channel_id=1, source_target_pairs={{0,8},{8,0},{16,24},{24,16},{32,40},{40,32},{48,56},{56,48},{64,72... | collective-permute-start | bytes 983048 | tf_op jit(solution)/shard_map/ppermute | solution.py:254
  36.6 6.0 %all-to-all-start.1 = ((bf16[8,48,512]{2,1,0:T(8,128)(2,1)}), bf16[8,48,512]{2,1,0:T(8,128)(2,1)S(1)}, u32[]{:S(2)}, u32[]{:S(2)}) async-start(bf16[8,48,512]{2,1,0:T(8,128)(2,1)} %get-tuple-element.20), calls=%async_computation.1 | async-start | bytes 786432 | tf_op jit(solution)/shard_map/all_to_all | solution.py:287
  42.6 4.6 %collective-permute-start.4 = (bf16[256,256]{1,0:T(8,128)(2,1)S(1)}, bf16[256,256]{1,0:T(8,128)(2,1)S(1)}, u32[]{:S(2)}, u32[]{:S(2)}) collective-permute-start(bf16[256,256]{1,0:T(8,128)(2,1)S(1)} %get-tuple-element.23), channel_id=1, source_target_pairs={{32,8},{48,24},{64,40},{80,56},{96,72},{112,88},{128,104},{144,120... | collective-permute-start | bytes 393224 | tf_op jit(solution)/shard_map/ppermute | solution.py:250
  47.2 0.0 collective-permute-done.3.received
  47.2 0.1 merge.1
  47.2 2.6 %collective-permute-start.5 = (bf16[384,256]{1,0:T(8,128)(2,1)S(1)}, bf16[384,256]{1,0:T(8,128)(2,1)S(1)}, u32[]{:S(2)}, u32[]{:S(2)}) collective-permute-start(bf16[384,256]{1,0:T(8,128)(2,1)S(1)} %merge.1), channel_id=1, source_target_pairs={{16,0},{24,8},{32,16},{40,24},{48,32},{56,40},{64,48},{72,56},{80,... | collective-permute-start | bytes 589832 | tf_op jit(solution)/shard_map/ppermute | solution.py:250
  49.9 0.9 %collective-permute-done.4.apart = bf16[256,256]{1,0:T(8,128)(2,1)S(1)} collective-permute-done((bf16[256,256]{1,0:T(8,128)(2,1)S(1)}, bf16[256,256]{1,0:T(8,128)(2,1)S(1)}, u32[]{:S(2)}, u32[]{:S(2)}) %collective-permute-start.4) | collective-permute-done | bytes 131104 | tf_op jit(solution)/shard_map/ppermute | solution.py:250
  50.8 8.3 %collective-permute-done.5.shifted = bf16[384,256]{1,0:T(8,128)(2,1)S(1)} collective-permute-done((bf16[384,256]{1,0:T(8,128)(2,1)S(1)}, bf16[384,256]{1,0:T(8,128)(2,1)S(1)}, u32[]{:S(2)}, u32[]{:S(2)}) %collective-permute-start.5) | collective-permute-done | bytes 196640 | tf_op jit(solution)/shard_map/ppermute | solution.py:250
  59.1 0.7 %sum.1 = (bf16[384,128]{1,0:T(8,128)(2,1)}, bf16[384,128]{1,0:T(8,128)(2,1)}) custom-call(f32[384,256]{1,0:T(8,128)S(1)} %fold.1.folded, bf16[384,256]{1,0:T(8,128)(2,1)S(1)} %collective-permute-done.5.shifted), custom_call_target="tpu_custom_call" | custom-call | tf_op jit(solution)/shard_map/sum/pallas_call | solution.py:366
  59.9 0.0 all-to-all-done.1.chunks
  59.9 0.8 %place.1 = bf16[48,4096]{1,0:T(8,128)(2,1)} custom-call(bf16[8,48,512]{2,1,0:T(8,128)(2,1)S(1)} %all-to-all-done.1.chunks), custom_call_target="tpu_custom_call" | custom-call | tf_op jit(solution)/shard_map/place/pallas_call | solution.py:375
  (2 shorter events, 0.0 us)
Async XLA Ops:
  2.9 23.6 %all-to-all-start = ((bf16[8,48,512]{2,1,0:T(8,128)(2,1)}), bf16[8,48,512]{2,1,0:T(8,128)(2,1)S(1)}, u32[]{:S(2)}, u32[]{:S(2)}) async-start(bf16[8,48,512]{2,1,0:T(8,128)(2,1)} %get-tuple-element.15), calls=%async_computation | async-start | bytes 786432 | tf_op jit(solution)/shard_map/all_to_all | solution.py:287
  10.0 16.5 %collective-permute-start.1 = (bf16[384,256]{1,0:T(8,128)(2,1)S(1)}, bf16[384,256]{1,0:T(8,128)(2,1)S(1)}, u32[]{:S(2)}, u32[]{:S(2)}) collective-permute-start(bf16[384,256]{1,0:T(8,128)(2,1)S(1)} %later.1.own), channel_id=1, source_target_pairs={{0,16},{8,24},{16,32},{24,40},{32,48},{40,56},{48,64},{56,72},{64,... | collective-permute-start | bytes 589832 | tf_op jit(solution)/shard_map/ppermute | solution.py:250
  15.4 11.1 %collective-permute-start = (bf16[384,256]{1,0:T(8,128)(2,1)S(1)}, bf16[384,256]{1,0:T(8,128)(2,1)S(1)}, u32[]{:S(2)}, u32[]{:S(2)}) collective-permute-start(bf16[384,256]{1,0:T(8,128)(2,1)S(1)} %later.1.own), channel_id=1, source_target_pairs={{0,8},{8,16},{16,24},{24,32},{32,40},{40,48},{48,56},{56,64},{64,7... | collective-permute-start | bytes 589832 | tf_op jit(solution)/shard_map/ppermute | solution.py:250
  18.7 7.8 %collective-permute-start.2 = (bf16[256,256]{1,0:T(8,128)(2,1)S(1)}, bf16[256,256]{1,0:T(8,128)(2,1)S(1)}, u32[]{:S(2)}, u32[]{:S(2)}) collective-permute-start(bf16[256,256]{1,0:T(8,128)(2,1)S(1)} %get-tuple-element.19), channel_id=1, source_target_pairs={{0,24},{8,32},{16,40},{24,48},{32,56},{40,64},{48,72},{56,80},{64,... | collective-permute-start | bytes 393224 | tf_op jit(solution)/shard_map/ppermute | solution.py:250
  34.7 12.5 %collective-permute-start.3 = (bf16[640,256]{1,0:T(8,128)(2,1)S(1)}, bf16[640,256]{1,0:T(8,128)(2,1)S(1)}, u32[]{:S(2)}, u32[]{:S(2)}) collective-permute-start(bf16[640,256]{1,0:T(8,128)(2,1)S(1)} %get-tuple-element.22), channel_id=1, source_target_pairs={{0,8},{8,0},{16,24},{24,16},{32,40},{40,32},{48,56},{56,48},{64,72... | collective-permute-start | bytes 983048 | tf_op jit(solution)/shard_map/ppermute | solution.py:254
  36.6 23.3 %all-to-all-start.1 = ((bf16[8,48,512]{2,1,0:T(8,128)(2,1)}), bf16[8,48,512]{2,1,0:T(8,128)(2,1)S(1)}, u32[]{:S(2)}, u32[]{:S(2)}) async-start(bf16[8,48,512]{2,1,0:T(8,128)(2,1)} %get-tuple-element.20), calls=%async_computation.1 | async-start | bytes 786432 | tf_op jit(solution)/shard_map/all_to_all | solution.py:287
  42.6 8.2 %collective-permute-start.4 = (bf16[256,256]{1,0:T(8,128)(2,1)S(1)}, bf16[256,256]{1,0:T(8,128)(2,1)S(1)}, u32[]{:S(2)}, u32[]{:S(2)}) collective-permute-start(bf16[256,256]{1,0:T(8,128)(2,1)S(1)} %get-tuple-element.23), channel_id=1, source_target_pairs={{32,8},{48,24},{64,40},{80,56},{96,72},{112,88},{128,104},{144,120... | collective-permute-start | bytes 393224 | tf_op jit(solution)/shard_map/ppermute | solution.py:250
  47.2 11.9 %collective-permute-start.5 = (bf16[384,256]{1,0:T(8,128)(2,1)S(1)}, bf16[384,256]{1,0:T(8,128)(2,1)S(1)}, u32[]{:S(2)}, u32[]{:S(2)}) collective-permute-start(bf16[384,256]{1,0:T(8,128)(2,1)S(1)} %merge.1), channel_id=1, source_target_pairs={{16,0},{24,8},{32,16},{40,24},{48,32},{56,40},{64,48},{72,56},{80,... | collective-permute-start | bytes 589832 | tf_op jit(solution)/shard_map/ppermute | solution.py:250

commit v7 on v6

--- a/solution.py
+++ b/solution.py
@@ -51,7 +51,7 @@
 
 
 def peer_at(position, parts):
-    return lax.rem(position + lax.rem(lax.axis_index("ctx"), 2) * (parts // 2), parts)
+    return lax.rem(position + lax.rem(lax.axis_index("ctx"), 2) * (parts // 4), parts)
 
 
 def on_odd_core():
@@ -279,7 +279,7 @@
     pair = sds((SPAN, 2 * HEAD), bf16)
     tail = sds((TAIL, 2 * HEAD), bf16)
     rings = [
-        [c * parts + (p + (c % 2) * (parts // 2)) % parts for p in range(parts)]
+        [c * parts + (p + (c % 2) * (parts // 4)) % parts for p in range(parts)]
         for c in range(length)
     ]
 

time: 61.2 us -> 59.4 us (0.971)
  waiting for transfers between devices: 13.8 us -> 12.5 us
    ppermute x5, starting transfers between devices: 19.1 us -> 17.3 us  [passed_along(): return lax.ppermute(value, 'ctx', pairs)]
    ppermute x5, waiting for transfers between devices: 13.8 us -> 12.4 us  [passed_along(): return lax.ppermute(value, 'ctx', pairs)]
    all_to_all x2, starting transfers between devices: 13.1 us -> 14.3 us  [exchanged(): lax.all_to_all(value, ('ctx', 'kvh'), split_axis=0, concat_axis=0, axis_i...]
where the time goes in v7:
time: 59.4 us; the launch traced here: 58.9 us
  starting transfers between devices  33.7 us (57%)
  waiting for transfers between devices  12.5 us (21%)
  Pallas kernels  12.1 us (20%)
  between operations  0.73 us (1%)
    ppermute x5, starting transfers between devices, passed_along(): return lax.ppermute(value, 'ctx', pairs)  17.3 us
    all_to_all x2, starting transfers between devices, exchanged(): lax.all_to_all(value, ('ctx', 'kvh'), split_axis=0, concat_axis=0, axis_i...  14.3 us
    ppermute x5, waiting for transfers between devices, passed_along(): return lax.ppermute(value, 'ctx', pairs)  12.4 us
    pallas_call x1, Pallas kernels, body(): pl.pallas_call(attention_kernel, out_shape=(chunked, sds((SPAN + TAIL, 2...  8.16 us
    pallas_call x1, Pallas kernels, body(): pl.pallas_call(prepare_kernel, out_shape=(chunked, pair, tail, sds((SPAN,...  2.24 us
    ppermute x1, starting transfers between devices, core_swapped(): lax.ppermute(value, 'ctx', [(i, i ^ 1) for i in range(lax.axis_size('ctx'...  2.02 us
  transfers between devices with their start and end apart: 8, of which 3 were waited for; matrix products, arithmetic and copies ran while one was open for 0% of the time, Pallas kernels for 1%

profile of v7, /device:TPU:198, one launch (start us, length us, event | category | flops | bytes accessed | tf_op | source)
XLA Modules:
  0.0 58.9 jit_solution(4147488338097360246)
XLA Ops:
  0.6 2.2 %prepare.1 = (bf16[8,48,512]{2,1,0:T(8,128)(2,1)}, bf16[384,256]{1,0:T(8,128)(2,1)S(1)}, bf16[256,256]{1,0:T(8,128)(2,1)S(1)}, bf16[384,512]{1,0:T(8,128)(2,1)S(1)}, s32[24,512]{1,0:T(8,128)S(1)}) custom-call(s32[3]{0:T(128)} %start_hbm.1, bf16[384,512]{1,0:T(8,128)(2,1)} %query_hbm.1, bf16[48,4096]{1,0:T(8,128)(2,1)} %grad_hbm.1, bf16[384,128]{1,0:T(8,128)(2,1)} %key_hbm.1, ...), custom_call_target="tpu_custom_call" | custom-call | tf_op jit(solution)/shard_map/prepare/pallas_call | solution.py:291
  2.9 7.1 %all-to-all-start = ((bf16[8,48,512]{2,1,0:T(8,128)(2,1)}), bf16[8,48,512]{2,1,0:T(8,128)(2,1)S(1)}, u32[]{:S(2)}, u32[]{:S(2)}) async-start(bf16[8,48,512]{2,1,0:T(8,128)(2,1)} %get-tuple-element.15), calls=%async_computation | async-start | bytes 786432 | tf_op jit(solution)/shard_map/all_to_all | solution.py:287
  10.0 5.4 %collective-permute-start.1 = (bf16[384,256]{1,0:T(8,128)(2,1)S(1)}, bf16[384,256]{1,0:T(8,128)(2,1)S(1)}, u32[]{:S(2)}, u32[]{:S(2)}) collective-permute-start(bf16[384,256]{1,0:T(8,128)(2,1)S(1)} %later.1.own), channel_id=1, source_target_pairs={{0,16},{8,24},{16,32},{24,40},{32,48},{40,56},{48,64},{56,72},{64,... | collective-permute-start | bytes 589832 | tf_op jit(solution)/shard_map/ppermute | solution.py:250
  15.4 1.9 %collective-permute-start = (bf16[384,256]{1,0:T(8,128)(2,1)S(1)}, bf16[384,256]{1,0:T(8,128)(2,1)S(1)}, u32[]{:S(2)}, u32[]{:S(2)}) collective-permute-start(bf16[384,256]{1,0:T(8,128)(2,1)S(1)} %later.1.own), channel_id=1, source_target_pairs={{0,8},{8,16},{16,24},{24,32},{32,40},{40,48},{48,56},{56,64},{64,7... | collective-permute-start | bytes 589832 | tf_op jit(solution)/shard_map/ppermute | solution.py:250
  17.4 4.6 %collective-permute-start.2 = (bf16[256,256]{1,0:T(8,128)(2,1)S(1)}, bf16[256,256]{1,0:T(8,128)(2,1)S(1)}, u32[]{:S(2)}, u32[]{:S(2)}) collective-permute-start(bf16[256,256]{1,0:T(8,128)(2,1)S(1)} %get-tuple-element.19), channel_id=1, source_target_pairs={{0,24},{8,32},{16,40},{24,48},{32,56},{40,64},{48,72},{56,80},{64,... | collective-permute-start | bytes 393224 | tf_op jit(solution)/shard_map/ppermute | solution.py:250
  22.0 3.2 %collective-permute-done.2.far = bf16[256,256]{1,0:T(8,128)(2,1)S(1)} collective-permute-done((bf16[256,256]{1,0:T(8,128)(2,1)S(1)}, bf16[256,256]{1,0:T(8,128)(2,1)S(1)}, u32[]{:S(2)}, u32[]{:S(2)}) %collective-permute-start.2) | collective-permute-done | bytes 131104 | tf_op jit(solution)/shard_map/ppermute | solution.py:250
  25.1 0.0 collective-permute-done.1.mid
  25.1 0.0 collective-permute-done.near
  25.1 0.0 all-to-all-done.chunks
  25.2 8.2 %attention.1 = (bf16[8,48,512]{2,1,0:T(8,128)(2,1)}, bf16[640,256]{1,0:T(8,128)(2,1)S(1)}, bf16[384,256]{1,0:T(8,128)(2,1)S(1)}, bf16[256,256]{1,0:T(8,128)(2,1)S(1)}, f32[384,256]{1,0:T(8,128)S(1)}) custom-call(bf16[8,48,512]{2,1,0:T(8,128)(2,1)S(1)} %all-to-all-done.chunks, bf16[384,512]{1,0:T(8,128)(2,1)S(1)} %get-tuple-element.16.query_ref, ...), custom_call_target="tpu_custom_call" | custom-call | flops 2717908992 | bytes 8388608 | tf_op jit(solution)/shard_map/attention/pallas_call | solution.py:316
  33.3 2.0 %collective-permute-start.3 = (bf16[640,256]{1,0:T(8,128)(2,1)S(1)}, bf16[640,256]{1,0:T(8,128)(2,1)S(1)}, u32[]{:S(2)}, u32[]{:S(2)}) collective-permute-start(bf16[640,256]{1,0:T(8,128)(2,1)S(1)} %get-tuple-element.22), channel_id=1, source_target_pairs={{0,8},{8,0},{16,24},{24,16},{32,40},{40,32},{48,56},{56,48},{64,72... | collective-permute-start | bytes 983048 | tf_op jit(solution)/shard_map/ppermute | solution.py:254
  35.4 7.2 %all-to-all-start.1 = ((bf16[8,48,512]{2,1,0:T(8,128)(2,1)}), bf16[8,48,512]{2,1,0:T(8,128)(2,1)S(1)}, u32[]{:S(2)}, u32[]{:S(2)}) async-start(bf16[8,48,512]{2,1,0:T(8,128)(2,1)} %get-tuple-element.20), calls=%async_computation.1 | async-start | bytes 786432 | tf_op jit(solution)/shard_map/all_to_all | solution.py:287
  42.6 2.8 %collective-permute-start.4 = (bf16[256,256]{1,0:T(8,128)(2,1)S(1)}, bf16[256,256]{1,0:T(8,128)(2,1)S(1)}, u32[]{:S(2)}, u32[]{:S(2)}) collective-permute-start(bf16[256,256]{1,0:T(8,128)(2,1)S(1)} %get-tuple-element.23), channel_id=1, source_target_pairs={{32,8},{48,24},{64,40},{80,56},{96,72},{112,88},{128,104},{144,120... | collective-permute-start | bytes 393224 | tf_op jit(solution)/shard_map/ppermute | solution.py:250
  45.4 0.0 collective-permute-done.3.received
  45.4 0.1 merge.1
  45.4 2.6 %collective-permute-start.5 = (bf16[384,256]{1,0:T(8,128)(2,1)S(1)}, bf16[384,256]{1,0:T(8,128)(2,1)S(1)}, u32[]{:S(2)}, u32[]{:S(2)}) collective-permute-start(bf16[384,256]{1,0:T(8,128)(2,1)S(1)} %merge.1), channel_id=1, source_target_pairs={{16,0},{24,8},{32,16},{40,24},{48,32},{56,40},{64,48},{72,56},{80,... | collective-permute-start | bytes 589832 | tf_op jit(solution)/shard_map/ppermute | solution.py:250
  48.1 0.9 %collective-permute-done.4.apart = bf16[256,256]{1,0:T(8,128)(2,1)S(1)} collective-permute-done((bf16[256,256]{1,0:T(8,128)(2,1)S(1)}, bf16[256,256]{1,0:T(8,128)(2,1)S(1)}, u32[]{:S(2)}, u32[]{:S(2)}) %collective-permute-start.4) | collective-permute-done | bytes 131104 | tf_op jit(solution)/shard_map/ppermute | solution.py:250
  49.0 8.3 %collective-permute-done.5.shifted = bf16[384,256]{1,0:T(8,128)(2,1)S(1)} collective-permute-done((bf16[384,256]{1,0:T(8,128)(2,1)S(1)}, bf16[384,256]{1,0:T(8,128)(2,1)S(1)}, u32[]{:S(2)}, u32[]{:S(2)}) %collective-permute-start.5) | collective-permute-done | bytes 196640 | tf_op jit(solution)/shard_map/ppermute | solution.py:250
  57.3 0.7 %sum.1 = (bf16[384,128]{1,0:T(8,128)(2,1)}, bf16[384,128]{1,0:T(8,128)(2,1)}) custom-call(f32[384,256]{1,0:T(8,128)S(1)} %fold.1.folded, bf16[384,256]{1,0:T(8,128)(2,1)S(1)} %collective-permute-done.5.shifted), custom_call_target="tpu_custom_call" | custom-call | tf_op jit(solution)/shard_map/sum/pallas_call | solution.py:366
  58.1 0.0 all-to-all-done.1.chunks
  58.1 0.8 %place.1 = bf16[48,4096]{1,0:T(8,128)(2,1)} custom-call(bf16[8,48,512]{2,1,0:T(8,128)(2,1)S(1)} %all-to-all-done.1.chunks), custom_call_target="tpu_custom_call" | custom-call | tf_op jit(solution)/shard_map/place/pallas_call | solution.py:375
  (2 shorter events, 0.0 us)
Async XLA Ops:
  2.9 22.3 %all-to-all-start = ((bf16[8,48,512]{2,1,0:T(8,128)(2,1)}), bf16[8,48,512]{2,1,0:T(8,128)(2,1)S(1)}, u32[]{:S(2)}, u32[]{:S(2)}) async-start(bf16[8,48,512]{2,1,0:T(8,128)(2,1)} %get-tuple-element.15), calls=%async_computation | async-start | bytes 786432 | tf_op jit(solution)/shard_map/all_to_all | solution.py:287
  10.0 15.1 %collective-permute-start.1 = (bf16[384,256]{1,0:T(8,128)(2,1)S(1)}, bf16[384,256]{1,0:T(8,128)(2,1)S(1)}, u32[]{:S(2)}, u32[]{:S(2)}) collective-permute-start(bf16[384,256]{1,0:T(8,128)(2,1)S(1)} %later.1.own), channel_id=1, source_target_pairs={{0,16},{8,24},{16,32},{24,40},{32,48},{40,56},{48,64},{56,72},{64,... | collective-permute-start | bytes 589832 | tf_op jit(solution)/shard_map/ppermute | solution.py:250
  15.4 9.7 %collective-permute-start = (bf16[384,256]{1,0:T(8,128)(2,1)S(1)}, bf16[384,256]{1,0:T(8,128)(2,1)S(1)}, u32[]{:S(2)}, u32[]{:S(2)}) collective-permute-start(bf16[384,256]{1,0:T(8,128)(2,1)S(1)} %later.1.own), channel_id=1, source_target_pairs={{0,8},{8,16},{16,24},{24,32},{32,40},{40,48},{48,56},{56,64},{64,7... | collective-permute-start | bytes 589832 | tf_op jit(solution)/shard_map/ppermute | solution.py:250
  17.4 7.8 %collective-permute-start.2 = (bf16[256,256]{1,0:T(8,128)(2,1)S(1)}, bf16[256,256]{1,0:T(8,128)(2,1)S(1)}, u32[]{:S(2)}, u32[]{:S(2)}) collective-permute-start(bf16[256,256]{1,0:T(8,128)(2,1)S(1)} %get-tuple-element.19), channel_id=1, source_target_pairs={{0,24},{8,32},{16,40},{24,48},{32,56},{40,64},{48,72},{56,80},{64,... | collective-permute-start | bytes 393224 | tf_op jit(solution)/shard_map/ppermute | solution.py:250
  33.3 12.0 %collective-permute-start.3 = (bf16[640,256]{1,0:T(8,128)(2,1)S(1)}, bf16[640,256]{1,0:T(8,128)(2,1)S(1)}, u32[]{:S(2)}, u32[]{:S(2)}) collective-permute-start(bf16[640,256]{1,0:T(8,128)(2,1)S(1)} %get-tuple-element.22), channel_id=1, source_target_pairs={{0,8},{8,0},{16,24},{24,16},{32,40},{40,32},{48,56},{56,48},{64,72... | collective-permute-start | bytes 983048 | tf_op jit(solution)/shard_map/ppermute | solution.py:254
  35.4 22.7 %all-to-all-start.1 = ((bf16[8,48,512]{2,1,0:T(8,128)(2,1)}), bf16[8,48,512]{2,1,0:T(8,128)(2,1)S(1)}, u32[]{:S(2)}, u32[]{:S(2)}) async-start(bf16[8,48,512]{2,1,0:T(8,128)(2,1)} %get-tuple-element.20), calls=%async_computation.1 | async-start | bytes 786432 | tf_op jit(solution)/shard_map/all_to_all | solution.py:287
  42.6 6.4 %collective-permute-start.4 = (bf16[256,256]{1,0:T(8,128)(2,1)S(1)}, bf16[256,256]{1,0:T(8,128)(2,1)S(1)}, u32[]{:S(2)}, u32[]{:S(2)}) collective-permute-start(bf16[256,256]{1,0:T(8,128)(2,1)S(1)} %get-tuple-element.23), channel_id=1, source_target_pairs={{32,8},{48,24},{64,40},{80,56},{96,72},{112,88},{128,104},{144,120... | collective-permute-start | bytes 393224 | tf_op jit(solution)/shard_map/ppermute | solution.py:250
  45.4 11.9 %collective-permute-start.5 = (bf16[384,256]{1,0:T(8,128)(2,1)S(1)}, bf16[384,256]{1,0:T(8,128)(2,1)S(1)}, u32[]{:S(2)}, u32[]{:S(2)}) collective-permute-start(bf16[384,256]{1,0:T(8,128)(2,1)S(1)} %merge.1), channel_id=1, source_target_pairs={{16,0},{24,8},{32,16},{40,24},{48,32},{56,40},{64,48},{72,56},{80,... | collective-permute-start | bytes 589832 | tf_op jit(solution)/shard_map/ppermute | solution.py:250
